TPU v7x, 256 devices: a whole 4x4x8 slice. The times are simulated.
256 devices in a mesh: section: 16 (over z_lo, y), fsdp: 16 (over z_hi, x, core).
Axes of the slice: x: 4, y: 4, z: 8 (z_hi: 2, z_lo: 4; z = z_hi * 4 + z_lo), core: 2. Of those that a mesh axis runs over, the one named last changes fastest.
Arguments:
- residual: bfloat16 [512, 4608], P('fsdp', 'section'), may hold values from -12 to 12
- final_gain: bfloat16 [4608], P('section'), may hold values from 0.099609375 to 1.8984375
- embedding: bfloat16 [256000, 4608], P(('section', 'fsdp')), may hold values from -0.25 to 0.25
- labels: int32 [512], replicated, may hold values from 0 to 255999
- token_weight: float32 [512], replicated, may hold values from 1 to 8
Outputs:
- token_loss: float32 [512], P('fsdp')
- grad_residual: float32 [512, 4608], P('fsdp', 'section')
All inputs are finite; a program needn't handle non-finite values.
Results may differ from a plain program's by a relative error of at most 0.003.
Values may be sent and summed in bfloat16 or wider, within the bound.
No kernel may reach another device: no remote copies, remote signals or barrier semaphores. Data moves between devices by JAX's collectives and lax.ppermute only.
A program may use at most 64 MiB of HBM per device.

v0:
```python
import jax
import jax.numpy as jnp
from jax import lax
from jax.sharding import PartitionSpec as P

D = 4608


EPS = 1e-06
CAP = 30.0


def on_device(residual, final_gain, embedding, labels, token_weight):
    values = residual.astype(jnp.float32)
    local_squares = jnp.sum(values * values, axis=1)
    total_squares = lax.psum(local_squares, "section")
    scaling = lax.rsqrt(total_squares / D + EPS)[:, None]
    normed_piece = (values * scaling * final_gain.astype(jnp.float32)).astype(jnp.bfloat16)
    token_rows = lax.all_gather(normed_piece, "section", axis=1, tiled=True)
    normed = lax.all_gather(token_rows, "fsdp", axis=0, tiled=True)
    block_rows = embedding.shape[0]
    first_id = (
        lax.axis_index("section") * lax.axis_size("fsdp") + lax.axis_index("fsdp")
    ) * block_rows
    logits = lax.dot_general(
        normed, embedding, (((1,), (1,)), ((), ())), preferred_element_type=jnp.float32
    )
    capped = CAP * jnp.tanh(logits / CAP)
    onehot = labels[:, None] == first_id + jnp.arange(block_rows, dtype=jnp.int32)[None, :]
    sum_exp, target = lax.psum(
        (jnp.sum(jnp.exp(capped), axis=1), jnp.sum(jnp.where(onehot, capped, 0.0), axis=1)),
        ("section", "fsdp"),
    )
    log_total = jnp.log(sum_exp)
    own_rows = residual.shape[0]
    row_first = lax.axis_index("fsdp") * own_rows
    token_loss = lax.dynamic_slice_in_dim(log_total - target, row_first, own_rows, 0)
    weights = jnp.exp(capped - log_total[:, None])
    logit_grad = (
        (weights - onehot.astype(jnp.float32)) * token_weight[:, None] * (1.0 - (capped / CAP) ** 2)
    ).astype(jnp.bfloat16)
    full_term = jnp.dot(logit_grad, embedding, preferred_element_type=jnp.float32)
    feature_share = lax.psum_scatter(full_term, "section", scatter_dimension=1, tiled=True)
    grad_normed = lax.psum_scatter(feature_share, "fsdp", scatter_dimension=0, tiled=True)
    upstream = grad_normed * final_gain.astype(jnp.float32)
    inner_sum = lax.psum(jnp.sum(upstream * values, axis=1), "section")[:, None]
    grad_residual = scaling * upstream - values * scaling**3 * inner_sum / D
    return (token_loss, grad_residual)


def solution(mesh):
    in_specs = (P("fsdp", "section"), P("section"), P(("section", "fsdp"), None), P(), P())
    out_specs = (P("fsdp"), P("fsdp", "section"))
    return jax.shard_map(
        on_device, mesh=mesh, in_specs=in_specs, out_specs=out_specs, check_vma=False
    )
```

profile of v0, /device:TPU:32, one launch (start us, length us, event | category | flops | bytes accessed | tf_op | source)
XLA Modules:
  0.0 503.2 jit_solution(11409257867134773594)
XLA Ops:
  7.2 0.0 all-gather.3.cloned.1.call-start
  7.2 0.9 fusion.15
  8.1 37.2 %psum.28 = f32[32]{0:T(128)S(1)} all-reduce(f32[32]{0:T(128)S(1)} %fusion.15), channel_id=1, replica_groups=mesh['section'=16,'fsdp'=16] {'section'}, use_global_device_ids=true, to_apply=%region_1.0 | all-reduce | flops 32 | bytes 256 | tf_op jit(solution)/shard_map/psum | solution.py:16
  45.3 0.7 convert_element_type.17
  46.0 0.8 fusion.22
  46.8 38.8 %all-gather = bf16[16,288,32]{1,2,0:T(8,128)(2,1)S(1)} all-gather(bf16[1,288,32]{1,2,0:T(8,128)(2,1)S(1)} %fusion.22), channel_id=1, replica_groups=mesh['section'=16,'fsdp'=16] {'section'}, dimensions={0}, use_global_device_ids=true | all-gather | bytes 313344 | tf_op jit(solution)/shard_map/all_gather | solution.py:19
  85.6 0.1 copy.10
  85.7 1.1 reshape.19
  86.8 0.0 all-gather.3.cloned.1.call-update
  86.8 0.0 reduce-scatter.5.cloned.1.call-start
  86.9 86.5 %all-gather.3.cloned.1.call-done = bf16[512,4608]{1,0:T(8,128)(2,1)} async-done(((bf16[32,4608]{1,0:T(8,128)(2,1)}), bf16[512,4608]{1,0:T(8,128)(2,1)}) %all-gather.3.cloned.1.call-update) | async-done | bytes 4718608 | tf_op jit(solution)/shard_map/all_gather | solution.py:20
  173.4 9.4 %exponential_reduce_fusion = (f32[512]{0:T(512)S(1)}, f32[512]{0:T(512)S(1)}, f32[512,1000]{0,1:T(8,128)S(1)}) fusion(s32[1000]{0:T(1024)S(1)} %iota_add_fusion, s32[512]{0:T(512)S(1)} %copy-done.1, bf16[512,4608]{1,0:T(8,128)(2,1)} %all-gather.3.cloned.1.call-done, bf16[1000,4608]{1,0:T(8,128)(2,1)} %param.7), kind=kOutput, calls=%fused_computation.7 | convolution fusion | flops 4721662976 | bytes 15992736 | tf_op jit(solution)/shard_map/dot_general | solution.py:25
  182.8 77.3 %all-reduce = (f32[512]{0:T(512)S(1)}, f32[512]{0:T(512)S(1)}) all-reduce(f32[512]{0:T(512)S(1)} %get-tuple-element.5, f32[512]{0:T(512)S(1)} %get-tuple-element.4), channel_id=1, replica_groups=mesh['section'=16,'fsdp'=16] {'section','fsdp'}, use_global_device_ids=true, to_apply=%region_5.6 | all-reduce | flops 1024 | bytes 8192 | tf_op jit(solution)/shard_map/psum | solution.py:30
  260.2 14.1 %fusion.6 = f32[512,4608]{0,1:T(8,128)} fusion(bf16[1000,4608]{1,0:T(8,128)(2,1)} %param.7, f32[512,1000]{0,1:T(8,128)S(1)} %get-tuple-element.12, f32[512]{0:T(512)S(1)} %copy-done.2, f32[512]{0:T(512)S(1)} %get-tuple-element.8, s32[512]{0:T(512)S(1)} %copy-done.1, s32[1000]{0:T(1024)S(1)} %iota_add_fusion), kind=kOutput, calls=%fused_computation.10 | convolution fusion | flops 4724224000 | bytes 20711328 | tf_op jit(solution)/shard_map/dot_general | solution.py:42
  274.3 0.0 reduce-scatter.5.cloned.1.call-update
  274.3 0.0 reduce-scatter.7.cloned.1.call-start
  274.4 103.7 %reduce-scatter.5.cloned.1.call-done = f32[512,288]{0,1:T(8,128)} async-done(((f32[512,4608]{0,1:T(8,128)}), f32[512,288]{0,1:T(8,128)}) %reduce-scatter.5.cloned.1.call-update) | async-done | bytes 589840 | tf_op jit(solution)/shard_map/reduce_scatter | solution.py:43
  378.1 2.2 copy.12
  380.3 0.0 reduce-scatter.7.cloned.1.call-update
  380.4 0.6 dynamic_slice.3
  380.9 78.8 %reduce-scatter.7.cloned.1.call-done = f32[32,288]{1,0:T(8,128)} async-done(((f32[512,288]{1,0:T(8,128)}), f32[32,288]{1,0:T(8,128)}) %reduce-scatter.7.cloned.1.call-update) | async-done | bytes 36880 | tf_op jit(solution)/shard_map/reduce_scatter | solution.py:44
  459.7 0.9 fusion.21
  460.6 34.5 %psum.31 = f32[32]{0:T(128)S(1)} all-reduce(f32[32]{0:T(128)S(1)} %fusion.21), channel_id=1, replica_groups=mesh['section'=16,'fsdp'=16] {'section'}, use_global_device_ids=true, to_apply=%region_9.10 | all-reduce | flops 32 | bytes 256 | tf_op jit(solution)/shard_map/psum | solution.py:46
  495.2 1.5 fusion.20
  (9 shorter events, 0.0 us)
Async XLA Ops:
  7.2 166.3 %copy-start.1 = (s32[512]{0:T(512)S(1)}, s32[512]{0:T(512)}, u32[]{:S(2)}) copy-start(s32[512]{0:T(512)} %param.8) | copy-start | bytes 6148
  7.2 166.2 %all-gather.3.cloned.1.call-start = ((), (), s32[]{:S(2)}) async-start(), calls=%async_computation.2 | async-start | bytes 5013504 | tf_op jit(solution)/shard_map/all_gather | solution.py:20
  86.8 291.3 %reduce-scatter.5.cloned.1.call-start = ((), (), s32[]{:S(2)}) async-start(), calls=%async_computation.3 | async-start | bytes 10027008 | tf_op jit(solution)/shard_map/reduce_scatter | solution.py:43
  86.9 173.3 %copy-start.2 = (f32[512]{0:T(512)S(1)}, f32[512]{0:T(512)}, u32[]{:S(2)}) copy-start(f32[512]{0:T(512)} %param.9) | copy-start | bytes 6148
  274.3 185.4 %copy-start = (bf16[32,288]{1,0:T(8,128)(2,1)S(1)}, bf16[32,288]{1,0:T(8,128)(2,1)}, u32[]{:S(2)}) copy-start(bf16[32,288]{1,0:T(8,128)(2,1)} %param.5) | copy-start | bytes 55300
  274.3 185.4 %reduce-scatter.7.cloned.1.call-start = ((), (), s32[]{:S(2)}) async-start(), calls=%async_computation.4 | async-start | bytes 835584 | tf_op jit(solution)/shard_map/reduce_scatter | solution.py:44
Sparse Core Ops, SparseCore 0:
  87.0 86.4 all-gather.2
  274.4 103.6 reduce-scatter.4
  382.2 77.5 reduce-scatter.6
where the time goes:
time: 511 us; the launch traced here: 503 us
  waiting for transfers between devices  269 us (53%)
  blocking collectives  188 us (37%)
  matrix products  23.5 us (5%)
  between operations  13.8 us (3%)
    reduce_scatter x1, waiting for transfers between devices, on_device(): lax.psum_scatter(full_term, 'section', scatter_dimension=1, tiled=True)  104 us
    all_gather x1, waiting for transfers between devices, on_device(): normed = lax.all_gather(token_rows, 'fsdp', axis=0, tiled=True)  86.5 us
    reduce_scatter x1, waiting for transfers between devices, on_device(): lax.psum_scatter(feature_share, 'fsdp', scatter_dimension=0, tiled=True)  78.8 us
    psum x1, blocking collectives, on_device(): lax.psum((jnp.sum(jnp.exp(capped), axis=1), jnp.sum(jnp.where(onehot, cap...  77.3 us
    all_gather x1, blocking collectives, on_device(): token_rows = lax.all_gather(normed_piece, 'section', axis=1, tiled=True)  38.8 us
    psum x1, blocking collectives, on_device(): total_squares = lax.psum(local_squares, 'section')  37.2 us
    psum x1, blocking collectives, on_device(): inner_sum = lax.psum(jnp.sum(upstream * values, axis=1), 'section')[:, None]  34.5 us
    dot_general x1, matrix products, on_device(): jnp.dot(logit_grad, embedding, preferred_element_type=jnp.float32)  14.1 us
  transfers between devices with their start and end apart: 3, of which 3 were waited for; matrix products, arithmetic and copies ran while one was open for 0% of the time, Pallas kernels for 0%

commit v1 on v0

v1 whole, which is shorter than its diff:
```python
import functools

import jax
import jax.numpy as jnp
from jax import lax
from jax.experimental import pallas as pl
from jax.experimental.pallas import tpu as pltpu
from jax.sharding import Mesh, PartitionSpec as P

D = 4608
EPS = 1e-06
CAP = 30.0
ROWS = 1000
PADDED = 1024
PIECE = 288
WIDE = 1152
BLOCK = 64
TILES = WIDE // 128
SLOTS = 7
PACKED = TILES * BLOCK + 16
F32 = jnp.float32
BF16 = jnp.bfloat16
VMEM = pltpu.MemorySpace.VMEM
BIG = pltpu.CompilerParams(vmem_limit_bytes=56 * 1024 * 1024)


def permute_kernel(in_ref, out_ref):
    block = in_ref[...]
    rows = pl.program_id(0) * block.shape[0] + lax.broadcasted_iota(jnp.int32, (block.shape[0], 1), 0)
    for y in range(4):
        parts = [block[:, (z * 4 + y) * PIECE : (z * 4 + y + 1) * PIECE].astype(F32) for z in range(4)]
        wide = jnp.concatenate(parts, axis=1)
        out_ref[:, y * WIDE : (y + 1) * WIDE] = jnp.where(rows < ROWS, wide, 0.0).astype(BF16)


def permute_embedding(embedding):
    step = 128
    return pl.pallas_call(
        permute_kernel,
        grid=(PADDED // step,),
        in_specs=[pl.BlockSpec((step, D), lambda i: (i, 0))],
        out_specs=pl.BlockSpec((step, D), lambda i: (i, 0)),
        out_shape=jax.ShapeDtypeStruct((PADDED, D), BF16),
        compiler_params=BIG,
        cost_estimate=pl.CostEstimate(flops=0, bytes_accessed=4 * ROWS * D, transcendentals=0),
        name="permute_embedding",
    )(embedding)


def pack_kernel(in_ref, out_ref):
    for zh in range(2):
        parts = [in_ref[zl * 2 + zh, 0:32, :].astype(F32) for zl in range(4)]
        wide = jnp.concatenate(parts, axis=1)
        for k in range(TILES):
            tile = wide[:, k * 128 : (k + 1) * 128].astype(BF16)
            for copy in range(16):
                out_ref[copy, k * BLOCK + zh * 32 : k * BLOCK + zh * 32 + 32, :] = tile
    gains = jnp.concatenate([in_ref[zl * 2, 32:48, :].astype(F32) for zl in range(4)], axis=1)
    rows = [gains[0:1, k * 128 : (k + 1) * 128] for k in range(TILES)]
    tile = jnp.concatenate(rows + [jnp.zeros((16 - TILES, 128), F32)], axis=0).astype(BF16)
    for copy in range(16):
        out_ref[copy, TILES * BLOCK : PACKED, :] = tile


def pack_tokens(gathered):
    return pl.pallas_call(
        pack_kernel,
        out_shape=jax.ShapeDtypeStruct((16, PACKED, 128), BF16),
        compiler_params=BIG,
        name="pack_tokens",
    )(gathered)


def logits_kernel(first_ref, packed_ref, embedding_ref, labels_ref, slot_ref, e_ref, stats_ref, scale_ref, normed, logits):
    y = pl.program_id(0)

    @pl.when(y == 0)
    def _():
        gains = [packed_ref[b * 4, TILES * BLOCK : PACKED, :].astype(F32) for b in range(4)]
        for x in range(4):
            squares = jnp.zeros((BLOCK, 128), F32)
            for b in range(4):
                for k in range(TILES):
                    v = packed_ref[b * 4 + x, k * BLOCK : (k + 1) * BLOCK, :].astype(F32)
                    squares += v * v
            scale = lax.rsqrt(jnp.sum(squares, axis=1, keepdims=True) / D + EPS)
            scale_ref[x * BLOCK : (x + 1) * BLOCK, :] = jnp.broadcast_to(scale, (BLOCK, 128))
            for b in range(4):
                for k in range(TILES):
                    v = packed_ref[b * 4 + x, k * BLOCK : (k + 1) * BLOCK, :].astype(F32)
                    normed[b, x * BLOCK : (x + 1) * BLOCK, k * 128 : (k + 1) * 128] = (
                        v * scale * gains[b][k : k + 1, :]
                    ).astype(BF16)

    term = lax.dot_general(
        embedding_ref[...], normed[y], (((1,), (1,)), ((), ())), preferred_element_type=F32
    )

    @pl.when(y == 0)
    def _():
        logits[...] = term

    @pl.when(y > 0)
    def _():
        logits[...] += term

    @pl.when(y == 3)
    def _():
        raw = logits[...]
        ratio = jnp.tanh(raw / CAP)
        row = lax.broadcasted_iota(jnp.int32, raw.shape, 0)
        inside = row < ROWS
        is_label = jnp.logical_and(inside, row + first_ref[0] == labels_ref[...])
        exps = jnp.where(inside, jnp.exp(CAP * ratio), 0.0)
        others = jnp.where(is_label, 0.0, exps * (1.0 - ratio * ratio))
        stats_ref[0:1, :] = jnp.sum(exps, axis=0, keepdims=True)
        stats_ref[1:2, :] = jnp.sum(others * raw, axis=0, keepdims=True)
        stats_ref[2:3, :] = jnp.sum(jnp.where(is_label, raw, 0.0), axis=0, keepdims=True)
        stats_ref[3:8, :] = jnp.zeros((5, raw.shape[1]), F32)
        e_ref[0:256, :] = others.T.astype(BF16)
        e_ref[256:288, :] = slot_ref[...]


def logits_of(first, packed, embedding, labels, slots):
    return pl.pallas_call(
        logits_kernel,
        grid=(4,),
        in_specs=[
            pl.BlockSpec(memory_space=pltpu.MemorySpace.SMEM),
            pl.BlockSpec((16, PACKED, 128), lambda y: (0, 0, 0)),
            pl.BlockSpec((PADDED, WIDE), lambda y: (0, y)),
            pl.BlockSpec((1, 256), lambda y: (0, 0)),
            pl.BlockSpec((32, PADDED), lambda y: (0, 0)),
        ],
        out_specs=[
            pl.BlockSpec((288, PADDED), lambda y: (0, 0)),
            pl.BlockSpec((8, 256), lambda y: (0, 0)),
            pl.BlockSpec((256, 128), lambda y: (0, 0)),
        ],
        out_shape=[
            jax.ShapeDtypeStruct((288, PADDED), BF16),
            jax.ShapeDtypeStruct((8, 256), F32),
            jax.ShapeDtypeStruct((256, 128), F32),
        ],
        scratch_shapes=[pltpu.VMEM((4, 256, WIDE), BF16), pltpu.VMEM((PADDED, 256), F32)],
        compiler_params=BIG,
        cost_estimate=pl.CostEstimate(flops=2 * 256 * PADDED * D, bytes_accessed=2 * PADDED * D, transcendentals=2 * 256 * PADDED),
        name="logits",
    )(first, packed, embedding, labels, slots)


def three_pieces(value):
    high = value.astype(BF16).astype(F32)
    middle = (value - high).astype(BF16).astype(F32)
    low = (value - high - middle).astype(BF16).astype(F32)
    return [high, middle, low]


def stats_row(values):
    pieces = []
    for value in values:
        for piece in three_pieces(value):
            pieces += [piece, jnp.zeros((1, 128 - BLOCK), F32)]
    return jnp.concatenate(pieces, axis=1)


def read_stats(row):
    return [
        sum(row[:, (3 * i + j) * 128 : (3 * i + j) * 128 + BLOCK] for j in (2, 1, 0))
        for i in range(3)
    ]


def gradient_kernel(with_other, *refs):
    if with_other:
        e_ref, embedding_ref, stats_ref, other_ref, out_ref = refs
    else:
        e_ref, embedding_ref, stats_ref, out_ref = refs
    term = jnp.dot(e_ref[...], embedding_ref[...], preferred_element_type=F32)
    last = lax.broadcasted_iota(jnp.int32, (8, WIDE), 0) == 7
    for x in range(4):
        main = term[x * BLOCK : (x + 1) * BLOCK, :]
        extra = term[256 + 8 * x : 256 + 8 * x + 8, :]
        values = [stats_ref[i : i + 1, x * BLOCK : (x + 1) * BLOCK] for i in range(3)]
        if with_other:
            main = main + other_ref[x, 0:BLOCK, :].astype(F32)
            other_extra = other_ref[x, BLOCK : BLOCK + 8, :].astype(F32)
            extra = extra + other_extra
            values = [a + b for a, b in zip(values, read_stats(other_extra[7:8, :]))]
        row = jnp.broadcast_to(stats_row(values), (8, WIDE))
        out_ref[x, 0:BLOCK, :] = main.astype(BF16)
        out_ref[x, BLOCK : BLOCK + 8, :] = jnp.where(last, row, extra).astype(BF16)


def gradient_of(e, embedding, stats, other=None):
    payload = pl.BlockSpec((4, BLOCK + 8, WIDE), lambda y: (y, 0, 0))
    in_specs = [
        pl.BlockSpec((288, PADDED), lambda y: (0, 0)),
        pl.BlockSpec((PADDED, WIDE), lambda y: (0, y)),
        pl.BlockSpec((8, 256), lambda y: (0, 0)),
    ]
    args = [e, embedding, stats]
    if other is not None:
        in_specs.append(payload)
        args.append(other)
    return pl.pallas_call(
        functools.partial(gradient_kernel, other is not None),
        grid=(4,),
        in_specs=in_specs,
        out_specs=payload,
        out_shape=jax.ShapeDtypeStruct((16, BLOCK + 8, WIDE), BF16),
        compiler_params=BIG,
        cost_estimate=pl.CostEstimate(flops=2 * 288 * PADDED * D, bytes_accessed=2 * PADDED * D, transcendentals=0),
        name="gradient",
    )(*args)


def plane_kernel(in_ref, place_ref, more_ref, out_ref):
    total = in_ref[0, 0:BLOCK, :].astype(F32)
    for source in range(1, 16):
        total += in_ref[source, 0:BLOCK, :].astype(F32)
    extras = [in_ref[source, BLOCK : BLOCK + 8, :].astype(F32) for source in range(16)]
    stacked = jnp.concatenate(extras, axis=0).astype(BF16)
    label_rows = jnp.dot(place_ref[...], stacked, preferred_element_type=F32) + more_ref[...].astype(F32)
    row = extras[0][7:8, :]
    for source in range(1, 16):
        row = row + extras[source][7:8, :]
    pieces = []
    for value in read_stats(row):
        pieces += three_pieces(value)
    sums = jnp.concatenate(pieces + [jnp.zeros((1, 640 - 9 * BLOCK), F32)], axis=1)
    sums = jnp.broadcast_to(sums, (16, 640)).astype(BF16)
    for zl in range(4):
        for zh in range(2):
            main = total[zh * 32 : zh * 32 + 32, zl * PIECE : (zl + 1) * PIECE]
            rows = label_rows[zh * 32 : zh * 32 + 32, zl * PIECE : (zl + 1) * PIECE]
            both = jnp.concatenate([main, rows, jnp.zeros((32, 640 - 2 * PIECE), F32)], axis=1)
            out_ref[zl * 2 + zh, 0:32, :] = both.astype(BF16)
            out_ref[zl * 2 + zh, 32:48, :] = sums


def plane_sum(received, place, more):
    return pl.pallas_call(
        plane_kernel,
        out_shape=jax.ShapeDtypeStruct((8, 48, 640), BF16),
        compiler_params=BIG,
        name="plane_sum",
    )(received, place, more)


def final_kernel(half_ref, in_ref, values_ref, gain_ref, weight_ref, scale_ref, loss_ref, grad_ref):
    total = in_ref[0, 0:32, :].astype(F32)
    row = in_ref[0, 32:48, :].astype(F32)[0:1, :]
    for source in range(1, 8):
        total += in_ref[source, 0:32, :].astype(F32)
        row = row + in_ref[source, 32:48, :].astype(F32)[0:1, :]
    pick = lax.broadcasted_iota(jnp.int32, (32, BLOCK), 1) == half_ref[0] * 32 + lax.broadcasted_iota(
        jnp.int32, (32, BLOCK), 0
    )

    def column(i):
        value = sum(row[:, (3 * i + j) * BLOCK : (3 * i + j + 1) * BLOCK] for j in (2, 1, 0))
        return jnp.sum(jnp.where(pick, jnp.broadcast_to(value, (32, BLOCK)), 0.0), axis=1, keepdims=True)

    sum_exp, inner_others, raw = column(0), column(1), column(2)
    weight = weight_ref[...]
    scaling = scale_ref[:, 0:1]
    ratio = jnp.tanh(raw / CAP)
    capped = CAP * ratio
    log_total = jnp.log(sum_exp)
    loss = log_total - capped
    coefficient = (jnp.exp(capped - log_total) - 1.0) * weight * (1.0 - ratio * ratio)
    coefficient = coefficient.astype(BF16).astype(F32)
    share = weight / sum_exp
    grad_normed = total[:, 0:PIECE] * share + total[:, PIECE : 2 * PIECE] * coefficient
    inner = (inner_others * share + coefficient * raw) / scaling
    upstream = grad_normed * gain_ref[...].astype(F32)
    values = values_ref[...].astype(F32)
    grad_ref[...] = scaling * upstream - values * (scaling * scaling * scaling * inner / D)
    eye = lax.broadcasted_iota(jnp.int32, (32, 128), 0) == lax.broadcasted_iota(jnp.int32, (32, 128), 1)
    loss_ref[...] = jnp.sum(jnp.where(eye, jnp.broadcast_to(loss, (32, 128)), 0.0), axis=0, keepdims=True)


def finish(half, received, values, gain, weight, scale):
    spec = pl.BlockSpec(memory_space=VMEM)
    return pl.pallas_call(
        final_kernel,
        in_specs=[pl.BlockSpec(memory_space=pltpu.MemorySpace.SMEM)] + [spec] * 5,
        out_specs=[spec] * 2,
        out_shape=[jax.ShapeDtypeStruct((1, 128), F32), jax.ShapeDtypeStruct((32, PIECE), F32)],
        compiler_params=BIG,
        name="finish",
    )(half, received, values, gain, weight, scale)


def swap_cores(array):
    return lax.ppermute(array, "core", [(0, 1), (1, 0)])


def on_device(residual, final_gain, embedding, labels, token_weight):
    zl, y, zh, x, core = (lax.axis_index(name) for name in ("z_lo", "y", "z_hi", "x", "core"))
    chip = ((zl * 4 + y) * 2 + zh) * 4 + x
    first = (chip * 2 + core) * ROWS

    mine = jnp.concatenate([residual, final_gain[None, :], jnp.zeros((15, PIECE), BF16)], axis=0)
    gathered = lax.all_to_all(
        jnp.broadcast_to(mine[None], (8, 48, PIECE)), ("z_lo", "z_hi"), 0, 0, tiled=True
    )
    packed = lax.all_to_all(pack_tokens(gathered), ("y", "x"), 0, 0, tiled=True)

    token = jnp.arange(512, dtype=jnp.int32)
    group = (token // 32) % 2 * 4 + (token // 64) % 4
    owner = labels // (2 * ROWS)
    key = owner * 8 + group
    same = jnp.logical_and(key[:, None] == key[None, :], token[None, :] < token[:, None])
    rank = jnp.sum(same.astype(jnp.int32), axis=1)
    turn, slot = rank // SLOTS, rank % SLOTS
    slots = jnp.arange(64, dtype=jnp.int32)
    vocab = jnp.arange(PADDED, dtype=jnp.int32)

    def slot_rows(number):
        taken = jnp.where(jnp.logical_and(owner == chip, turn == number), group * 8 + slot, -1)
        match = taken[None, :] == slots[:, None]
        held = jnp.sum(jnp.where(match, (labels - first)[None, :] + 1, 0), axis=1) - 1
        return (held[:, None] == vocab[None, :]).astype(BF16)

    def by_half(array):
        return array.reshape(2, 4, 2, 32).transpose(2, 1, 0, 3)

    def own_tokens(array):
        return lax.dynamic_slice(by_half(array), (core, x, 0, 0), (1, 1, 2, 32)).reshape(BLOCK)

    own_owner, own_turn, own_slot = own_tokens(owner), own_tokens(turn), own_tokens(slot)
    own_chip = jnp.arange(16, dtype=jnp.int32)
    own_chip = ((zl * 4 + own_chip // 4) * 2 + zh) * 4 + own_chip % 4

    def places(number):
        hit = jnp.logical_and(own_owner[:, None] == own_chip[None, :], (own_turn == number)[:, None])
        at = own_slot[:, None] == jnp.arange(8, dtype=jnp.int32)[None, :]
        return jnp.logical_and(hit[:, :, None], at[:, None, :]).astype(BF16).reshape(BLOCK, 128)

    table = permute_embedding(embedding)

    def more_rows(carry):
        number, rows = carry
        found = jnp.dot(slot_rows(number), table, preferred_element_type=F32).astype(BF16)
        found = found.reshape(2, 4, 8, 4, WIDE).transpose(0, 3, 1, 2, 4).reshape(2, 16, 8, WIDE)
        ours = lax.dynamic_index_in_dim(found, core, 0, keepdims=False)
        theirs = lax.dynamic_index_in_dim(found, 1 - core, 0, keepdims=False)
        ours = ours + swap_cores(theirs)
        ours = lax.all_to_all(ours, ("y", "x"), 0, 0, tiled=True).reshape(128, WIDE)
        return number + 1, rows + jnp.dot(places(number), ours, preferred_element_type=F32).astype(BF16)

    rounds = jnp.max(turn) + 1
    _, more = lax.while_loop(
        lambda carry: carry[0] < rounds, more_rows, (jnp.int32(1), jnp.zeros((BLOCK, WIDE), BF16))
    )

    label_halves = by_half(labels).reshape(2, 1, 256)
    slot_halves = slot_rows(0).reshape(2, 32, PADDED)

    def half_of(array, which):
        return lax.dynamic_index_in_dim(array, which, 0, keepdims=False)

    start = first.reshape(1)
    other_packed = swap_cores(packed)
    e, stats, scale = logits_of(start, packed, table, half_of(label_halves, core), half_of(slot_halves, core))
    e_other, stats_other, _ = logits_of(
        start, other_packed, table, half_of(label_halves, 1 - core), half_of(slot_halves, 1 - core)
    )
    from_other = swap_cores(gradient_of(e_other, table, stats_other))
    payload = gradient_of(e, table, stats, from_other)
    plane = lax.all_to_all(payload, ("y", "x"), 0, 0, tiled=True)
    column = lax.all_to_all(plane_sum(plane, places(0), more), ("z_lo", "z_hi"), 0, 0, tiled=True)

    own_first = ((zh * 4 + x) * 2 + core) * 32
    weight = lax.dynamic_slice_in_dim(token_weight, own_first, 32, 0).reshape(32, 1)
    own_scale = lax.dynamic_slice_in_dim(scale, x * BLOCK + zh * 32, 32, 0)
    loss, grad = finish(zh.reshape(1), column, residual, final_gain.reshape(1, PIECE), weight, own_scale)
    return (loss[0, 0:32], grad)


def solution(mesh):
    fine = Mesh(mesh.devices.reshape(4, 4, 2, 4, 2), ("z_lo", "y", "z_hi", "x", "core"))
    section, fsdp = ("z_lo", "y"), ("z_hi", "x", "core")
    in_specs = (P(fsdp, section), P(section), P(section + fsdp, None), P(), P())
    out_specs = (P(fsdp), P(fsdp, section))
    return jax.shard_map(on_device, mesh=fine, in_specs=in_specs, out_specs=out_specs, check_vma=False)
```

time: 511 us -> 191 us (0.37); the launches traced: 503 us -> 190 us
  waiting for transfers between devices: 269 us -> 54.2 us
  blocking collectives: 188 us -> 58.1 us
  Pallas kernels: 0 us -> 55.1 us
  matrix products: 23.5 us -> 0 us
  between operations: 13.8 us -> 1.45 us
  local copies, waits for them, and re-layouts: 4.04 us -> 11.3 us
  starting transfers between devices: 0.12 us -> 7.18 us
    reduce_scatter x2 -> x0, waiting for transfers between devices: 183 us -> none  [the longest x1 104 us: on_device(): lax.psum_scatter(full_term, 'section', scatter_dimension=1, tiled=True)]
    psum x3 -> x0, blocking collectives: 149 us -> none  [the longest x1 77.3 us: on_device(): lax.psum((jnp.sum(jnp.exp(capped), axis=1), jnp.sum(jnp.where(onehot, cap...]
    all_gather x1 -> x0, waiting for transfers between devices: 86.5 us -> none  [on_device(): normed = lax.all_gather(token_rows, 'fsdp', axis=0, tiled=True)]
    all_to_all x0 -> x2, blocking collectives: none -> 58.1 us  [the longest x1 38.6 us: on_device(): packed = lax.all_to_all(pack_tokens(gathered), ('y', 'x'), 0, 0, tiled=True)]
    pallas_call x0 -> x8, Pallas kernels: none -> 55.1 us  [the longest x2 19.3 us: logits_of(): pl.pallas_call(logits_kernel, grid=(4,), in_specs=[pl.BlockSpec(memory_sp...]
    all_to_all x0 -> x2, waiting for transfers between devices: none -> 54.2 us  [the longest x1 41.9 us: on_device(): plane = lax.all_to_all(payload, ('y', 'x'), 0, 0, tiled=True)]
    all_gather x1 -> x0, blocking collectives: 38.8 us -> none  [on_device(): token_rows = lax.all_gather(normed_piece, 'section', axis=1, tiled=True)]
    dot_general x2 -> x0, matrix products: 23.5 us -> none  [the longest x1 14.1 us: on_device(): jnp.dot(logit_grad, embedding, preferred_element_type=jnp.float32)]
  transfers between devices with their start and end apart: 3 -> 4, of which waited for: 3 -> 2; matrix products, arithmetic and copies ran while one was open for 0% -> 4% of each run, Pallas kernels for 0% -> 12%
where the time goes in v1:
time: 191 us; the launch traced here: 190 us
  blocking collectives  58.1 us (30%)
  Pallas kernels  55.1 us (29%)
  waiting for transfers between devices  54.2 us (28%)
  local copies, waits for them, and re-layouts  11.3 us (6%)
  starting transfers between devices  7.18 us (4%)
  other arithmetic  2.78 us (1%)
    all_to_all x1, waiting for transfers between devices, on_device(): plane = lax.all_to_all(payload, ('y', 'x'), 0, 0, tiled=True)  41.9 us
    all_to_all x1, blocking collectives, on_device(): packed = lax.all_to_all(pack_tokens(gathered), ('y', 'x'), 0, 0, tiled=True)  38.6 us
    all_to_all x1, blocking collectives, on_device(): lax.all_to_all(jnp.broadcast_to(mine[None], (8, 48, PIECE)), ('z_lo', 'z_...  19.5 us
    pallas_call x2, Pallas kernels, logits_of(): pl.pallas_call(logits_kernel, grid=(4,), in_specs=[pl.BlockSpec(memory_sp...  19.3 us
    pallas_call x2, Pallas kernels, gradient_of(): pl.pallas_call(functools.partial(gradient_kernel, other is not None), gri...  15.6 us
    pallas_call x1, Pallas kernels, permute_embedding(): pl.pallas_call(permute_kernel, grid=(PADDED // step,), in_specs=[pl.Block...  12.5 us
    all_to_all x1, waiting for transfers between devices, on_device(): lax.all_to_all(plane_sum(plane, places(0), more), ('z_lo', 'z_hi'), 0, 0,...  12.3 us
    unnamed x18, local copies, waits for them, and re-layouts  3.84 us
  transfers between devices with their start and end apart: 4, of which 2 were waited for; matrix products, arithmetic and copies ran while one was open for 4% of the time, Pallas kernels for 12%

profile of v1, /device:TPU:32, one launch (start us, length us, event | category | flops | bytes accessed | tf_op | source)
XLA Modules:
  0.0 190.3 jit_solution(1476402254677908841)
XLA Ops:
  0.6 0.7 broadcast_in_dim.55.gain_ref
  1.4 0.8 maximum_maximum_fusion
  2.3 19.5 %all_to_all.31.in_ref = bf16[8,48,288]{2,1,0:T(8,128)(2,1)} all-to-all(bf16[8,48,288]{2,1,0:T(8,128)(2,1)S(1)} %broadcast_in_dim.57), channel_id=1, replica_groups=mesh['z_lo'=4,'y'=4,'z_hi'=2,'x'=4,'core'=2] {'z_lo','z_hi'}, dimensions={0} | all-to-all | bytes 442368 | tf_op jit(solution)/shard_map/all_to_all | solution.py:306
  21.8 2.6 %pack_tokens.1 = bf16[16,592,128]{2,1,0:T(8,128)(2,1)} custom-call(bf16[8,48,288]{2,1,0:T(8,128)(2,1)} %all_to_all.31.in_ref), custom_call_target="tpu_custom_call" | custom-call | tf_op jit(solution)/shard_map/pack_tokens/pallas_call | solution.py:66
  24.4 38.6 %all_to_all.32.packed_ref = bf16[16,592,128]{2,1,0:T(8,128)(2,1)S(1)} all-to-all(bf16[16,592,128]{2,1,0:T(8,128)(2,1)} %pack_tokens.1), channel_id=1, replica_groups=mesh['z_lo'=4,'y'=4,'z_hi'=2,'x'=4,'core'=2] {'y','x'}, dimensions={0} | all-to-all | bytes 4849664 | tf_op jit(solution)/shard_map/all_to_all | solution.py:309
  63.0 12.5 %permute_embedding.1.embedding_ref.refs_1_ = bf16[1024,4608]{1,0:T(8,128)(2,1)} custom-call(bf16[1000,4608]{1,0:T(8,128)(2,1)} %in_ref.1), custom_call_target="tpu_custom_call" | custom-call | bytes 18432000 | tf_op jit(solution)/shard_map/permute_embedding/pallas_call | solution.py:38
  75.9 0.7 fusion.54
  78.2 9.7 %logits.3 = (bf16[288,1024]{1,0:T(8,128)(2,1)}, f32[8,256]{1,0:T(8,128)}, f32[256,128]{1,0:T(8,128)}) custom-call(s32[1]{0:T(128)} %bitcast.1.first_ref, bf16[16,592,128]{2,1,0:T(8,128)(2,1)} %collective-permute-done.1.packed_ref, bf16[1024,4608]{1,0:T(8,128)(2,1)} %permute_embedding.1.embedding_ref.refs_1_, s32[1,256]{1,0:T(1,128)} %get-tuple-element.347.labels_ref, ...), custom_call_target="tpu_custom_call" | custom-call | flops 2415919104 | bytes 9437184 | tf_op jit(solution)/shard_map/logits/pallas_call | solution.py:125
  87.9 7.6 %gradient.2 = bf16[16,72,1152]{2,1,0:T(8,128)(2,1)} custom-call(bf16[288,1024]{1,0:T(8,128)(2,1)} %get-tuple-element.248.refs_0_, bf16[1024,4608]{1,0:T(8,128)(2,1)} %permute_embedding.1.embedding_ref.refs_1_, f32[8,256]{1,0:T(8,128)} %get-tuple-element.249.refs_2_), custom_call_target="tpu_custom_call" | custom-call | flops 2717908992 | bytes 9437184 | tf_op jit(solution)/shard_map/gradient/pallas_call | solution.py:206
  97.9 9.7 %logits.2 = (bf16[288,1024]{1,0:T(8,128)(2,1)}, f32[8,256]{1,0:T(8,128)}, f32[256,128]{1,0:T(8,128)}) custom-call(s32[1]{0:T(128)} %bitcast.1.first_ref, bf16[16,592,128]{2,1,0:T(8,128)(2,1)} %copy-done.2, bf16[1024,4608]{1,0:T(8,128)(2,1)} %permute_embedding.1.embedding_ref.refs_1_, s32[1,256]{1,0:T(1,128)} %get-tuple-element.348.labels_ref, ...), custom_call_target="tpu_custom_call" | custom-call | flops 2415919104 | bytes 9437184 | tf_op jit(solution)/shard_map/logits/pallas_call | solution.py:125
  107.6 1.5 copy-done.3
  109.1 8.1 %gradient.3 = bf16[16,72,1152]{2,1,0:T(8,128)(2,1)} custom-call(bf16[288,1024]{1,0:T(8,128)(2,1)} %get-tuple-element.246.refs_0_, bf16[1024,4608]{1,0:T(8,128)(2,1)} %permute_embedding.1.embedding_ref.refs_1_, f32[8,256]{1,0:T(8,128)} %get-tuple-element.247.refs_2_, bf16[16,72,1152]{2,1,0:T(8,128)(2,1)} %copy-done.3), custom_call_target="tpu_custom_call" | custom-call | flops 2717908992 | bytes 9437184 | tf_op jit(solution)/shard_map/gradient/pallas_call | solution.py:206
  117.4 3.7 %all-to-all-start.3 = ((bf16[16,72,1152]{2,1,0:T(8,128)(2,1)}), bf16[16,72,1152]{2,1,0:T(8,128)(2,1)S(1)}, u32[]{:S(2)}, u32[]{:S(2)}) async-start(bf16[16,72,1152]{2,1,0:T(8,128)(2,1)} %gradient.3), calls=%async_computation.3 | async-start | bytes 5308416 | tf_op jit(solution)/shard_map/all_to_all | solution.py:373
  121.4 0.7 copy.27.place_ref
  122.1 41.9 %all-to-all-done.3.in_ref = bf16[16,72,1152]{2,1,0:T(8,128)(2,1)S(1)} async-done(((bf16[16,72,1152]{2,1,0:T(8,128)(2,1)}), bf16[16,72,1152]{2,1,0:T(8,128)(2,1)S(1)}, u32[]{:S(2)}, u32[]{:S(2)}) %all-to-all-start.3) | async-done | bytes 2654240 | tf_op jit(solution)/shard_map/all_to_all | solution.py:373
  164.0 1.5 copy-done.1
  165.5 3.0 %plane_sum.1 = bf16[8,48,640]{2,1,0:T(8,128)(2,1)} custom-call(bf16[16,72,1152]{2,1,0:T(8,128)(2,1)} %copy-done.1, bf16[64,128]{1,0:T(8,128)(2,1)} %copy.27.place_ref, bf16[64,1152]{1,0:T(8,128)(2,1)S(1)} %get-tuple-element.250.more_ref), custom_call_target="tpu_custom_call" | custom-call | tf_op jit(solution)/shard_map/plane_sum/pallas_call | solution.py:243
  168.5 3.4 %all-to-all-start.4 = ((bf16[8,48,640]{2,1,0:T(8,128)(2,1)}), bf16[8,48,640]{2,1,0:T(8,128)(2,1)S(1)}, u32[]{:S(2)}, u32[]{:S(2)}) async-start(bf16[8,48,640]{2,1,0:T(8,128)(2,1)} %plane_sum.1), calls=%async_computation.4 | async-start | bytes 983040 | tf_op jit(solution)/shard_map/all_to_all | solution.py:374
  172.1 0.7 copy.28.weight_ref
  172.8 1.3 constant_dynamic-slice_fusion.2.scale_ref
  174.1 12.3 %all-to-all-done.4.in_ref = bf16[8,48,640]{2,1,0:T(8,128)(2,1)S(1)} async-done(((bf16[8,48,640]{2,1,0:T(8,128)(2,1)}), bf16[8,48,640]{2,1,0:T(8,128)(2,1)S(1)}, u32[]{:S(2)}, u32[]{:S(2)}) %all-to-all-start.4) | async-done | bytes 491552 | tf_op jit(solution)/shard_map/all_to_all | solution.py:374
  186.4 0.8 copy-done.4
  187.2 2.0 %finish.1 = (f32[1,128]{1,0:T(1,128)}, f32[32,288]{1,0:T(8,128)}) custom-call(s32[1]{0:T(128)} %bitcast.half_ref, bf16[8,48,640]{2,1,0:T(8,128)(2,1)} %copy-done.4, bf16[32,288]{1,0:T(8,128)(2,1)} %values_ref.1, bf16[1,288]{1,0:T(2,128)(2,1)} %copy-done.6, f32[32,1]{1,0:T(8,128)} %copy.28.weight_ref, f32[32,128]{1,0:T(8,128)} %constant_dynamic-slice_fusion.2.scale_ref), custom_call_target="tpu_custom_call" | custom-call | tf_op jit(solution)/shard_map/finish/pallas_call | solution.py:286
  189.2 1.1 slice_bitcast_fusion
  (54 shorter events, 4.5 us)
Async XLA Ops:
  0.6 171.4 %copy-start = (f32[512]{0:T(512)S(1)}, f32[512]{0:T(512)}, u32[]{:S(2)}) copy-start(f32[512]{0:T(512)} %param.11) | copy-start | bytes 6148
  1.3 61.6 %copy-start.6 = (bf16[1,288]{1,0:T(2,128)(2,1)}, bf16[1,288]{1,0:T(2,128)(2,1)S(1)}, u32[]{:S(2)}) copy-start(bf16[1,288]{1,0:T(2,128)(2,1)S(1)} %broadcast_in_dim.55.gain_ref) | copy-start | bytes 1732
  63.0 12.5 %copy-start.2 = (bf16[16,592,128]{2,1,0:T(8,128)(2,1)}, bf16[16,592,128]{2,1,0:T(8,128)(2,1)S(1)}, u32[]{:S(2)}) copy-start(bf16[16,592,128]{2,1,0:T(8,128)(2,1)S(1)} %all_to_all.32.packed_ref) | copy-start | bytes 7274500
  63.0 15.2 %collective-permute-start.1 = (bf16[16,592,128]{2,1,0:T(8,128)(2,1)S(1)}, bf16[16,592,128]{2,1,0:T(8,128)(2,1)}, u32[]{:S(2)}, u32[]{:S(2)}) collective-permute-start(bf16[16,592,128]{2,1,0:T(8,128)(2,1)S(1)} %all_to_all.32.packed_ref), channel_id=1, source_target_pairs={{0,1},{1,0},{2,3},{3,2},{4,5},{5,4},{6,7},{7,6},{8,9},{9,8},{10,11... | collective-permute-start | bytes 7274504 | tf_op jit(solution)/shard_map/ppermute | solution.py:297
  63.0 12.5 %copy-start.5 = (s32[512]{0:T(512)S(1)}, s32[512]{0:T(512)}, u32[]{:S(2)}) copy-start(s32[512]{0:T(512)} %param.10) | copy-start | bytes 6148
  95.4 12.1 %collective-permute-start.2 = (bf16[16,72,1152]{2,1,0:T(8,128)(2,1)}, bf16[16,72,1152]{2,1,0:T(8,128)(2,1)S(1)}, u32[]{:S(2)}, u32[]{:S(2)}) collective-permute-start(bf16[16,72,1152]{2,1,0:T(8,128)(2,1)} %gradient.2), channel_id=1, source_target_pairs={{0,1},{1,0},{2,3},{3,2},{4,5},{5,4},{6,7},{7,6},{8,9},{9,8},{10,11... | collective-permute-start | bytes 7962632 | tf_op jit(solution)/shard_map/ppermute | solution.py:297
  97.0 10.6 %copy-start.7 = (s32[2,1,1,32]{3,2,1,0:T(1,128)}, s32[2,1,1,32]{3,2,1,0:T(1,128)S(1)}, u32[]{:S(2)}) copy-start(s32[2,1,1,32]{3,2,1,0:T(1,128)S(1)} %get-tuple-element.334) | copy-start | bytes 772
  97.0 10.6 %copy-start.8 = (s32[2,1,1,32]{3,2,1,0:T(1,128)}, s32[2,1,1,32]{3,2,1,0:T(1,128)S(1)}, u32[]{:S(2)}) copy-start(s32[2,1,1,32]{3,2,1,0:T(1,128)S(1)} %get-tuple-element.352) | copy-start | bytes 772
  107.6 1.5 copy-start.3
  117.4 46.6 %all-to-all-start.3 = ((bf16[16,72,1152]{2,1,0:T(8,128)(2,1)}), bf16[16,72,1152]{2,1,0:T(8,128)(2,1)S(1)}, u32[]{:S(2)}, u32[]{:S(2)}) async-start(bf16[16,72,1152]{2,1,0:T(8,128)(2,1)} %gradient.3), calls=%async_computation.3 | async-start | bytes 5308416 | tf_op jit(solution)/shard_map/all_to_all | solution.py:373
  164.0 1.5 copy-start.1
  168.5 17.9 %all-to-all-start.4 = ((bf16[8,48,640]{2,1,0:T(8,128)(2,1)}), bf16[8,48,640]{2,1,0:T(8,128)(2,1)S(1)}, u32[]{:S(2)}, u32[]{:S(2)}) async-start(bf16[8,48,640]{2,1,0:T(8,128)(2,1)} %plane_sum.1), calls=%async_computation.4 | async-start | bytes 983040 | tf_op jit(solution)/shard_map/all_to_all | solution.py:374
  186.4 0.8 copy-start.4

commit v2 on v1

--- a/solution.py
+++ b/solution.py
@@ -21,16 +21,24 @@
 F32 = jnp.float32
 BF16 = jnp.bfloat16
 VMEM = pltpu.MemorySpace.VMEM
-BIG = pltpu.CompilerParams(vmem_limit_bytes=56 * 1024 * 1024)
+WHOLE = pl.BlockSpec(memory_space=VMEM)
+SCALARS = pl.BlockSpec(memory_space=pltpu.MemorySpace.SMEM)
+BIG = pltpu.CompilerParams(vmem_limit_bytes=20 * 1024 * 1024)
+
+
+def near(array):
+    return pltpu.with_memory_space_constraint(array, VMEM)
 
 
 def permute_kernel(in_ref, out_ref):
+    step = in_ref.shape[0]
     block = in_ref[...]
-    rows = pl.program_id(0) * block.shape[0] + lax.broadcasted_iota(jnp.int32, (block.shape[0], 1), 0)
+    first = pl.multiple_of(pl.program_id(0) * step, step)
+    rows = first + lax.broadcasted_iota(jnp.int32, (step, 1), 0)
     for y in range(4):
         parts = [block[:, (z * 4 + y) * PIECE : (z * 4 + y + 1) * PIECE].astype(F32) for z in range(4)]
         wide = jnp.concatenate(parts, axis=1)
-        out_ref[:, y * WIDE : (y + 1) * WIDE] = jnp.where(rows < ROWS, wide, 0.0).astype(BF16)
+        out_ref[pl.ds(first, step), y * WIDE : (y + 1) * WIDE] = jnp.where(rows < ROWS, wide, 0.0).astype(BF16)
 
 
 def permute_embedding(embedding):
@@ -39,8 +47,8 @@
         permute_kernel,
         grid=(PADDED // step,),
         in_specs=[pl.BlockSpec((step, D), lambda i: (i, 0))],
-        out_specs=pl.BlockSpec((step, D), lambda i: (i, 0)),
-        out_shape=jax.ShapeDtypeStruct((PADDED, D), BF16),
+        out_specs=WHOLE,
+        out_shape=pltpu.VMEM((PADDED, D), BF16),
         compiler_params=BIG,
         cost_estimate=pl.CostEstimate(flops=0, bytes_accessed=4 * ROWS * D, transcendentals=0),
         name="permute_embedding",
@@ -65,88 +73,62 @@
 def pack_tokens(gathered):
     return pl.pallas_call(
         pack_kernel,
-        out_shape=jax.ShapeDtypeStruct((16, PACKED, 128), BF16),
+        in_specs=[WHOLE],
+        out_specs=WHOLE,
+        out_shape=pltpu.VMEM((16, PACKED, 128), BF16),
         compiler_params=BIG,
         name="pack_tokens",
-    )(gathered)
-
-
-def logits_kernel(first_ref, packed_ref, embedding_ref, labels_ref, slot_ref, e_ref, stats_ref, scale_ref, normed, logits):
-    y = pl.program_id(0)
-
-    @pl.when(y == 0)
-    def _():
-        gains = [packed_ref[b * 4, TILES * BLOCK : PACKED, :].astype(F32) for b in range(4)]
-        for x in range(4):
-            squares = jnp.zeros((BLOCK, 128), F32)
-            for b in range(4):
-                for k in range(TILES):
-                    v = packed_ref[b * 4 + x, k * BLOCK : (k + 1) * BLOCK, :].astype(F32)
-                    squares += v * v
-            scale = lax.rsqrt(jnp.sum(squares, axis=1, keepdims=True) / D + EPS)
-            scale_ref[x * BLOCK : (x + 1) * BLOCK, :] = jnp.broadcast_to(scale, (BLOCK, 128))
-            for b in range(4):
-                for k in range(TILES):
-                    v = packed_ref[b * 4 + x, k * BLOCK : (k + 1) * BLOCK, :].astype(F32)
-                    normed[b, x * BLOCK : (x + 1) * BLOCK, k * 128 : (k + 1) * 128] = (
-                        v * scale * gains[b][k : k + 1, :]
-                    ).astype(BF16)
-
-    term = lax.dot_general(
-        embedding_ref[...], normed[y], (((1,), (1,)), ((), ())), preferred_element_type=F32
+    )(near(gathered))
+
+
+def logits_kernel(first_ref, packed_ref, embedding_ref, labels_ref, slot_ref, e_ref, stats_ref, scale_ref, normed):
+    gains = [packed_ref[b * 4, TILES * BLOCK : PACKED, :].astype(F32) for b in range(4)]
+    for x in range(4):
+        squares = jnp.zeros((BLOCK, 128), F32)
+        for b in range(4):
+            for k in range(TILES):
+                v = packed_ref[b * 4 + x, k * BLOCK : (k + 1) * BLOCK, :].astype(F32)
+                squares += v * v
+        scale = lax.rsqrt(jnp.sum(squares, axis=1, keepdims=True) / D + EPS)
+        scale_ref[x * BLOCK : (x + 1) * BLOCK, :] = jnp.broadcast_to(scale, (BLOCK, 128))
+        for b in range(4):
+            for k in range(TILES):
+                v = packed_ref[b * 4 + x, k * BLOCK : (k + 1) * BLOCK, :].astype(F32)
+                normed[x * BLOCK : (x + 1) * BLOCK, b * WIDE + k * 128 : b * WIDE + (k + 1) * 128] = (
+                    v * scale * gains[b][k : k + 1, :]
+                ).astype(BF16)
+    raw = lax.dot_general(
+        embedding_ref[...], normed[...], (((1,), (1,)), ((), ())), preferred_element_type=F32
     )
-
-    @pl.when(y == 0)
-    def _():
-        logits[...] = term
-
-    @pl.when(y > 0)
-    def _():
-        logits[...] += term
-
-    @pl.when(y == 3)
-    def _():
-        raw = logits[...]
-        ratio = jnp.tanh(raw / CAP)
-        row = lax.broadcasted_iota(jnp.int32, raw.shape, 0)
-        inside = row < ROWS
-        is_label = jnp.logical_and(inside, row + first_ref[0] == labels_ref[...])
-        exps = jnp.where(inside, jnp.exp(CAP * ratio), 0.0)
-        others = jnp.where(is_label, 0.0, exps * (1.0 - ratio * ratio))
-        stats_ref[0:1, :] = jnp.sum(exps, axis=0, keepdims=True)
-        stats_ref[1:2, :] = jnp.sum(others * raw, axis=0, keepdims=True)
-        stats_ref[2:3, :] = jnp.sum(jnp.where(is_label, raw, 0.0), axis=0, keepdims=True)
-        stats_ref[3:8, :] = jnp.zeros((5, raw.shape[1]), F32)
-        e_ref[0:256, :] = others.T.astype(BF16)
-        e_ref[256:288, :] = slot_ref[...]
+    ratio = jnp.tanh(raw / CAP)
+    row = lax.broadcasted_iota(jnp.int32, raw.shape, 0)
+    inside = row < ROWS
+    is_label = jnp.logical_and(inside, row + first_ref[0] == labels_ref[...])
+    exps = jnp.where(inside, jnp.exp(CAP * ratio), 0.0)
+    others = jnp.where(is_label, 0.0, exps * (1.0 - ratio * ratio))
+    stats_ref[0:1, :] = jnp.sum(exps, axis=0, keepdims=True)
+    stats_ref[1:2, :] = jnp.sum(others * raw, axis=0, keepdims=True)
+    stats_ref[2:3, :] = jnp.sum(jnp.where(is_label, raw, 0.0), axis=0, keepdims=True)
+    stats_ref[3:8, :] = jnp.zeros((5, raw.shape[1]), F32)
+    e_ref[0:256, :] = others.T.astype(BF16)
+    e_ref[256:288, :] = slot_ref[...]
 
 
 def logits_of(first, packed, embedding, labels, slots):
     return pl.pallas_call(
         logits_kernel,
-        grid=(4,),
-        in_specs=[
-            pl.BlockSpec(memory_space=pltpu.MemorySpace.SMEM),
-            pl.BlockSpec((16, PACKED, 128), lambda y: (0, 0, 0)),
-            pl.BlockSpec((PADDED, WIDE), lambda y: (0, y)),
-            pl.BlockSpec((1, 256), lambda y: (0, 0)),
-            pl.BlockSpec((32, PADDED), lambda y: (0, 0)),
+        in_specs=[SCALARS] + [WHOLE] * 4,
+        out_specs=[WHOLE] * 3,
+        out_shape=[
+            pltpu.VMEM((288, PADDED), BF16),
+            pltpu.VMEM((8, 256), F32),
+            pltpu.VMEM((256, 128), F32),
         ],
-        out_specs=[
-            pl.BlockSpec((288, PADDED), lambda y: (0, 0)),
-            pl.BlockSpec((8, 256), lambda y: (0, 0)),
-            pl.BlockSpec((256, 128), lambda y: (0, 0)),
-        ],
-        out_shape=[
-            jax.ShapeDtypeStruct((288, PADDED), BF16),
-            jax.ShapeDtypeStruct((8, 256), F32),
-            jax.ShapeDtypeStruct((256, 128), F32),
-        ],
-        scratch_shapes=[pltpu.VMEM((4, 256, WIDE), BF16), pltpu.VMEM((PADDED, 256), F32)],
+        scratch_shapes=[pltpu.VMEM((256, D), BF16)],
         compiler_params=BIG,
         cost_estimate=pl.CostEstimate(flops=2 * 256 * PADDED * D, bytes_accessed=2 * PADDED * D, transcendentals=2 * 256 * PADDED),
         name="logits",
-    )(first, packed, embedding, labels, slots)
+    )(first, near(packed), near(embedding), near(labels), near(slots))
 
 
 def three_pieces(value):
@@ -171,48 +153,76 @@
     ]
 
 
-def gradient_kernel(with_other, *refs):
-    if with_other:
-        e_ref, embedding_ref, stats_ref, other_ref, out_ref = refs
-    else:
-        e_ref, embedding_ref, stats_ref, out_ref = refs
-    term = jnp.dot(e_ref[...], embedding_ref[...], preferred_element_type=F32)
+def gradient_kernel(e_ref, embedding_ref, stats_ref, out_ref):
+    last = lax.broadcasted_iota(jnp.int32, (8, WIDE), 0) == 7
+    rows = []
+    for x in range(4):
+        values = [stats_ref[i : i + 1, x * BLOCK : (x + 1) * BLOCK] for i in range(3)]
+        rows.append(jnp.broadcast_to(stats_row(values), (8, WIDE)))
+    for y in range(4):
+        term = jnp.dot(e_ref[...], embedding_ref[:, y * WIDE : (y + 1) * WIDE], preferred_element_type=F32)
+        for x in range(4):
+            out_ref[y * 4 + x, 0:BLOCK, :] = term[x * BLOCK : (x + 1) * BLOCK, :].astype(BF16)
+            extra = term[256 + 8 * x : 256 + 8 * x + 8, :]
+            out_ref[y * 4 + x, BLOCK : BLOCK + 8, :] = jnp.where(last, rows[x], extra).astype(BF16)
+
+
+def gradient_of(e, embedding, stats):
+    return pl.pallas_call(
+        gradient_kernel,
+        in_specs=[WHOLE] * 3,
+        out_specs=WHOLE,
+        out_shape=pltpu.VMEM((16, BLOCK + 8, WIDE), BF16),
+        compiler_params=BIG,
+        cost_estimate=pl.CostEstimate(flops=2 * 288 * PADDED * D, bytes_accessed=2 * PADDED * D, transcendentals=0),
+        name="gradient",
+    )(e, near(embedding), stats)
+
+
+def product_kernel(e_ref, embedding_ref, out_ref):
+    for y in range(4):
+        out_ref[:, y * WIDE : (y + 1) * WIDE] = jnp.dot(
+            e_ref[...], embedding_ref[:, y * WIDE : (y + 1) * WIDE], preferred_element_type=F32
+        )
+
+
+def product_of(e, embedding):
+    return pl.pallas_call(
+        product_kernel,
+        in_specs=[WHOLE] * 2,
+        out_specs=WHOLE,
+        out_shape=pltpu.VMEM((288, D), F32),
+        compiler_params=BIG,
+        cost_estimate=pl.CostEstimate(flops=2 * 288 * PADDED * D, bytes_accessed=2 * PADDED * D, transcendentals=0),
+        name="product",
+    )(e, near(embedding))
+
+
+def combine_kernel(term_ref, stats_ref, other_ref, out_ref):
     last = lax.broadcasted_iota(jnp.int32, (8, WIDE), 0) == 7
     for x in range(4):
-        main = term[x * BLOCK : (x + 1) * BLOCK, :]
-        extra = term[256 + 8 * x : 256 + 8 * x + 8, :]
         values = [stats_ref[i : i + 1, x * BLOCK : (x + 1) * BLOCK] for i in range(3)]
-        if with_other:
-            main = main + other_ref[x, 0:BLOCK, :].astype(F32)
-            other_extra = other_ref[x, BLOCK : BLOCK + 8, :].astype(F32)
-            extra = extra + other_extra
-            values = [a + b for a, b in zip(values, read_stats(other_extra[7:8, :]))]
-        row = jnp.broadcast_to(stats_row(values), (8, WIDE))
-        out_ref[x, 0:BLOCK, :] = main.astype(BF16)
-        out_ref[x, BLOCK : BLOCK + 8, :] = jnp.where(last, row, extra).astype(BF16)
-
-
-def gradient_of(e, embedding, stats, other=None):
-    payload = pl.BlockSpec((4, BLOCK + 8, WIDE), lambda y: (y, 0, 0))
-    in_specs = [
-        pl.BlockSpec((288, PADDED), lambda y: (0, 0)),
-        pl.BlockSpec((PADDED, WIDE), lambda y: (0, y)),
-        pl.BlockSpec((8, 256), lambda y: (0, 0)),
-    ]
-    args = [e, embedding, stats]
-    if other is not None:
-        in_specs.append(payload)
-        args.append(other)
-    return pl.pallas_call(
-        functools.partial(gradient_kernel, other is not None),
-        grid=(4,),
-        in_specs=in_specs,
-        out_specs=payload,
-        out_shape=jax.ShapeDtypeStruct((16, BLOCK + 8, WIDE), BF16),
-        compiler_params=BIG,
-        cost_estimate=pl.CostEstimate(flops=2 * 288 * PADDED * D, bytes_accessed=2 * PADDED * D, transcendentals=0),
-        name="gradient",
-    )(*args)
+        others = read_stats(other_ref[x, BLOCK : BLOCK + 8, :].astype(F32)[7:8, :])
+        row = jnp.broadcast_to(stats_row([a + b for a, b in zip(values, others)]), (8, WIDE))
+        for y in range(4):
+            columns = slice(y * WIDE, (y + 1) * WIDE)
+            main = term_ref[x * BLOCK : (x + 1) * BLOCK, columns] + other_ref[y * 4 + x, 0:BLOCK, :].astype(F32)
+            out_ref[y * 4 + x, 0:BLOCK, :] = main.astype(BF16)
+            extra = term_ref[256 + 8 * x : 256 + 8 * x + 8, columns] + other_ref[
+                y * 4 + x, BLOCK : BLOCK + 8, :
+            ].astype(F32)
+            out_ref[y * 4 + x, BLOCK : BLOCK + 8, :] = jnp.where(last, row, extra).astype(BF16)
+
+
+def combine(term, stats, other):
+    return pl.pallas_call(
+        combine_kernel,
+        in_specs=[WHOLE] * 3,
+        out_specs=WHOLE,
+        out_shape=pltpu.VMEM((16, BLOCK + 8, WIDE), BF16),
+        compiler_params=BIG,
+        name="combine",
+    )(term, stats, near(other))
 
 
 def plane_kernel(in_ref, place_ref, more_ref, out_ref):
@@ -242,10 +252,12 @@
 def plane_sum(received, place, more):
     return pl.pallas_call(
         plane_kernel,
-        out_shape=jax.ShapeDtypeStruct((8, 48, 640), BF16),
+        in_specs=[WHOLE] * 3,
+        out_specs=WHOLE,
+        out_shape=pltpu.VMEM((8, 48, 640), BF16),
         compiler_params=BIG,
         name="plane_sum",
-    )(received, place, more)
+    )(near(received), near(place), near(more))
 
 
 def final_kernel(half_ref, in_ref, values_ref, gain_ref, weight_ref, scale_ref, loss_ref, grad_ref):
@@ -282,15 +294,14 @@
 
 
 def finish(half, received, values, gain, weight, scale):
-    spec = pl.BlockSpec(memory_space=VMEM)
     return pl.pallas_call(
         final_kernel,
-        in_specs=[pl.BlockSpec(memory_space=pltpu.MemorySpace.SMEM)] + [spec] * 5,
-        out_specs=[spec] * 2,
+        in_specs=[SCALARS] + [WHOLE] * 5,
+        out_specs=[WHOLE] * 2,
         out_shape=[jax.ShapeDtypeStruct((1, 128), F32), jax.ShapeDtypeStruct((32, PIECE), F32)],
         compiler_params=BIG,
         name="finish",
-    )(half, received, values, gain, weight, scale)
+    )(half, *(near(a) for a in (received, values, gain, weight, scale)))
 
 
 def swap_cores(array):
@@ -306,7 +317,8 @@
     gathered = lax.all_to_all(
         jnp.broadcast_to(mine[None], (8, 48, PIECE)), ("z_lo", "z_hi"), 0, 0, tiled=True
     )
-    packed = lax.all_to_all(pack_tokens(gathered), ("y", "x"), 0, 0, tiled=True)
+    copies, late_embedding = lax.optimization_barrier((pack_tokens(gathered), embedding))
+    packed = lax.all_to_all(copies, ("y", "x"), 0, 0, tiled=True)
 
     token = jnp.arange(512, dtype=jnp.int32)
     group = (token // 32) % 2 * 4 + (token // 64) % 4
@@ -339,12 +351,12 @@
         at = own_slot[:, None] == jnp.arange(8, dtype=jnp.int32)[None, :]
         return jnp.logical_and(hit[:, :, None], at[:, None, :]).astype(BF16).reshape(BLOCK, 128)
 
-    table = permute_embedding(embedding)
+    table = permute_embedding(late_embedding)
 
     def more_rows(carry):
         number, rows = carry
-        found = jnp.dot(slot_rows(number), table, preferred_element_type=F32).astype(BF16)
-        found = found.reshape(2, 4, 8, 4, WIDE).transpose(0, 3, 1, 2, 4).reshape(2, 16, 8, WIDE)
+        found = jnp.dot(slot_rows(number)[:, :ROWS], embedding, preferred_element_type=F32).astype(BF16)
+        found = found.reshape(2, 4, 8, 4, 4, PIECE).transpose(0, 4, 1, 2, 3, 5).reshape(2, 16, 8, WIDE)
         ours = lax.dynamic_index_in_dim(found, core, 0, keepdims=False)
         theirs = lax.dynamic_index_in_dim(found, 1 - core, 0, keepdims=False)
         ours = ours + swap_cores(theirs)
@@ -363,18 +375,30 @@
         return lax.dynamic_index_in_dim(array, which, 0, keepdims=False)
 
     start = first.reshape(1)
-    other_packed = swap_cores(packed)
-    e, stats, scale = logits_of(start, packed, table, half_of(label_halves, core), half_of(slot_halves, core))
-    e_other, stats_other, _ = logits_of(
-        start, other_packed, table, half_of(label_halves, 1 - core), half_of(slot_halves, 1 - core)
-    )
-    from_other = swap_cores(gradient_of(e_other, table, stats_other))
-    payload = gradient_of(e, table, stats, from_other)
-    plane = lax.all_to_all(payload, ("y", "x"), 0, 0, tiled=True)
-    column = lax.all_to_all(plane_sum(plane, places(0), more), ("z_lo", "z_hi"), 0, 0, tiled=True)
-
     own_first = ((zh * 4 + x) * 2 + core) * 32
     weight = lax.dynamic_slice_in_dim(token_weight, own_first, 32, 0).reshape(32, 1)
+    early = (
+        table,
+        half_of(label_halves, core),
+        half_of(slot_halves, core),
+        half_of(label_halves, 1 - core),
+        half_of(slot_halves, 1 - core),
+        places(0),
+        more,
+        weight,
+    )
+    packed, early = lax.optimization_barrier((packed, early))
+    table, own_labels, own_slots, other_labels, other_slots, place, more, weight = early
+    other_packed = swap_cores(packed)
+    e, stats, scale = logits_of(start, packed, table, own_labels, own_slots)
+    other_packed, e = lax.optimization_barrier((other_packed, e))
+    e_other, stats_other, _ = logits_of(start, other_packed, table, other_labels, other_slots)
+    other_part = gradient_of(e_other, table, stats_other)
+    other_part, e = lax.optimization_barrier((other_part, e))
+    payload = combine(product_of(e, table), stats, swap_cores(other_part))
+    plane = lax.all_to_all(payload, ("y", "x"), 0, 0, tiled=True)
+    column = lax.all_to_all(plane_sum(plane, place, more), ("z_lo", "z_hi"), 0, 0, tiled=True)
+
     own_scale = lax.dynamic_slice_in_dim(scale, x * BLOCK + zh * 32, 32, 0)
     loss, grad = finish(zh.reshape(1), column, residual, final_gain.reshape(1, PIECE), weight, own_scale)
     return (loss[0, 0:32], grad)

time: 191 us -> 159 us (0.83)
  blocking collectives: 58.1 us -> 0 us
  waiting for transfers between devices: 54.2 us -> 89.7 us
  Pallas kernels: 55.1 us -> 27.1 us
  starting transfers between devices: 7.18 us -> 23.4 us
    all_to_all x2 -> x0, blocking collectives: 58.1 us -> none  [the longest x1 38.6 us: on_device(): packed = lax.all_to_all(pack_tokens(gathered), ('y', 'x'), 0, 0, tiled=True)]
    all_to_all x1 -> x3, waiting for transfers between devices: 12.3 us -> 45.9 us  [the longest x1 24.1 us: on_device(): packed = lax.all_to_all(copies, ('y', 'x'), 0, 0, tiled=True)]
    pallas_call x7 -> x8, Pallas kernels: 42.6 us -> 18.3 us  [the longest x2 6.92 us: logits_of(): pl.pallas_call(logits_kernel, in_specs=[SCALARS] + [WHOLE] * 4, out_specs...]
    all_to_all x1 -> x3, starting transfers between devices: 3.43 us -> 19 us  [the longest x1 8.57 us: on_device(): lax.all_to_all(jnp.broadcast_to(mine[None], (8, 48, PIECE)), ('z_lo', 'z_...]
    unnamed x18 -> x16, local copies, waits for them, and re-layouts: 3.84 us -> 8.86 us
    pallas_call x1, Pallas kernels: 12.5 us -> 8.75 us  [permute_embedding(): pl.pallas_call(permute_kernel, grid=(PADDED // step,), in_specs=[pl.Block...]
  transfers between devices with their start and end apart: 4 -> 6, of which waited for: 2 -> 5; matrix products, arithmetic and copies ran while one was open for 4% -> 2% of each run, Pallas kernels for 12% -> 10%
where the time goes in v2:
time: 159 us; the launch traced here: 158 us
  waiting for transfers between devices  89.7 us (56%)
  Pallas kernels  27.1 us (17%)
  starting transfers between devices  23.4 us (15%)
  local copies, waits for them, and re-layouts  12.7 us (8%)
  other arithmetic  3.43 us (2%)
    all_to_all x1, waiting for transfers between devices, on_device(): plane = lax.all_to_all(payload, ('y', 'x'), 0, 0, tiled=True)  42.4 us
    all_to_all x1, waiting for transfers between devices, on_device(): packed = lax.all_to_all(copies, ('y', 'x'), 0, 0, tiled=True)  24.1 us
    all_to_all x1, waiting for transfers between devices, on_device(): lax.all_to_all(plane_sum(plane, place, more), ('z_lo', 'z_hi'), 0, 0, til...  14.2 us
    unnamed x16, local copies, waits for them, and re-layouts  8.86 us
    pallas_call x1, Pallas kernels, permute_embedding(): pl.pallas_call(permute_kernel, grid=(PADDED // step,), in_specs=[pl.Block...  8.75 us
    all_to_all x1, starting transfers between devices, on_device(): lax.all_to_all(jnp.broadcast_to(mine[None], (8, 48, PIECE)), ('z_lo', 'z_...  8.57 us
    all_to_all x1, waiting for transfers between devices, on_device(): lax.all_to_all(jnp.broadcast_to(mine[None], (8, 48, PIECE)), ('z_lo', 'z_...  7.62 us
    all_to_all x1, starting transfers between devices, on_device(): packed = lax.all_to_all(copies, ('y', 'x'), 0, 0, tiled=True)  7.05 us
  transfers between devices with their start and end apart: 6, of which 5 were waited for; matrix products, arithmetic and copies ran while one was open for 2% of the time, Pallas kernels for 10%

profile of v2, /device:TPU:32, one launch (start us, length us, event | category | flops | bytes accessed | tf_op | source)
XLA Modules:
  0.0 157.8 jit_solution(15254110963053771361)
XLA Ops:
  1.4 0.7 multiply_add_fusion
  2.4 0.8 maximum_maximum_fusion
  3.2 0.7 broadcast_in_dim.57
  3.9 8.6 %all-to-all-start.1 = ((bf16[8,48,288]{2,1,0:T(8,128)(2,1)}), bf16[8,48,288]{2,1,0:T(8,128)(2,1)S(1)}, u32[]{:S(2)}, u32[]{:S(2)}) async-start(bf16[8,48,288]{2,1,0:T(8,128)(2,1)} %broadcast_in_dim.57), calls=%async_computation.1 | async-start | bytes 589824 | tf_op jit(solution)/shard_map/all_to_all | solution.py:317
  15.6 7.6 %all-to-all-done.1.in_ref = bf16[8,48,288]{2,1,0:T(8,128)(2,1)S(1)} async-done(((bf16[8,48,288]{2,1,0:T(8,128)(2,1)}), bf16[8,48,288]{2,1,0:T(8,128)(2,1)S(1)}, u32[]{:S(2)}, u32[]{:S(2)}) %all-to-all-start.1) | async-done | bytes 221216 | tf_op jit(solution)/shard_map/all_to_all | solution.py:317
  23.2 1.6 %pack_tokens.1 = bf16[16,592,128]{2,1,0:T(8,128)(2,1)} custom-call(bf16[8,48,288]{2,1,0:T(8,128)(2,1)S(1)} %all-to-all-done.1.in_ref), custom_call_target="tpu_custom_call" | custom-call | tf_op jit(solution)/shard_map/pack_tokens/pallas_call | solution.py:74
  24.9 7.0 %all-to-all-start.2 = ((bf16[16,592,128]{2,1,0:T(8,128)(2,1)}), bf16[16,592,128]{2,1,0:T(8,128)(2,1)S(1)}, u32[]{:S(2)}, u32[]{:S(2)}) async-start(bf16[16,592,128]{2,1,0:T(8,128)(2,1)} %pack_tokens.1), calls=%async_computation.2 | async-start | bytes 4849664 | tf_op jit(solution)/shard_map/all_to_all | solution.py:321
  32.9 8.7 %permute_embedding.1.embedding_ref = bf16[1024,4608]{1,0:T(8,128)(2,1)S(1)} custom-call(bf16[1000,4608]{1,0:T(8,128)(2,1)} %get-tuple-element.643), custom_call_target="tpu_custom_call" | custom-call | bytes 18432000 | tf_op jit(solution)/shard_map/permute_embedding/pallas_call | solution.py:46
  41.7 3.6 %copy-done.1 = bf16[1024,4608]{1,0:T(8,128)(2,1)} copy-done((bf16[1024,4608]{1,0:T(8,128)(2,1)}, bf16[1024,4608]{1,0:T(8,128)(2,1)S(1)}, u32[]{:S(2)}) %copy-start.1) | copy-done | bytes 9437208
  45.3 24.1 %all-to-all-done.2.packed_ref = bf16[16,592,128]{2,1,0:T(8,128)(2,1)S(1)} async-done(((bf16[16,592,128]{2,1,0:T(8,128)(2,1)}), bf16[16,592,128]{2,1,0:T(8,128)(2,1)S(1)}, u32[]{:S(2)}, u32[]{:S(2)}) %all-to-all-start.2) | async-done | bytes 2424864 | tf_op jit(solution)/shard_map/all_to_all | solution.py:321
  69.4 3.7 %copy-done.2 = bf16[1024,4608]{1,0:T(8,128)(2,1)S(1)} copy-done((bf16[1024,4608]{1,0:T(8,128)(2,1)S(1)}, bf16[1024,4608]{1,0:T(8,128)(2,1)}, u32[]{:S(2)}) %copy-start.2) | copy-done | bytes 9437208
  73.1 3.3 %logits.2 = (bf16[288,1024]{1,0:T(8,128)(2,1)S(1)}, f32[8,256]{1,0:T(8,128)S(1)}, f32[256,128]{1,0:T(8,128)S(1)}) custom-call(s32[1]{0:T(128)} %bitcast.1.first_ref, bf16[16,592,128]{2,1,0:T(8,128)(2,1)S(1)} %all-to-all-done.2.packed_ref, bf16[1024,4608]{1,0:T(8,128)(2,1)S(1)} %copy-done.2, s32[1,256]{1,0:T(1,128)S(1)} %get-tuple-element.266.labels_ref, ...), custom_call_target="tpu_custom_call" | custom-call | flops 2415919104 | bytes 9437184 | tf_op jit(solution)/shard_map/logits/pallas_call | solution.py:118
  76.5 3.6 %logits.3 = (bf16[288,1024]{1,0:T(8,128)(2,1)S(1)}, f32[8,256]{1,0:T(8,128)S(1)}, f32[256,128]{1,0:T(8,128)}) custom-call(s32[1]{0:T(128)} %bitcast.1.first_ref, bf16[16,592,128]{2,1,0:T(8,128)(2,1)S(1)} %collective-permute-done.1.packed_ref, bf16[1024,4608]{1,0:T(8,128)(2,1)S(1)} %copy-done.2, s32[1,256]{1,0:T(1,128)S(1)} %get-tuple-element.270.labels_ref, ...), custom_call_target="tpu_custom_call" | custom-call | flops 2415919104 | bytes 9437184 | tf_op jit(solution)/shard_map/logits/pallas_call | solution.py:118
  80.1 3.3 %gradient.1 = bf16[16,72,1152]{2,1,0:T(8,128)(2,1)S(1)} custom-call(bf16[288,1024]{1,0:T(8,128)(2,1)S(1)} %get-tuple-element.272.e_ref, bf16[1024,4608]{1,0:T(8,128)(2,1)S(1)} %copy-done.2, f32[8,256]{1,0:T(8,128)S(1)} %get-tuple-element.273.stats_ref), custom_call_target="tpu_custom_call" | custom-call | flops 2717908992 | bytes 9437184 | tf_op jit(solution)/shard_map/gradient/pallas_call | solution.py:171
  84.0 3.2 %product.1.term_ref = f32[288,4608]{1,0:T(8,128)S(1)} custom-call(bf16[288,1024]{1,0:T(8,128)(2,1)S(1)} %get-tuple-element.275.e_ref, bf16[1024,4608]{1,0:T(8,128)(2,1)S(1)} %copy-done.2), custom_call_target="tpu_custom_call" | custom-call | flops 2717908992 | bytes 9437184 | tf_op jit(solution)/shard_map/product/pallas_call | solution.py:190
  87.2 1.3 collective-permute-done.2.other_ref
  88.5 1.0 combine.1
  89.6 1.5 copy-done.3
  91.1 3.7 %all-to-all-start.3 = ((bf16[16,72,1152]{2,1,0:T(8,128)(2,1)}), bf16[16,72,1152]{2,1,0:T(8,128)(2,1)S(1)}, u32[]{:S(2)}, u32[]{:S(2)}) async-start(bf16[16,72,1152]{2,1,0:T(8,128)(2,1)} %copy-done.3), calls=%async_computation.3 | async-start | bytes 5308416 | tf_op jit(solution)/shard_map/all_to_all | solution.py:399
  94.9 42.4 %all-to-all-done.3.in_ref = bf16[16,72,1152]{2,1,0:T(8,128)(2,1)S(1)} async-done(((bf16[16,72,1152]{2,1,0:T(8,128)(2,1)}), bf16[16,72,1152]{2,1,0:T(8,128)(2,1)S(1)}, u32[]{:S(2)}, u32[]{:S(2)}) %all-to-all-start.3) | async-done | bytes 2654240 | tf_op jit(solution)/shard_map/all_to_all | solution.py:399
  137.4 1.3 plane_sum.1
  138.6 3.4 %all-to-all-start.4 = ((bf16[8,48,640]{2,1,0:T(8,128)(2,1)}), bf16[8,48,640]{2,1,0:T(8,128)(2,1)S(1)}, u32[]{:S(2)}, u32[]{:S(2)}) async-start(bf16[8,48,640]{2,1,0:T(8,128)(2,1)} %plane_sum.1), calls=%async_computation.4 | async-start | bytes 983040 | tf_op jit(solution)/shard_map/all_to_all | solution.py:400
  142.2 14.2 %all-to-all-done.4.in_ref = bf16[8,48,640]{2,1,0:T(8,128)(2,1)S(1)} async-done(((bf16[8,48,640]{2,1,0:T(8,128)(2,1)}), bf16[8,48,640]{2,1,0:T(8,128)(2,1)S(1)}, u32[]{:S(2)}, u32[]{:S(2)}) %all-to-all-start.4) | async-done | bytes 491552 | tf_op jit(solution)/shard_map/all_to_all | solution.py:400
  156.3 1.0 finish.1
  (55 shorter events, 5.6 us)
Async XLA Ops:
  0.6 31.9 %copy-start = (f32[512]{0:T(512)S(1)}, f32[512]{0:T(512)}, u32[]{:S(2)}) copy-start(f32[512]{0:T(512)} %param.11) | copy-start | bytes 6148
  0.6 24.3 %copy-start.5 = (s32[512]{0:T(512)S(1)}, s32[512]{0:T(512)}, u32[]{:S(2)}) copy-start(s32[512]{0:T(512)} %param.10) | copy-start | bytes 6148
  3.9 19.3 %all-to-all-start.1 = ((bf16[8,48,288]{2,1,0:T(8,128)(2,1)}), bf16[8,48,288]{2,1,0:T(8,128)(2,1)S(1)}, u32[]{:S(2)}, u32[]{:S(2)}) async-start(bf16[8,48,288]{2,1,0:T(8,128)(2,1)} %broadcast_in_dim.57), calls=%async_computation.1 | async-start | bytes 589824 | tf_op jit(solution)/shard_map/all_to_all | solution.py:317
  15.4 9.5 %copy-start.6 = (s32[2,1,1,32]{3,2,1,0:T(1,128)}, s32[2,1,1,32]{3,2,1,0:T(1,128)S(1)}, u32[]{:S(2)}) copy-start(s32[2,1,1,32]{3,2,1,0:T(1,128)S(1)} %get-tuple-element.364) | copy-start | bytes 772
  15.4 9.5 %copy-start.7 = (s32[2,1,1,32]{3,2,1,0:T(1,128)}, s32[2,1,1,32]{3,2,1,0:T(1,128)S(1)}, u32[]{:S(2)}) copy-start(s32[2,1,1,32]{3,2,1,0:T(1,128)S(1)} %get-tuple-element.382) | copy-start | bytes 772
  24.9 44.5 %all-to-all-start.2 = ((bf16[16,592,128]{2,1,0:T(8,128)(2,1)}), bf16[16,592,128]{2,1,0:T(8,128)(2,1)S(1)}, u32[]{:S(2)}, u32[]{:S(2)}) async-start(bf16[16,592,128]{2,1,0:T(8,128)(2,1)} %pack_tokens.1), calls=%async_computation.2 | async-start | bytes 4849664 | tf_op jit(solution)/shard_map/all_to_all | solution.py:321
  41.7 3.6 %copy-start.1 = (bf16[1024,4608]{1,0:T(8,128)(2,1)}, bf16[1024,4608]{1,0:T(8,128)(2,1)S(1)}, u32[]{:S(2)}) copy-start(bf16[1024,4608]{1,0:T(8,128)(2,1)S(1)} %permute_embedding.1.embedding_ref) | copy-start | bytes 28311556
  69.4 7.0 %collective-permute-start.1 = (bf16[16,592,128]{2,1,0:T(8,128)(2,1)S(1)}, bf16[16,592,128]{2,1,0:T(8,128)(2,1)S(1)}, u32[]{:S(2)}, u32[]{:S(2)}) collective-permute-start(bf16[16,592,128]{2,1,0:T(8,128)(2,1)S(1)} %all-to-all-done.2.packed_ref), channel_id=1, source_target_pairs={{0,1},{1,0},{2,3},{3,2},{4,5},{5,4},{6,7},{7,6},{8,9},{9,8},{10,11... | collective-permute-start | bytes 7274504 | tf_op jit(solution)/shard_map/ppermute | solution.py:308
  69.4 3.7 %copy-start.2 = (bf16[1024,4608]{1,0:T(8,128)(2,1)S(1)}, bf16[1024,4608]{1,0:T(8,128)(2,1)}, u32[]{:S(2)}) copy-start(bf16[1024,4608]{1,0:T(8,128)(2,1)} %copy-done.1) | copy-start | bytes 28311556
  83.4 5.2 %collective-permute-start.2 = (bf16[16,72,1152]{2,1,0:T(8,128)(2,1)S(1)}, bf16[16,72,1152]{2,1,0:T(8,128)(2,1)S(1)}, u32[]{:S(2)}, u32[]{:S(2)}) collective-permute-start(bf16[16,72,1152]{2,1,0:T(8,128)(2,1)S(1)} %gradient.1), channel_id=1, source_target_pairs={{0,1},{1,0},{2,3},{3,2},{4,5},{5,4},{6,7},{7,6},{8,9},{9,8},{10,11... | collective-permute-start | bytes 7962632 | tf_op jit(solution)/shard_map/ppermute | solution.py:308
  89.6 1.5 copy-start.3
  91.1 46.3 %all-to-all-start.3 = ((bf16[16,72,1152]{2,1,0:T(8,128)(2,1)}), bf16[16,72,1152]{2,1,0:T(8,128)(2,1)S(1)}, u32[]{:S(2)}, u32[]{:S(2)}) async-start(bf16[16,72,1152]{2,1,0:T(8,128)(2,1)} %copy-done.3), calls=%async_computation.3 | async-start | bytes 5308416 | tf_op jit(solution)/shard_map/all_to_all | solution.py:399
  94.8 61.5 %copy-start.4 = (bf16[32,288]{1,0:T(8,128)(2,1)S(1)}, bf16[32,288]{1,0:T(8,128)(2,1)}, u32[]{:S(2)}) copy-start(bf16[32,288]{1,0:T(8,128)(2,1)} %values_ref.1) | copy-start | bytes 55300
  138.6 17.7 %all-to-all-start.4 = ((bf16[8,48,640]{2,1,0:T(8,128)(2,1)}), bf16[8,48,640]{2,1,0:T(8,128)(2,1)S(1)}, u32[]{:S(2)}, u32[]{:S(2)}) async-start(bf16[8,48,640]{2,1,0:T(8,128)(2,1)} %plane_sum.1), calls=%async_computation.4 | async-start | bytes 983040 | tf_op jit(solution)/shard_map/all_to_all | solution.py:400

commit v3 on v2

v3 whole, which is shorter than its diff:
```python
import functools

import jax
import jax.numpy as jnp
from jax import lax
from jax.experimental import pallas as pl
from jax.experimental.pallas import tpu as pltpu
from jax.sharding import Mesh, PartitionSpec as P

D = 4608
EPS = 1e-06
CAP = 30.0
ROWS = 1000
PADDED = 1024
PIECE = 288
WIDE = 1152
HALF = 2 * WIDE
BLOCK = 64
ROOM = BLOCK + 8
TILES = WIDE // 128
SLOTS = 7
PACKED = TILES * BLOCK + 16
F32 = jnp.float32
BF16 = jnp.bfloat16
VMEM = pltpu.MemorySpace.VMEM
WHOLE = pl.BlockSpec(memory_space=VMEM)
SCALARS = pl.BlockSpec(memory_space=pltpu.MemorySpace.SMEM)
BIG = pltpu.CompilerParams(vmem_limit_bytes=20 * 1024 * 1024)


def near(array):
    return pltpu.with_memory_space_constraint(array, VMEM)


CHIPS = ("z_lo", "y1", "y0", "z_hi", "x1", "x0")
SHIFTS = {(0, 1): (1, 0), (1, 0): (0, 1), (1, 1): (-1, -1)}


def this_chip():
    number = 0
    for name in CHIPS:
        number = number * lax.axis_size(name) + lax.axis_index(name)
    return number


def first_row():
    return (this_chip() * 2 + lax.axis_index("core")) * ROWS


def label_kernel(labels_ref, own_labels, own_slots, other_labels, other_slots, place_ref, rounds_ref):
    zl, y1, y0, zh, x1, x0, core = (lax.axis_index(name) for name in (*CHIPS, "core"))
    labels = labels_ref[...]
    token = lax.broadcasted_iota(jnp.int32, (1, 512), 1)
    group = (token >> 5 & 1) * 4 + (token >> 6 & 1) * 2 + (token >> 7 & 1)
    owner = ((labels.astype(F32) + 0.5) * (1.0 / (2 * ROWS))).astype(jnp.int32)
    key = owner * 8 + group
    square = (512, 512)
    down = lax.broadcasted_iota(jnp.int32, square, 0)
    across = lax.broadcasted_iota(jnp.int32, square, 1)
    keys = jnp.broadcast_to(key, square)
    key_down = jnp.sum(jnp.where(down == across, keys, 0), axis=1, keepdims=True)
    earlier = jnp.logical_and(jnp.broadcast_to(key_down, square) == keys, down < across)
    rank = jnp.sum(earlier.astype(jnp.int32), axis=0, keepdims=True)
    turn = ((rank.astype(F32) + 0.5) * (1.0 / SLOTS)).astype(jnp.int32)
    slot = rank - turn * SLOTS
    rounds_ref[...] = jnp.broadcast_to(jnp.max(turn, axis=1, keepdims=True) + 1, (1, 128))

    taken = jnp.where(jnp.logical_and(owner == this_chip(), turn == 0), group * 8 + slot, -1)
    shifted_labels = labels - first_row() + 1
    for half, label_ref, slot_ref in ((core, own_labels, own_slots), (1 - core, other_labels, other_slots)):
        at = lax.broadcasted_iota(jnp.int32, (32, 512), 0)
        wanted = half * 32 + (at + 16 * x0 & 31)
        match = jnp.broadcast_to(taken, (32, 512)) == wanted
        held = jnp.sum(jnp.where(match, jnp.broadcast_to(shifted_labels, (32, 512)), 0), axis=1, keepdims=True) - 1
        vocab = lax.broadcasted_iota(jnp.int32, (32, PADDED), 1)
        slot_ref[...] = jnp.where(vocab == held, 1.0, 0.0).astype(BF16)
        chunks = []
        for chunk in range(8):
            rx, from_x1, from_zh = chunk // 4, chunk // 2 % 2, chunk % 2
            picked = jnp.zeros((1, 32), jnp.int32)
            for from_x0 in range(2):
                for from_core in range(2):
                    source = ((from_zh * 2 + from_x1) * 2 + from_x0) * 2 + from_core
                    use = jnp.logical_and(half == from_core, (x0 + rx) % 2 == from_x0)
                    picked = jnp.where(use, labels[:, source * 32 : source * 32 + 32], picked)
            chunks.append(picked)
        label_ref[...] = jnp.concatenate(chunks, axis=1)

    code = jnp.broadcast_to(jnp.where(turn == 0, owner * 8 + slot, -1), (BLOCK, 512))
    at = lax.broadcasted_iota(jnp.int32, (BLOCK, 512), 0)
    own = (at >> 5) * 256 + x1 * 128 + x0 * 64 + core * 32 + (at & 31)
    pick = lax.broadcasted_iota(jnp.int32, (BLOCK, 512), 1) == own
    own_code = jnp.sum(jnp.where(pick, code, 0), axis=1, keepdims=True)
    column = lax.broadcasted_iota(jnp.int32, (BLOCK, 128), 1)
    parity = column >> 3 & 3
    from_y = (column >> 6) * 2 + y0 + 4
    from_x = (column >> 5 & 1) * 2 + x0 + 4
    for index, (dx, dy) in enumerate(SHIFTS.values()):
        from_y = from_y - jnp.where(parity == index + 1, dy, 0)
        from_x = from_x - jnp.where(parity == index + 1, dx, 0)
    chip = ((zl * 4 + (from_y & 3)) * 2 + zh) * 4 + (from_x & 3)
    place_ref[...] = jnp.where(own_code == chip * 8 + (column & 7), 1.0, 0.0).astype(BF16)


def label_places(labels):
    return pl.pallas_call(
        label_kernel,
        in_specs=[WHOLE],
        out_specs=[WHOLE] * 6,
        out_shape=[
            pltpu.VMEM((1, 256), jnp.int32),
            pltpu.VMEM((32, PADDED), BF16),
            pltpu.VMEM((1, 256), jnp.int32),
            pltpu.VMEM((32, PADDED), BF16),
            pltpu.VMEM((BLOCK, 128), BF16),
            jax.ShapeDtypeStruct((1, 128), jnp.int32),
        ],
        compiler_params=BIG,
        cost_estimate=pl.CostEstimate(flops=10 * 512 * 512, bytes_accessed=1 << 20, transcendentals=0),
        name="label_places",
    )(labels)


def permute_kernel(in_ref, out_ref):
    step = in_ref.shape[0]
    first = pl.multiple_of(pl.program_id(0) * step, step)
    rows = first + lax.broadcasted_iota(jnp.int32, (step, 1), 0)
    block = jnp.where(rows < ROWS, in_ref[...].astype(F32), 0.0)
    for y0 in range(2):

        @pl.when(lax.axis_index("y0") == y0)
        def _():
            for at in range(4):
                y = at % 2 * 2 + (at // 2 + y0) % 2
                parts = [block[:, (z * 4 + y) * PIECE : (z * 4 + y + 1) * PIECE] for z in range(4)]
                wide = jnp.concatenate(parts, axis=1).astype(BF16)
                out_ref[pl.ds(first, step), at * WIDE : (at + 1) * WIDE] = wide


def permute_embedding(embedding):
    step = 128
    return pl.pallas_call(
        permute_kernel,
        grid=(PADDED // step,),
        in_specs=[pl.BlockSpec((step, D), lambda i: (i, 0))],
        out_specs=WHOLE,
        out_shape=pltpu.VMEM((PADDED, D), BF16),
        compiler_params=BIG,
        cost_estimate=pl.CostEstimate(flops=0, bytes_accessed=4 * ROWS * D, transcendentals=0),
        name="permute_embedding",
    )(embedding)


def spread_kernel(residual_ref, gain_ref, out_ref):
    values = residual_ref[...].astype(F32)
    gain = gain_ref[...].astype(F32)
    corner = jnp.concatenate([values[8 * g : 8 * g + 8, 256:PIECE] for g in range(4)], axis=1)
    last = jnp.concatenate([gain[:, 256:PIECE], jnp.zeros((1, 96), F32)], axis=1)
    rows = [values[:, 0:128], values[:, 128:256], corner, gain[:, 0:128], gain[:, 128:256], last, jnp.zeros((5, 128), F32)]
    tiles = jnp.concatenate(rows, axis=0).astype(BF16)
    for copy in range(8):
        out_ref[copy] = tiles


def spread(residual, gain):
    return pl.pallas_call(
        spread_kernel,
        in_specs=[WHOLE] * 2,
        out_specs=WHOLE,
        out_shape=pltpu.VMEM((8, 80, 128), BF16),
        compiler_params=BIG,
        name="spread",
    )(residual, gain)


def pack_kernel(in_ref, out_ref):
    for zh in range(2):
        parts = []
        for zl in range(4):
            tiles = in_ref[zl * 2 + zh].astype(F32)
            corner = jnp.concatenate([tiles[64:72, 32 * g : 32 * g + 32] for g in range(4)], axis=0)
            parts += [tiles[0:32, :], tiles[32:64, :], corner]
        wide = jnp.concatenate(parts, axis=1)
        for k in range(TILES):
            tile = wide[:, k * 128 : (k + 1) * 128].astype(BF16)
            for copy in range(4):
                out_ref[copy, k * BLOCK + zh * 32 : k * BLOCK + zh * 32 + 32, :] = tile
    parts = []
    for zl in range(4):
        tiles = in_ref[zl * 2].astype(F32)
        parts += [tiles[72:73, :], tiles[73:74, :], tiles[74:75, 0:32]]
    gains = jnp.concatenate(parts, axis=1)
    rows = [gains[:, k * 128 : (k + 1) * 128] for k in range(TILES)]
    tile = jnp.concatenate(rows + [jnp.zeros((16 - TILES, 128), F32)], axis=0).astype(BF16)
    for copy in range(4):
        out_ref[copy, TILES * BLOCK : PACKED, :] = tile


def pack_tokens(gathered):
    return pl.pallas_call(
        pack_kernel,
        in_specs=[WHOLE],
        out_specs=WHOLE,
        out_shape=pltpu.VMEM((4, PACKED, 128), BF16),
        compiler_params=BIG,
        name="pack_tokens",
    )(near(gathered))


def logits_kernel(*refs):
    blocks, (embedding_ref, labels_ref, slot_ref, e_ref, stats_ref, scale_ref, normed) = refs[:4], refs[4:]
    gains = [
        [blocks[ry * 2][y1 * 2, TILES * BLOCK : PACKED, :].astype(F32) for y1 in range(2)] for ry in range(2)
    ]
    for x in range(4):
        tokens = slice(x * BLOCK, (x + 1) * BLOCK)

        def tile(ry, y1, k):
            return blocks[ry * 2 + x // 2][y1 * 2 + x % 2, k * BLOCK : (k + 1) * BLOCK, :].astype(F32)

        places = [(ry, y1, k) for ry in range(2) for y1 in range(2) for k in range(TILES)]
        squares = jnp.zeros((BLOCK, 128), F32)
        for place in places:
            v = tile(*place)
            squares += v * v
        scale = lax.rsqrt(jnp.sum(squares, axis=1, keepdims=True) / D + EPS)
        scale_ref[tokens, :] = jnp.broadcast_to(scale, (BLOCK, 128))
        for ry, y1, k in places:
            column = ry * HALF + y1 * WIDE + k * 128
            normed[tokens, column : column + 128] = (
                tile(ry, y1, k) * scale * gains[ry][y1][k : k + 1, :]
            ).astype(BF16)
    raw = lax.dot_general(
        embedding_ref[...], normed[...], (((1,), (1,)), ((), ())), preferred_element_type=F32
    )
    ratio = jnp.tanh(raw / CAP)
    row = lax.broadcasted_iota(jnp.int32, raw.shape, 0)
    inside = row < ROWS
    is_label = jnp.logical_and(inside, row + first_row() == labels_ref[...])
    exps = jnp.where(inside, jnp.exp(CAP * ratio), 0.0)
    others = jnp.where(is_label, 0.0, exps * (1.0 - ratio * ratio))
    stats_ref[0:1, :] = jnp.sum(exps, axis=0, keepdims=True)
    stats_ref[1:2, :] = jnp.sum(others * raw, axis=0, keepdims=True)
    stats_ref[2:3, :] = jnp.sum(jnp.where(is_label, raw, 0.0), axis=0, keepdims=True)
    stats_ref[3:8, :] = jnp.zeros((5, raw.shape[1]), F32)
    e_ref[0:256, :] = others.T.astype(BF16)
    e_ref[256:288, :] = slot_ref[...]


def logits_of(blocks, embedding, labels, slots):
    return pl.pallas_call(
        logits_kernel,
        in_specs=[WHOLE] * 7,
        out_specs=[WHOLE] * 3,
        out_shape=[
            pltpu.VMEM((288, PADDED), BF16),
            pltpu.VMEM((8, 256), F32),
            pltpu.VMEM((256, 128), F32),
        ],
        scratch_shapes=[pltpu.VMEM((256, D), BF16)],
        compiler_params=BIG,
        cost_estimate=pl.CostEstimate(flops=2 * 256 * PADDED * D, bytes_accessed=2 * PADDED * D, transcendentals=2 * 256 * PADDED),
        name="logits",
    )(*(near(a) for a in (*blocks, embedding, labels, slots)))


def three_pieces(value):
    high = value.astype(BF16).astype(F32)
    middle = (value - high).astype(BF16).astype(F32)
    low = (value - high - middle).astype(BF16).astype(F32)
    return [high, middle, low]


def stats_row(values):
    pieces = []
    for value in values:
        for piece in three_pieces(value):
            pieces += [piece, jnp.zeros((1, 128 - BLOCK), F32)]
    return jnp.concatenate(pieces, axis=1)


def read_stats(row):
    return [
        sum(row[:, (3 * i + j) * 128 : (3 * i + j) * 128 + BLOCK] for j in (2, 1, 0))
        for i in range(3)
    ]


def gradient_kernel(ry, e_ref, embedding_ref, stats_ref, out_ref):
    last = lax.broadcasted_iota(jnp.int32, (8, WIDE), 0) == 7
    rows = []
    for x in range(4):
        values = [stats_ref[i : i + 1, x * BLOCK : (x + 1) * BLOCK] for i in range(3)]
        rows.append(jnp.broadcast_to(stats_row(values), (8, WIDE)))
    for y1 in range(2):
        column = ry * HALF + y1 * WIDE
        term = jnp.dot(e_ref[...], embedding_ref[:, column : column + WIDE], preferred_element_type=F32)
        for x in range(4):
            at = (x // 2 * 2 + y1) * 2 + x % 2
            out_ref[at, 0:BLOCK, :] = term[x * BLOCK : (x + 1) * BLOCK, :].astype(BF16)
            extra = term[256 + 8 * x : 256 + 8 * x + 8, :]
            out_ref[at, BLOCK:ROOM, :] = jnp.where(last, rows[x], extra).astype(BF16)


def gradient_of(ry, e, embedding, stats):
    return pl.pallas_call(
        functools.partial(gradient_kernel, ry),
        in_specs=[WHOLE] * 3,
        out_specs=WHOLE,
        out_shape=pltpu.VMEM((8, ROOM, WIDE), BF16),
        compiler_params=BIG,
        cost_estimate=pl.CostEstimate(flops=288 * PADDED * D, bytes_accessed=PADDED * D, transcendentals=0),
        name="gradient",
    )(e, near(embedding), stats)


def product_kernel(ry, e_ref, embedding_ref, out_ref):
    out_ref[...] = jnp.dot(
        e_ref[...], embedding_ref[:, ry * HALF : (ry + 1) * HALF], preferred_element_type=F32
    )


def product_of(ry, e, embedding):
    return pl.pallas_call(
        functools.partial(product_kernel, ry),
        in_specs=[WHOLE] * 2,
        out_specs=WHOLE,
        out_shape=pltpu.VMEM((288, HALF), F32),
        compiler_params=BIG,
        cost_estimate=pl.CostEstimate(flops=288 * PADDED * D, bytes_accessed=PADDED * D, transcendentals=0),
        name="product",
    )(e, near(embedding))


def combine_kernel(term_ref, stats_ref, other_ref, *out_refs):
    last = lax.broadcasted_iota(jnp.int32, (8, WIDE), 0) == 7
    for x in range(4):
        values = [stats_ref[i : i + 1, x * BLOCK : (x + 1) * BLOCK] for i in range(3)]
        others = read_stats(other_ref[x // 2 * 4 + x % 2, BLOCK:ROOM, :].astype(F32)[7:8, :])
        row = jnp.broadcast_to(stats_row([a + b for a, b in zip(values, others)]), (8, WIDE))
        for y1 in range(2):
            at = (x // 2 * 2 + y1) * 2 + x % 2
            out_ref = out_refs[x // 2]
            columns = slice(y1 * WIDE, (y1 + 1) * WIDE)
            main = term_ref[x * BLOCK : (x + 1) * BLOCK, columns] + other_ref[at, 0:BLOCK, :].astype(F32)
            out_ref[y1 * 2 + x % 2, 0:BLOCK, :] = main.astype(BF16)
            extra = term_ref[256 + 8 * x : 256 + 8 * x + 8, columns] + other_ref[at, BLOCK:ROOM, :].astype(F32)
            out_ref[y1 * 2 + x % 2, BLOCK:ROOM, :] = jnp.where(last, row, extra).astype(BF16)


def combine(term, stats, other):
    return pl.pallas_call(
        combine_kernel,
        in_specs=[WHOLE] * 3,
        out_specs=[WHOLE] * 2,
        out_shape=[pltpu.VMEM((4, ROOM, WIDE), BF16)] * 2,
        compiler_params=BIG,
        name="combine",
    )(term, stats, near(other))


def class_kernel(*refs):
    in_refs, out_ref = refs[:4], refs[4]
    last = lax.broadcasted_iota(jnp.int32, (8, WIDE), 0) == 7
    for block in range(4):
        total = in_refs[0][block, 0:BLOCK, :].astype(F32)
        for ref in in_refs[1:]:
            total += ref[block, 0:BLOCK, :].astype(F32)
        out_ref[block, 0:BLOCK, :] = total.astype(BF16)
        extras = [ref[block, BLOCK:ROOM, :].astype(F32) for ref in in_refs]
        row = sum(extra[7:8, :] for extra in extras)
        row = jnp.broadcast_to(stats_row(read_stats(row)), (8, WIDE))
        extras = [jnp.where(last, row if i == 0 else 0.0, extra) for i, extra in enumerate(extras)]
        out_ref[block, BLOCK : BLOCK + 32, :] = jnp.concatenate(extras, axis=0).astype(BF16)


def class_sum(blocks):
    return pl.pallas_call(
        class_kernel,
        in_specs=[WHOLE] * 4,
        out_specs=WHOLE,
        out_shape=pltpu.VMEM((4, BLOCK + 32, WIDE), BF16),
        compiler_params=BIG,
        name="class_sum",
    )(*(near(a) for a in blocks))


def plane_kernel(in_ref, place_ref, more_ref, out_ref):
    total = in_ref[0, 0:BLOCK, :].astype(F32)
    for source in range(1, 4):
        total += in_ref[source, 0:BLOCK, :].astype(F32)
    extras = [in_ref[source, BLOCK : BLOCK + 32, :].astype(F32) for source in range(4)]
    stacked = jnp.concatenate(extras, axis=0).astype(BF16)
    label_rows = jnp.dot(place_ref[...], stacked, preferred_element_type=F32) + more_ref[...].astype(F32)
    row = sum(extra[7:8, :] for extra in extras)
    pieces = []
    for value in read_stats(row):
        pieces += three_pieces(value)
    sums = jnp.concatenate(pieces + [jnp.zeros((32 - 9, BLOCK), F32)], axis=0)
    for zl in range(4):
        for zh in range(2):
            main = total[zh * 32 : zh * 32 + 32, zl * PIECE : (zl + 1) * PIECE]
            rows = label_rows[zh * 32 : zh * 32 + 32, zl * PIECE : (zl + 1) * PIECE]
            out_ref[zl * 2 + zh] = jnp.concatenate([main, rows, sums], axis=1).astype(BF16)


def plane_sum(received, place, more):
    return pl.pallas_call(
        plane_kernel,
        in_specs=[WHOLE] * 3,
        out_specs=WHOLE,
        out_shape=pltpu.VMEM((8, 32, 640), BF16),
        compiler_params=BIG,
        name="plane_sum",
    )(near(received), near(place), near(more))


def final_kernel(in_ref, values_ref, gain_ref, weight_ref, scale_ref, loss_ref, grad_ref):
    zh, x1, x0, core = (lax.axis_index(name) for name in ("z_hi", "x1", "x0", "core"))
    total = in_ref[0].astype(F32)
    for source in range(1, 8):
        total += in_ref[source].astype(F32)
    sums = total[0:16, 2 * PIECE : 640]
    pick = lax.broadcasted_iota(jnp.int32, (32, BLOCK), 1) == zh * 32 + lax.broadcasted_iota(
        jnp.int32, (32, BLOCK), 0
    )

    def column(i):
        value = sum(sums[3 * i + j : 3 * i + j + 1, :] for j in (2, 1, 0))
        return jnp.sum(jnp.where(pick, jnp.broadcast_to(value, (32, BLOCK)), 0.0), axis=1, keepdims=True)

    sum_exp, inner_others, raw = column(0), column(1), column(2)
    own = (((zh * 2 + x1) * 2 + x0) * 2 + core) * 32 + lax.broadcasted_iota(jnp.int32, (32, 512), 0)
    own_weight = jnp.where(lax.broadcasted_iota(jnp.int32, (32, 512), 1) == own, weight_ref[...], 0.0)
    weight = jnp.sum(own_weight, axis=1, keepdims=True)
    scaling = scale_ref[pl.ds(pl.multiple_of(x1 * BLOCK + zh * 32, 32), 32), 0:1]
    ratio = jnp.tanh(raw / CAP)
    capped = CAP * ratio
    log_total = jnp.log(sum_exp)
    loss = log_total - capped
    coefficient = (jnp.exp(capped - log_total) - 1.0) * weight * (1.0 - ratio * ratio)
    coefficient = coefficient.astype(BF16).astype(F32)
    share = weight / sum_exp
    grad_normed = total[:, 0:PIECE] * share + total[:, PIECE : 2 * PIECE] * coefficient
    inner = (inner_others * share + coefficient * raw) / scaling
    upstream = grad_normed * gain_ref[...].astype(F32)
    values = values_ref[...].astype(F32)
    grad_ref[...] = scaling * upstream - values * (scaling * scaling * scaling * inner / D)
    eye = lax.broadcasted_iota(jnp.int32, (32, 32), 0) == lax.broadcasted_iota(jnp.int32, (32, 32), 1)
    loss_ref[...] = jnp.sum(jnp.where(eye, jnp.broadcast_to(loss, (32, 32)), 0.0), axis=0, keepdims=True)


def finish(received, values, gain, weight, scale):
    return pl.pallas_call(
        final_kernel,
        in_specs=[WHOLE] * 5,
        out_specs=[WHOLE] * 2,
        out_shape=[jax.ShapeDtypeStruct((1, 32), F32), jax.ShapeDtypeStruct((32, PIECE), F32)],
        compiler_params=BIG,
        name="finish",
    )(*(near(a) for a in (received, values, gain, weight, scale)))


def swap_cores(array):
    return lax.ppermute(array, "core", [(0, 1), (1, 0)])


def shifted(array, parity):
    dx, dy = SHIFTS[parity]
    pairs = []
    for chip in range(128):
        line, y, zh, x = chip // 32, chip // 8 % 4, chip // 4 % 2, chip % 4
        pairs.append((chip, ((line * 4 + (y + dy) % 4) * 2 + zh) * 4 + (x + dx) % 4))
    return lax.ppermute(array, CHIPS, pairs)


def later_rows(labels, embedding, rounds):
    def one_round(carry):
        number, rows = carry
        _, tokens = lax.optimization_barrier((number, labels))
        zl, y1, y0, zh, x1, x0, core = (lax.axis_index(name) for name in (*CHIPS, "core"))
        token = jnp.arange(512, dtype=jnp.int32)
        group = (token // 32) % 2 * 4 + (token // 64) % 2 * 2 + (token // 128) % 2
        owner = tokens // (2 * ROWS)
        key = owner * 8 + group
        same = jnp.logical_and(key[:, None] == key[None, :], token[None, :] < token[:, None])
        rank = jnp.sum(same.astype(jnp.int32), axis=1)
        turn, slot = rank // SLOTS, rank % SLOTS
        taken = jnp.where(jnp.logical_and(owner == this_chip(), turn == number), group * 8 + slot, -1)
        match = taken[None, :] == jnp.arange(64, dtype=jnp.int32)[:, None]
        held = jnp.sum(jnp.where(match, (tokens - first_row())[None, :] + 1, 0), axis=1) - 1
        chosen = (held[:, None] == jnp.arange(ROWS, dtype=jnp.int32)[None, :]).astype(BF16)
        found = jnp.dot(chosen, embedding, preferred_element_type=F32).astype(BF16)
        found = found.reshape(2, 2, 2, 8, 4, 4, PIECE).transpose(0, 5, 2, 1, 3, 4, 6).reshape(2, 16, 8, WIDE)
        ours = lax.dynamic_index_in_dim(found, core, 0, keepdims=False)
        theirs = lax.dynamic_index_in_dim(found, 1 - core, 0, keepdims=False)
        ours = ours + swap_cores(theirs)
        ours = lax.all_to_all(ours, ("y1", "y0", "x1", "x0"), 0, 0, tiled=True).reshape(128, WIDE)
        local = jnp.arange(BLOCK, dtype=jnp.int32)
        own = (((local // 32 * 2 + x1) * 2 + x0) * 2 + core) * 32 + local % 32
        place = jnp.arange(16, dtype=jnp.int32)
        chips = ((zl * 4 + place // 4) * 2 + zh) * 4 + place % 4
        hit = jnp.logical_and(owner[own][:, None] == chips[None, :], (turn[own] == number)[:, None])
        at = slot[own][:, None] == jnp.arange(8, dtype=jnp.int32)[None, :]
        put = jnp.logical_and(hit[:, :, None], at[:, None, :]).astype(BF16).reshape(BLOCK, 128)
        return number + 1, rows + jnp.dot(put, ours, preferred_element_type=F32).astype(BF16)

    start = (jnp.int32(1), jnp.zeros((BLOCK, WIDE), BF16))
    return lax.while_loop(lambda carry: carry[0] < rounds, one_round, start)[1]


def on_device(residual, final_gain, embedding, labels, token_weight):
    gain = final_gain.reshape(1, PIECE)
    gathered = lax.all_to_all(spread(residual, gain), ("z_lo", "z_hi"), 0, 0, tiled=True)
    own_labels, own_slots, other_labels, other_slots, place, rounds = label_places(labels.reshape(1, 512))
    more = later_rows(labels, embedding, rounds[0, 0])
    early = (own_labels, own_slots, other_labels, other_slots, place, more)
    copies, embedding, early = lax.optimization_barrier((pack_tokens(gathered), embedding, early))
    own_labels, own_slots, other_labels, other_slots, place, more = early

    packed = lax.all_to_all(copies, ("y1", "x1"), 0, 0, tiled=True)
    table = permute_embedding(embedding)
    blocks = [packed] + [shifted(packed, parity) for parity in SHIFTS]
    blocks[1:], table = lax.optimization_barrier((blocks[1:], table))
    other_blocks = [swap_cores(block) for block in blocks]

    e, stats, scale = logits_of(blocks, table, own_labels, own_slots)
    other_blocks, e = lax.optimization_barrier((other_blocks, e))
    e_other, stats_other, _ = logits_of(other_blocks, table, other_labels, other_slots)
    far_part, e_other = lax.optimization_barrier((gradient_of(1, e_other, table, stats_other), e_other))
    near_part, e = lax.optimization_barrier((gradient_of(0, e_other, table, stats_other), e))
    far_blocks = combine(product_of(1, e, table), stats, swap_cores(far_part))
    far_blocks, e = lax.optimization_barrier((far_blocks, e))
    near_blocks = combine(product_of(0, e, table), stats, swap_cores(near_part))
    parts = [*near_blocks, *far_blocks]
    mine = class_sum([parts[0]] + [shifted(part, parity) for part, parity in zip(parts[1:], SHIFTS)])
    plane = lax.all_to_all(mine, ("y1", "x1"), 0, 0, tiled=True)
    column = lax.all_to_all(plane_sum(plane, place, more), ("z_lo", "z_hi"), 0, 0, tiled=True)

    loss, grad = finish(column, residual, gain, token_weight.reshape(1, 512), scale)
    return (loss.reshape(32), grad)


def solution(mesh):
    fine = Mesh(mesh.devices.reshape(4, 2, 2, 2, 2, 2, 2), (*CHIPS, "core"))
    section, fsdp = ("z_lo", "y1", "y0"), ("z_hi", "x1", "x0", "core")
    in_specs = (P(fsdp, section), P(section), P(section + fsdp, None), P(), P())
    out_specs = (P(fsdp), P(fsdp, section))
    return jax.shard_map(on_device, mesh=fine, in_specs=in_specs, out_specs=out_specs, check_vma=False)
```

time: 159 us -> 127 us (0.80)
  waiting for transfers between devices: 89.7 us -> 24.6 us
  blocking collectives: 0 us -> 50.9 us
  local copies, waits for them, and re-layouts: 12.7 us -> 1.45 us
  starting transfers between devices: 23.4 us -> 19.6 us
  other arithmetic: 3.43 us -> 0 us
    all_to_all x4 -> x1, waiting for transfers between devices: 88.3 us -> 6.47 us  [on_device(): lax.all_to_all(spread(residual, gain), ('z_lo', 'z_hi'), 0, 0, tiled=True)]
    all_to_all x0 -> x3, blocking collectives: none -> 50.9 us  [the longest x1 19.2 us: on_device(): plane = lax.all_to_all(mine, ('y1', 'x1'), 0, 0, tiled=True)]
    ppermute x0 -> x6, waiting for transfers between devices: none -> 18.1 us  [shifted(): return lax.ppermute(array, CHIPS, pairs)]
    all_to_all x4 -> x1, starting transfers between devices: 22.8 us -> 8.57 us  [on_device(): lax.all_to_all(spread(residual, gain), ('z_lo', 'z_hi'), 0, 0, tiled=True)]
    ppermute x0 -> x6, starting transfers between devices: none -> 9.7 us  [shifted(): return lax.ppermute(array, CHIPS, pairs)]
    unnamed x16 -> x6, local copies, waits for them, and re-layouts: 8.86 us -> 0.75 us
    pallas_call x6 -> x12, Pallas kernels: 15.5 us -> 18.2 us  [the longest x2 6.9 us: logits_of(): pl.pallas_call(logits_kernel, in_specs=[WHOLE] * 7, out_specs=[WHOLE] * 3...]
  transfers between devices with their start and end apart: 6 -> 13, of which waited for: 5 -> 7; matrix products, arithmetic and copies ran while one was open for 2% -> 0% of each run, Pallas kernels for 10% -> 15%
where the time goes in v3:
time: 127 us; the launch traced here: 125 us
  blocking collectives  50.9 us (40%)
  Pallas kernels  27.4 us (22%)
  waiting for transfers between devices  24.6 us (19%)
  starting transfers between devices  19.6 us (15%)
  local copies, waits for them, and re-layouts  1.45 us (1%)
    all_to_all x1, blocking collectives, on_device(): plane = lax.all_to_all(mine, ('y1', 'x1'), 0, 0, tiled=True)  19.2 us
    all_to_all x1, blocking collectives, on_device(): packed = lax.all_to_all(copies, ('y1', 'x1'), 0, 0, tiled=True)  18.6 us
    ppermute x6, waiting for transfers between devices, shifted(): return lax.ppermute(array, CHIPS, pairs)  18.1 us
    all_to_all x1, blocking collectives, on_device(): lax.all_to_all(plane_sum(plane, place, more), ('z_lo', 'z_hi'), 0, 0, til...  13.1 us
    ppermute x6, starting transfers between devices, shifted(): return lax.ppermute(array, CHIPS, pairs)  9.7 us
    pallas_call x1, Pallas kernels, permute_embedding(): pl.pallas_call(permute_kernel, grid=(PADDED // step,), in_specs=[pl.Block...  8.71 us
    all_to_all x1, starting transfers between devices, on_device(): lax.all_to_all(spread(residual, gain), ('z_lo', 'z_hi'), 0, 0, tiled=True)  8.57 us
    pallas_call x2, Pallas kernels, logits_of(): pl.pallas_call(logits_kernel, in_specs=[WHOLE] * 7, out_specs=[WHOLE] * 3...  6.9 us
  transfers between devices with their start and end apart: 13, of which 7 were waited for; matrix products, arithmetic and copies ran while one was open for 0% of the time, Pallas kernels for 15%

profile of v3, /device:TPU:32, one launch (start us, length us, event | category | flops | bytes accessed | tf_op | source)
XLA Modules:
  0.0 125.4 jit_solution(17259484011700369717)
XLA Ops:
  1.3 0.7 copy-done
  2.1 0.7 spread.1
  2.8 8.6 %all-to-all-start.1 = ((bf16[8,80,128]{2,1,0:T(8,128)(2,1)}), bf16[8,80,128]{2,1,0:T(8,128)(2,1)S(1)}, u32[]{:S(2)}, u32[]{:S(2)}) async-start(bf16[8,80,128]{2,1,0:T(8,128)(2,1)} %spread.1), calls=%async_computation.1 | async-start | bytes 327680 | tf_op jit(solution)/shard_map/all_to_all | solution.py:514
  11.3 1.6 %label_places.1 = (s32[1,256]{1,0:T(1,128)S(1)}, bf16[32,1024]{1,0:T(8,128)(2,1)S(1)}, s32[1,256]{1,0:T(1,128)S(1)}, bf16[32,1024]{1,0:T(8,128)(2,1)S(1)}, bf16[...) custom-call(s32[1,512]{1,0:T(1,128)} %bitcast.35), custom_call_target="tpu_custom_call" | custom-call | flops 2621440 | bytes 1048576 | tf_op jit(solution)/shard_map/label_places/pallas_call | solution.py:106
  13.0 6.5 %all-to-all-done.1.in_ref = bf16[8,80,128]{2,1,0:T(8,128)(2,1)S(1)} async-done(((bf16[8,80,128]{2,1,0:T(8,128)(2,1)}), bf16[8,80,128]{2,1,0:T(8,128)(2,1)S(1)}, u32[]{:S(2)}, u32[]{:S(2)}) %all-to-all-start.1) | async-done | bytes 163872 | tf_op jit(solution)/shard_map/all_to_all | solution.py:514
  20.3 18.6 %all_to_all.30.refs_0_ = bf16[4,592,128]{2,1,0:T(8,128)(2,1)S(1)} all-to-all(bf16[4,592,128]{2,1,0:T(8,128)(2,1)S(1)} %pack_tokens.1), channel_id=1, replica_groups=mesh['z_lo'=4,'y1'=2,'y0'=2,'z_hi'=2,'x1'=2,'x0'=2,'core'=2] {'y1','x1'}, dimensions={0} | all-to-all | bytes 1212416 | tf_op jit(solution)/shard_map/all_to_all | solution.py:521
  39.3 1.6 %collective-permute-start.3 = (bf16[4,592,128]{2,1,0:T(8,128)(2,1)S(1)}, bf16[4,592,128]{2,1,0:T(8,128)(2,1)S(1)}, u32[]{:S(2)}, u32[]{:S(2)}) collective-permute-start(bf16[4,592,128]{2,1,0:T(8,128)(2,1)S(1)} %all_to_all.30.refs_0_), channel_id=1, source_target_pairs={{0,16},{2,18},{4,20},{6,22},{8,24},{10,26},{12,28},{14,30},{16,32}... | collective-permute-start | bytes 1818632 | tf_op jit(solution)/shard_map/ppermute | solution.py:474
  40.9 1.5 %collective-permute-start.2 = (bf16[4,592,128]{2,1,0:T(8,128)(2,1)S(1)}, bf16[4,592,128]{2,1,0:T(8,128)(2,1)S(1)}, u32[]{:S(2)}, u32[]{:S(2)}) collective-permute-start(bf16[4,592,128]{2,1,0:T(8,128)(2,1)S(1)} %all_to_all.30.refs_0_), channel_id=1, source_target_pairs={{0,2},{2,4},{4,6},{6,0},{8,10},{10,12},{12,14},{14,8},{16,18},{18,... | collective-permute-start | bytes 1818632 | tf_op jit(solution)/shard_map/ppermute | solution.py:474
  42.4 8.7 %permute_embedding.1.refs_4_.embedding_ref = bf16[1024,4608]{1,0:T(8,128)(2,1)S(1)} custom-call(bf16[1000,4608]{1,0:T(8,128)(2,1)} %get-tuple-element.348), custom_call_target="tpu_custom_call" | custom-call | bytes 18432000 | tf_op jit(solution)/shard_map/permute_embedding/pallas_call | solution.py:142
  51.3 1.9 %collective-permute-done.4.refs_3_ = bf16[4,592,128]{2,1,0:T(8,128)(2,1)S(1)} collective-permute-done((bf16[4,592,128]{2,1,0:T(8,128)(2,1)S(1)}, bf16[4,592,128]{2,1,0:T(8,128)(2,1)S(1)}, u32[]{:S(2)}, u32[]{:S(2)}) %collective-permute-start.4) | collective-permute-done | bytes 606240 | tf_op jit(solution)/shard_map/ppermute | solution.py:474
  53.2 0.7 collective-permute-done.3.refs_2_
  53.9 1.2 collective-permute-done.2.refs_1_
  55.7 3.3 %logits.2 = (bf16[288,1024]{1,0:T(8,128)(2,1)S(1)}, f32[8,256]{1,0:T(8,128)S(1)}, f32[256,128]{1,0:T(8,128)S(1)}) custom-call(bf16[4,592,128]{2,1,0:T(8,128)(2,1)S(1)} %all_to_all.30.refs_0_, bf16[4,592,128]{2,1,0:T(8,128)(2,1)S(1)} %collective-permute-done.2.refs_1_, bf16[4,592,128]{2,1,0:T(8,128)(2,1)S(1)} %collective-permute-done.3.refs_2_, ...), custom_call_target="tpu_custom_call" | custom-call | flops 2415919104 | bytes 9437184 | tf_op jit(solution)/shard_map/logits/pallas_call | solution.py:251
  59.0 3.6 %logits.3 = (bf16[288,1024]{1,0:T(8,128)(2,1)S(1)}, f32[8,256]{1,0:T(8,128)S(1)}, f32[256,128]{1,0:T(8,128)}) custom-call(bf16[4,592,128]{2,1,0:T(8,128)(2,1)S(1)} %collective-permute-done.1.refs_0_, bf16[4,592,128]{2,1,0:T(8,128)(2,1)S(1)} %collective-permute-done.5.refs_1_, bf16[4,592,128]{2,1,0:T(8,128)(2,1)S(1)} %collective-permute-done.6.refs_2_, ...), custom_call_target="tpu_custom_call" | custom-call | flops 2415919104 | bytes 9437184 | tf_op jit(solution)/shard_map/logits/pallas_call | solution.py:251
  62.6 1.7 %gradient.2 = bf16[8,72,1152]{2,1,0:T(8,128)(2,1)S(1)} custom-call(bf16[288,1024]{1,0:T(8,128)(2,1)S(1)} %get-tuple-element.192.e_ref, bf16[1024,4608]{1,0:T(8,128)(2,1)S(1)} %permute_embedding.1.refs_4_.embedding_ref, f32[8,256]{1,0:T(8,128)S(1)} %get-tuple-element.191.stats_ref), custom_call_target="tpu_custom_call" | custom-call | flops 1358954496 | bytes 4718592 | tf_op jit(solution)/shard_map/gradient/pallas_call | solution.py:306
  64.9 1.7 %gradient.3 = bf16[8,72,1152]{2,1,0:T(8,128)(2,1)S(1)} custom-call(bf16[288,1024]{1,0:T(8,128)(2,1)S(1)} %get-tuple-element.192.e_ref, bf16[1024,4608]{1,0:T(8,128)(2,1)S(1)} %permute_embedding.1.refs_4_.embedding_ref, f32[8,256]{1,0:T(8,128)S(1)} %get-tuple-element.191.stats_ref), custom_call_target="tpu_custom_call" | custom-call | flops 1358954496 | bytes 4718592 | tf_op jit(solution)/shard_map/gradient/pallas_call | solution.py:306
  66.8 1.6 %product.2.term_ref = f32[288,2304]{1,0:T(8,128)S(1)} custom-call(bf16[288,1024]{1,0:T(8,128)(2,1)S(1)} %get-tuple-element.199.e_ref, bf16[1024,4608]{1,0:T(8,128)(2,1)S(1)} %permute_embedding.1.refs_4_.embedding_ref), custom_call_target="tpu_custom_call" | custom-call | flops 1358954496 | bytes 4718592 | tf_op jit(solution)/shard_map/product/pallas_call | solution.py:324
  68.9 1.6 %product.3.term_ref = f32[288,2304]{1,0:T(8,128)S(1)} custom-call(bf16[288,1024]{1,0:T(8,128)(2,1)S(1)} %get-tuple-element.199.e_ref, bf16[1024,4608]{1,0:T(8,128)(2,1)S(1)} %permute_embedding.1.refs_4_.embedding_ref), custom_call_target="tpu_custom_call" | custom-call | flops 1358954496 | bytes 4718592 | tf_op jit(solution)/shard_map/product/pallas_call | solution.py:324
  72.1 5.1 %collective-permute-start.12 = (bf16[4,72,1152]{2,1,0:T(8,128)(2,1)S(1)}, bf16[4,72,1152]{2,1,0:T(8,128)(2,1)S(1)}, u32[]{:S(2)}, u32[]{:S(2)}) collective-permute-start(bf16[4,72,1152]{2,1,0:T(8,128)(2,1)S(1)} %get-tuple-element.204), channel_id=1, source_target_pairs={{0,54},{2,48},{4,50},{6,52},{8,62},{10,56},{12,58},{14,60},{16,6},... | collective-permute-start | bytes 1990664 | tf_op jit(solution)/shard_map/ppermute | solution.py:474
  77.2 12.6 %collective-permute-done.10.refs_1_ = bf16[4,72,1152]{2,1,0:T(8,128)(2,1)S(1)} collective-permute-done((bf16[4,72,1152]{2,1,0:T(8,128)(2,1)S(1)}, bf16[4,72,1152]{2,1,0:T(8,128)(2,1)S(1)}, u32[]{:S(2)}, u32[]{:S(2)}) %collective-permute-start.10) | collective-permute-done | bytes 663584 | tf_op jit(solution)/shard_map/ppermute | solution.py:474
  89.9 1.6 %collective-permute-done.12.refs_3_ = bf16[4,72,1152]{2,1,0:T(8,128)(2,1)S(1)} collective-permute-done((bf16[4,72,1152]{2,1,0:T(8,128)(2,1)S(1)}, bf16[4,72,1152]{2,1,0:T(8,128)(2,1)S(1)}, u32[]{:S(2)}, u32[]{:S(2)}) %collective-permute-start.12) | collective-permute-done | bytes 663584 | tf_op jit(solution)/shard_map/ppermute | solution.py:474
  91.9 19.2 %all_to_all.31.in_ref = bf16[4,96,1152]{2,1,0:T(8,128)(2,1)S(1)} all-to-all(bf16[4,96,1152]{2,1,0:T(8,128)(2,1)S(1)} %class_sum.1), channel_id=1, replica_groups=mesh['z_lo'=4,'y1'=2,'y0'=2,'z_hi'=2,'x1'=2,'x0'=2,'core'=2] {'y1','x1'}, dimensions={0} | all-to-all | bytes 1769472 | tf_op jit(solution)/shard_map/all_to_all | solution.py:537
  111.4 13.1 %all_to_all.32.in_ref = bf16[8,32,640]{2,1,0:T(8,128)(2,1)S(1)} all-to-all(bf16[8,32,640]{2,1,0:T(8,128)(2,1)S(1)} %plane_sum.1), channel_id=1, replica_groups=mesh['z_lo'=4,'y1'=2,'y0'=2,'z_hi'=2,'x1'=2,'x0'=2,'core'=2] {'z_lo','z_..., dimensions={0} | all-to-all | bytes 655360 | tf_op jit(solution)/shard_map/all_to_all | solution.py:538
  124.5 0.9 finish.1
  (29 shorter events, 6.1 us)
Async XLA Ops:
  1.3 0.7 copy-start
  2.8 16.7 %all-to-all-start.1 = ((bf16[8,80,128]{2,1,0:T(8,128)(2,1)}), bf16[8,80,128]{2,1,0:T(8,128)(2,1)S(1)}, u32[]{:S(2)}, u32[]{:S(2)}) async-start(bf16[8,80,128]{2,1,0:T(8,128)(2,1)} %spread.1), calls=%async_computation.1 | async-start | bytes 327680 | tf_op jit(solution)/shard_map/all_to_all | solution.py:514
  39.0 14.2 %collective-permute-start.4 = (bf16[4,592,128]{2,1,0:T(8,128)(2,1)S(1)}, bf16[4,592,128]{2,1,0:T(8,128)(2,1)S(1)}, u32[]{:S(2)}, u32[]{:S(2)}) collective-permute-start(bf16[4,592,128]{2,1,0:T(8,128)(2,1)S(1)} %all_to_all.30.refs_0_), channel_id=1, source_target_pairs={{0,54},{2,48},{4,50},{6,52},{8,62},{10,56},{12,58},{14,60},{16,6},... | collective-permute-start | bytes 1818632 | tf_op jit(solution)/shard_map/ppermute | solution.py:474
  39.3 14.6 %collective-permute-start.3 = (bf16[4,592,128]{2,1,0:T(8,128)(2,1)S(1)}, bf16[4,592,128]{2,1,0:T(8,128)(2,1)S(1)}, u32[]{:S(2)}, u32[]{:S(2)}) collective-permute-start(bf16[4,592,128]{2,1,0:T(8,128)(2,1)S(1)} %all_to_all.30.refs_0_), channel_id=1, source_target_pairs={{0,16},{2,18},{4,20},{6,22},{8,24},{10,26},{12,28},{14,30},{16,32}... | collective-permute-start | bytes 1818632 | tf_op jit(solution)/shard_map/ppermute | solution.py:474
  40.9 14.2 %collective-permute-start.2 = (bf16[4,592,128]{2,1,0:T(8,128)(2,1)S(1)}, bf16[4,592,128]{2,1,0:T(8,128)(2,1)S(1)}, u32[]{:S(2)}, u32[]{:S(2)}) collective-permute-start(bf16[4,592,128]{2,1,0:T(8,128)(2,1)S(1)} %all_to_all.30.refs_0_), channel_id=1, source_target_pairs={{0,2},{2,4},{4,6},{6,0},{8,10},{10,12},{12,14},{14,8},{16,18},{18,... | collective-permute-start | bytes 1818632 | tf_op jit(solution)/shard_map/ppermute | solution.py:474
  51.2 7.8 %collective-permute-start.1 = (bf16[4,592,128]{2,1,0:T(8,128)(2,1)S(1)}, bf16[4,592,128]{2,1,0:T(8,128)(2,1)S(1)}, u32[]{:S(2)}, u32[]{:S(2)}) collective-permute-start(bf16[4,592,128]{2,1,0:T(8,128)(2,1)S(1)} %all_to_all.30.refs_0_), channel_id=1, source_target_pairs={{0,1},{1,0},{2,3},{3,2},{4,5},{5,4},{6,7},{7,6},{8,9},{9,8},{10,11... | collective-permute-start | bytes 1818632 | tf_op jit(solution)/shard_map/ppermute | solution.py:465
  55.1 3.8 %collective-permute-start.5 = (bf16[4,592,128]{2,1,0:T(8,128)(2,1)S(1)}, bf16[4,592,128]{2,1,0:T(8,128)(2,1)S(1)}, u32[]{:S(2)}, u32[]{:S(2)}) collective-permute-start(bf16[4,592,128]{2,1,0:T(8,128)(2,1)S(1)} %collective-permute-done.2.refs_1_), channel_id=1, source_target_pairs={{0,1},{1,0},{2,3},{3,2},{4,5},{5,4},{6,7},{7,6},{8,9},{9,8},{10,11... | collective-permute-start | bytes 1818632 | tf_op jit(solution)/shard_map/ppermute | solution.py:465
  55.1 3.9 %collective-permute-start.6 = (bf16[4,592,128]{2,1,0:T(8,128)(2,1)S(1)}, bf16[4,592,128]{2,1,0:T(8,128)(2,1)S(1)}, u32[]{:S(2)}, u32[]{:S(2)}) collective-permute-start(bf16[4,592,128]{2,1,0:T(8,128)(2,1)S(1)} %collective-permute-done.3.refs_2_), channel_id=1, source_target_pairs={{0,1},{1,0},{2,3},{3,2},{4,5},{5,4},{6,7},{7,6},{8,9},{9,8},{10,11... | collective-permute-start | bytes 1818632 | tf_op jit(solution)/shard_map/ppermute | solution.py:465
  55.6 3.4 %collective-permute-start.7 = (bf16[4,592,128]{2,1,0:T(8,128)(2,1)S(1)}, bf16[4,592,128]{2,1,0:T(8,128)(2,1)S(1)}, u32[]{:S(2)}, u32[]{:S(2)}) collective-permute-start(bf16[4,592,128]{2,1,0:T(8,128)(2,1)S(1)} %collective-permute-done.4.refs_3_), channel_id=1, source_target_pairs={{0,1},{1,0},{2,3},{3,2},{4,5},{5,4},{6,7},{7,6},{8,9},{9,8},{10,11... | collective-permute-start | bytes 1818632 | tf_op jit(solution)/shard_map/ppermute | solution.py:465
  64.3 4.0 %collective-permute-start.8 = (bf16[8,72,1152]{2,1,0:T(8,128)(2,1)S(1)}, bf16[8,72,1152]{2,1,0:T(8,128)(2,1)S(1)}, u32[]{:S(2)}, u32[]{:S(2)}) collective-permute-start(bf16[8,72,1152]{2,1,0:T(8,128)(2,1)S(1)} %gradient.2), channel_id=1, source_target_pairs={{0,1},{1,0},{2,3},{3,2},{4,5},{5,4},{6,7},{7,6},{8,9},{9,8},{10,11... | collective-permute-start | bytes 3981320 | tf_op jit(solution)/shard_map/ppermute | solution.py:465
  66.7 3.8 %collective-permute-start.9 = (bf16[8,72,1152]{2,1,0:T(8,128)(2,1)S(1)}, bf16[8,72,1152]{2,1,0:T(8,128)(2,1)S(1)}, u32[]{:S(2)}, u32[]{:S(2)}) collective-permute-start(bf16[8,72,1152]{2,1,0:T(8,128)(2,1)S(1)} %gradient.3), channel_id=1, source_target_pairs={{0,1},{1,0},{2,3},{3,2},{4,5},{5,4},{6,7},{7,6},{8,9},{9,8},{10,11... | collective-permute-start | bytes 3981320 | tf_op jit(solution)/shard_map/ppermute | solution.py:465
  71.0 18.8 %collective-permute-start.10 = (bf16[4,72,1152]{2,1,0:T(8,128)(2,1)S(1)}, bf16[4,72,1152]{2,1,0:T(8,128)(2,1)S(1)}, u32[]{:S(2)}, u32[]{:S(2)}) collective-permute-start(bf16[4,72,1152]{2,1,0:T(8,128)(2,1)S(1)} %get-tuple-element.202), channel_id=1, source_target_pairs={{0,2},{2,4},{4,6},{6,0},{8,10},{10,12},{12,14},{14,8},{16,18},{18,... | collective-permute-start | bytes 1990664 | tf_op jit(solution)/shard_map/ppermute | solution.py:474
  71.7 18.2 %collective-permute-start.11 = (bf16[4,72,1152]{2,1,0:T(8,128)(2,1)S(1)}, bf16[4,72,1152]{2,1,0:T(8,128)(2,1)S(1)}, u32[]{:S(2)}, u32[]{:S(2)}) collective-permute-start(bf16[4,72,1152]{2,1,0:T(8,128)(2,1)S(1)} %get-tuple-element.203), channel_id=1, source_target_pairs={{0,16},{2,18},{4,20},{6,22},{8,24},{10,26},{12,28},{14,30},{16,32}... | collective-permute-start | bytes 1990664 | tf_op jit(solution)/shard_map/ppermute | solution.py:474
  72.1 19.4 %collective-permute-start.12 = (bf16[4,72,1152]{2,1,0:T(8,128)(2,1)S(1)}, bf16[4,72,1152]{2,1,0:T(8,128)(2,1)S(1)}, u32[]{:S(2)}, u32[]{:S(2)}) collective-permute-start(bf16[4,72,1152]{2,1,0:T(8,128)(2,1)S(1)} %get-tuple-element.204), channel_id=1, source_target_pairs={{0,54},{2,48},{4,50},{6,52},{8,62},{10,56},{12,58},{14,60},{16,6},... | collective-permute-start | bytes 1990664 | tf_op jit(solution)/shard_map/ppermute | solution.py:474
  91.9 32.6 %copy-start.1 = (bf16[32,288]{1,0:T(8,128)(2,1)S(1)}, bf16[32,288]{1,0:T(8,128)(2,1)}, u32[]{:S(2)}) copy-start(bf16[32,288]{1,0:T(8,128)(2,1)} %values_ref.1) | copy-start | bytes 55300
  91.9 32.6 %copy-start.2 = (f32[512]{0:T(512)S(1)}, f32[512]{0:T(512)}, u32[]{:S(2)}) copy-start(f32[512]{0:T(512)} %param.11) | copy-start | bytes 6148

commit v4 on v3

--- a/solution.py
+++ b/solution.py
@@ -34,6 +34,7 @@
 
 CHIPS = ("z_lo", "y1", "y0", "z_hi", "x1", "x0")
 SHIFTS = {(0, 1): (1, 0), (1, 0): (0, 1), (1, 1): (-1, -1)}
+PLACES = ((0, 0), *SHIFTS)
 
 
 def this_chip():
@@ -93,8 +94,8 @@
     own_code = jnp.sum(jnp.where(pick, code, 0), axis=1, keepdims=True)
     column = lax.broadcasted_iota(jnp.int32, (BLOCK, 128), 1)
     parity = column >> 3 & 3
-    from_y = (column >> 6) * 2 + y0 + 4
-    from_x = (column >> 5 & 1) * 2 + x0 + 4
+    from_y = (column >> 6 ^ y1) * 2 + y0 + 4
+    from_x = (column >> 5 & 1 ^ x1) * 2 + x0 + 4
     for index, (dx, dy) in enumerate(SHIFTS.values()):
         from_y = from_y - jnp.where(parity == index + 1, dy, 0)
         from_x = from_x - jnp.where(parity == index + 1, dx, 0)
@@ -121,20 +122,29 @@
     )(labels)
 
 
+def far(array):
+    return pltpu.with_memory_space_constraint(array, pltpu.MemorySpace.HBM)
+
+
 def permute_kernel(in_ref, out_ref):
     step = in_ref.shape[0]
-    first = pl.multiple_of(pl.program_id(0) * step, step)
-    rows = first + lax.broadcasted_iota(jnp.int32, (step, 1), 0)
-    block = jnp.where(rows < ROWS, in_ref[...].astype(F32), 0.0)
+    number = pl.program_id(0)
+    first = pl.multiple_of(number * step, step)
+    tail = PADDED - ROWS
     for y0 in range(2):
 
         @pl.when(lax.axis_index("y0") == y0)
         def _():
             for at in range(4):
                 y = at % 2 * 2 + (at // 2 + y0) % 2
-                parts = [block[:, (z * 4 + y) * PIECE : (z * 4 + y + 1) * PIECE] for z in range(4)]
-                wide = jnp.concatenate(parts, axis=1).astype(BF16)
-                out_ref[pl.ds(first, step), at * WIDE : (at + 1) * WIDE] = wide
+                parts = [in_ref[:, (z * 4 + y) * PIECE : (z * 4 + y + 1) * PIECE] for z in range(4)]
+                out_ref[pl.ds(first, step), at * WIDE : (at + 1) * WIDE] = jnp.concatenate(parts, axis=1)
+
+    @pl.when(number == PADDED // step - 1)
+    def _():
+        rows = lax.broadcasted_iota(jnp.int32, (32, 1), 0)
+        kept = out_ref[PADDED - 32 : PADDED, :].astype(F32)
+        out_ref[PADDED - 32 : PADDED, :] = jnp.where(rows < 32 - tail, kept, 0.0).astype(BF16)
 
 
 def permute_embedding(embedding):
@@ -151,26 +161,39 @@
     )(embedding)
 
 
-def spread_kernel(residual_ref, gain_ref, out_ref):
+def spread_kernel(residual_hbm, gain_hbm, out_ref, residual_ref, gain_ref, arrived):
+    copies = [
+        pltpu.make_async_copy(residual_hbm, residual_ref, arrived.at[0]),
+        pltpu.make_async_copy(gain_hbm, gain_ref, arrived.at[1]),
+    ]
+    for copy in copies:
+        copy.start()
+    for copy in copies:
+        copy.wait()
     values = residual_ref[...].astype(F32)
-    gain = gain_ref[...].astype(F32)
+    gain = gain_ref[...].astype(F32).reshape(1, PIECE)
     corner = jnp.concatenate([values[8 * g : 8 * g + 8, 256:PIECE] for g in range(4)], axis=1)
     last = jnp.concatenate([gain[:, 256:PIECE], jnp.zeros((1, 96), F32)], axis=1)
     rows = [values[:, 0:128], values[:, 128:256], corner, gain[:, 0:128], gain[:, 128:256], last, jnp.zeros((5, 128), F32)]
     tiles = jnp.concatenate(rows, axis=0).astype(BF16)
-    for copy in range(8):
-        out_ref[copy] = tiles
+    for place in range(8):
+        out_ref[place] = tiles
 
 
 def spread(residual, gain):
     return pl.pallas_call(
         spread_kernel,
-        in_specs=[WHOLE] * 2,
+        in_specs=[pl.BlockSpec(memory_space=pl.ANY)] * 2,
         out_specs=WHOLE,
         out_shape=pltpu.VMEM((8, 80, 128), BF16),
+        scratch_shapes=[
+            pltpu.VMEM((32, PIECE), BF16),
+            pltpu.VMEM((PIECE,), BF16),
+            pltpu.SemaphoreType.DMA((2,)),
+        ],
         compiler_params=BIG,
         name="spread",
-    )(residual, gain)
+    )(far(residual), far(gain))
 
 
 def pack_kernel(in_ref, out_ref):
@@ -183,8 +206,7 @@
         wide = jnp.concatenate(parts, axis=1)
         for k in range(TILES):
             tile = wide[:, k * 128 : (k + 1) * 128].astype(BF16)
-            for copy in range(4):
-                out_ref[copy, k * BLOCK + zh * 32 : k * BLOCK + zh * 32 + 32, :] = tile
+            out_ref[k * BLOCK + zh * 32 : k * BLOCK + zh * 32 + 32, :] = tile
     parts = []
     for zl in range(4):
         tiles = in_ref[zl * 2].astype(F32)
@@ -192,8 +214,7 @@
     gains = jnp.concatenate(parts, axis=1)
     rows = [gains[:, k * 128 : (k + 1) * 128] for k in range(TILES)]
     tile = jnp.concatenate(rows + [jnp.zeros((16 - TILES, 128), F32)], axis=0).astype(BF16)
-    for copy in range(4):
-        out_ref[copy, TILES * BLOCK : PACKED, :] = tile
+    out_ref[TILES * BLOCK : PACKED, :] = tile
 
 
 def pack_tokens(gathered):
@@ -201,10 +222,31 @@
         pack_kernel,
         in_specs=[WHOLE],
         out_specs=WHOLE,
-        out_shape=pltpu.VMEM((4, PACKED, 128), BF16),
+        out_shape=pltpu.VMEM((PACKED, 128), BF16),
         compiler_params=BIG,
         name="pack_tokens",
     )(near(gathered))
+
+
+def absolute(relative):
+    return (lax.axis_index("y1") + relative // 2) % 2 * 2 + (lax.axis_index("x1") + relative % 2) % 2
+
+
+def order_kernel(*refs):
+    in_refs, out_ref = refs[:4], refs[4]
+    for relative, ref in enumerate(in_refs):
+        out_ref[absolute(relative)] = ref[...]
+
+
+def in_order(pieces):
+    return pl.pallas_call(
+        order_kernel,
+        in_specs=[WHOLE] * 4,
+        out_specs=WHOLE,
+        out_shape=pltpu.VMEM((4, PACKED, 128), BF16),
+        compiler_params=BIG,
+        name="in_order",
+    )(*(near(a) for a in pieces))
 
 
 def logits_kernel(*refs):
@@ -360,36 +402,38 @@
 
 
 def class_kernel(*refs):
-    in_refs, out_ref = refs[:4], refs[4]
+    in_refs, out_refs = refs[:4], refs[4:]
     last = lax.broadcasted_iota(jnp.int32, (8, WIDE), 0) == 7
-    for block in range(4):
+    for relative, out_ref in enumerate(out_refs):
+        block = absolute(relative)
         total = in_refs[0][block, 0:BLOCK, :].astype(F32)
         for ref in in_refs[1:]:
             total += ref[block, 0:BLOCK, :].astype(F32)
-        out_ref[block, 0:BLOCK, :] = total.astype(BF16)
+        out_ref[0:BLOCK, :] = total.astype(BF16)
         extras = [ref[block, BLOCK:ROOM, :].astype(F32) for ref in in_refs]
         row = sum(extra[7:8, :] for extra in extras)
         row = jnp.broadcast_to(stats_row(read_stats(row)), (8, WIDE))
         extras = [jnp.where(last, row if i == 0 else 0.0, extra) for i, extra in enumerate(extras)]
-        out_ref[block, BLOCK : BLOCK + 32, :] = jnp.concatenate(extras, axis=0).astype(BF16)
+        out_ref[BLOCK : BLOCK + 32, :] = jnp.concatenate(extras, axis=0).astype(BF16)
 
 
 def class_sum(blocks):
     return pl.pallas_call(
         class_kernel,
         in_specs=[WHOLE] * 4,
-        out_specs=WHOLE,
-        out_shape=pltpu.VMEM((4, BLOCK + 32, WIDE), BF16),
+        out_specs=[WHOLE] * 4,
+        out_shape=[pltpu.VMEM((BLOCK + 32, WIDE), BF16)] * 4,
         compiler_params=BIG,
         name="class_sum",
     )(*(near(a) for a in blocks))
 
 
-def plane_kernel(in_ref, place_ref, more_ref, out_ref):
-    total = in_ref[0, 0:BLOCK, :].astype(F32)
-    for source in range(1, 4):
-        total += in_ref[source, 0:BLOCK, :].astype(F32)
-    extras = [in_ref[source, BLOCK : BLOCK + 32, :].astype(F32) for source in range(4)]
+def plane_kernel(*refs):
+    in_refs, (place_ref, more_ref, out_ref) = refs[:4], refs[4:]
+    total = in_refs[0][0:BLOCK, :].astype(F32)
+    for ref in in_refs[1:]:
+        total += ref[0:BLOCK, :].astype(F32)
+    extras = [ref[BLOCK : BLOCK + 32, :].astype(F32) for ref in in_refs]
     stacked = jnp.concatenate(extras, axis=0).astype(BF16)
     label_rows = jnp.dot(place_ref[...], stacked, preferred_element_type=F32) + more_ref[...].astype(F32)
     row = sum(extra[7:8, :] for extra in extras)
@@ -407,12 +451,12 @@
 def plane_sum(received, place, more):
     return pl.pallas_call(
         plane_kernel,
-        in_specs=[WHOLE] * 3,
+        in_specs=[WHOLE] * 6,
         out_specs=WHOLE,
         out_shape=pltpu.VMEM((8, 32, 640), BF16),
         compiler_params=BIG,
         name="plane_sum",
-    )(near(received), near(place), near(more))
+    )(*(near(a) for a in (*received, place, more)))
 
 
 def final_kernel(in_ref, values_ref, gain_ref, weight_ref, scale_ref, loss_ref, grad_ref):
@@ -465,8 +509,7 @@
     return lax.ppermute(array, "core", [(0, 1), (1, 0)])
 
 
-def shifted(array, parity):
-    dx, dy = SHIFTS[parity]
+def shifted(array, dx, dy):
     pairs = []
     for chip in range(128):
         line, y, zh, x = chip // 32, chip // 8 % 4, chip // 4 % 2, chip % 4
@@ -511,16 +554,15 @@
 
 def on_device(residual, final_gain, embedding, labels, token_weight):
     gain = final_gain.reshape(1, PIECE)
-    gathered = lax.all_to_all(spread(residual, gain), ("z_lo", "z_hi"), 0, 0, tiled=True)
-    own_labels, own_slots, other_labels, other_slots, place, rounds = label_places(labels.reshape(1, 512))
-    more = later_rows(labels, embedding, rounds[0, 0])
-    early = (own_labels, own_slots, other_labels, other_slots, place, more)
-    copies, embedding, early = lax.optimization_barrier((pack_tokens(gathered), embedding, early))
+    gathered = lax.all_to_all(spread(residual, final_gain), ("z_lo", "z_hi"), 0, 0, tiled=True)
+    *early, rounds = label_places(labels.reshape(1, 512))
+    early.append(later_rows(labels, embedding, rounds[0, 0]))
+    piece, embedding, early = lax.optimization_barrier((pack_tokens(gathered), embedding, early))
     own_labels, own_slots, other_labels, other_slots, place, more = early
 
-    packed = lax.all_to_all(copies, ("y1", "x1"), 0, 0, tiled=True)
+    packed = in_order([piece] + [shifted(piece, 2 * dx, 2 * dy) for dy, dx in PLACES[1:]])
     table = permute_embedding(embedding)
-    blocks = [packed] + [shifted(packed, parity) for parity in SHIFTS]
+    blocks = [packed] + [shifted(packed, *SHIFTS[parity]) for parity in PLACES[1:]]
     blocks[1:], table = lax.optimization_barrier((blocks[1:], table))
     other_blocks = [swap_cores(block) for block in blocks]
 
@@ -533,8 +575,8 @@
     far_blocks, e = lax.optimization_barrier((far_blocks, e))
     near_blocks = combine(product_of(0, e, table), stats, swap_cores(near_part))
     parts = [*near_blocks, *far_blocks]
-    mine = class_sum([parts[0]] + [shifted(part, parity) for part, parity in zip(parts[1:], SHIFTS)])
-    plane = lax.all_to_all(mine, ("y1", "x1"), 0, 0, tiled=True)
+    sums = class_sum([parts[0]] + [shifted(part, *SHIFTS[parity]) for part, parity in zip(parts[1:], PLACES[1:])])
+    plane = [sums[0]] + [shifted(block, 2 * dx, 2 * dy) for block, (dy, dx) in zip(sums[1:], PLACES[1:])]
     column = lax.all_to_all(plane_sum(plane, place, more), ("z_lo", "z_hi"), 0, 0, tiled=True)
 
     loss, grad = finish(column, residual, gain, token_weight.reshape(1, 512), scale)

time: 127 us -> 121 us (0.953)
  blocking collectives: 50.9 us -> 0 us
  waiting for transfers between devices: 24.6 us -> 53.6 us
  starting transfers between devices: 19.6 us -> 37.3 us
  local copies, waits for them, and re-layouts: 1.45 us -> 0.04 us
    all_to_all x3 -> x0, blocking collectives: 50.9 us -> none  [the longest x1 19.2 us: on_device(): plane = lax.all_to_all(mine, ('y1', 'x1'), 0, 0, tiled=True)]
    ppermute x6 -> x12, waiting for transfers between devices: 18.1 us -> 36.7 us  [shifted(): return lax.ppermute(array, CHIPS, pairs)]
    ppermute x6 -> x12, starting transfers between devices: 9.7 us -> 23.7 us  [shifted(): return lax.ppermute(array, CHIPS, pairs)]
    all_to_all x1 -> x2, waiting for transfers between devices: 6.47 us -> 16.8 us  [the longest x1 10.4 us: on_device(): lax.all_to_all(plane_sum(plane, place, more), ('z_lo', 'z_hi'), 0, 0, til...]
    all_to_all x1 -> x2, starting transfers between devices: 8.57 us -> 12 us  [the longest x1 8.58 us: on_device(): lax.all_to_all(spread(residual, final_gain), ('z_lo', 'z_hi'), 0, 0, tile...]
    pallas_call x3 -> x4, Pallas kernels: 1.38 us -> 2.94 us  [the longest x1 1.5 us: spread(): pl.pallas_call(spread_kernel, in_specs=[pl.BlockSpec(memory_space=pl.ANY)...]
    pallas_call x1, Pallas kernels: 8.71 us -> 7.28 us  [permute_embedding(): pl.pallas_call(permute_kernel, grid=(PADDED // step,), in_specs=[pl.Block...]
  transfers between devices with their start and end apart: 13 -> 20, of which waited for: 7 -> 13; matrix products, arithmetic and copies ran while one was open for 0% -> 0% of each run, Pallas kernels for 15% -> 15%
where the time goes in v4:
time: 121 us; the launch traced here: 120 us
  waiting for transfers between devices  53.6 us (44%)
  starting transfers between devices  37.3 us (31%)
  Pallas kernels  27.6 us (23%)
    ppermute x12, waiting for transfers between devices, shifted(): return lax.ppermute(array, CHIPS, pairs)  36.7 us
    ppermute x12, starting transfers between devices, shifted(): return lax.ppermute(array, CHIPS, pairs)  23.7 us
    all_to_all x1, waiting for transfers between devices, on_device(): lax.all_to_all(plane_sum(plane, place, more), ('z_lo', 'z_hi'), 0, 0, til...  10.4 us
    all_to_all x1, starting transfers between devices, on_device(): lax.all_to_all(spread(residual, final_gain), ('z_lo', 'z_hi'), 0, 0, tile...  8.58 us
    pallas_call x1, Pallas kernels, permute_embedding(): pl.pallas_call(permute_kernel, grid=(PADDED // step,), in_specs=[pl.Block...  7.28 us
    pallas_call x2, Pallas kernels, logits_of(): pl.pallas_call(logits_kernel, in_specs=[WHOLE] * 7, out_specs=[WHOLE] * 3...  6.92 us
    all_to_all x1, waiting for transfers between devices, on_device(): lax.all_to_all(spread(residual, final_gain), ('z_lo', 'z_hi'), 0, 0, tile...  6.47 us
    pallas_call x2, Pallas kernels, gradient_of(): pl.pallas_call(functools.partial(gradient_kernel, ry), in_specs=[WHOLE] *...  3.46 us
  transfers between devices with their start and end apart: 20, of which 13 were waited for; matrix products, arithmetic and copies ran while one was open for 0% of the time, Pallas kernels for 15%

profile of v4, /device:TPU:32, one launch (start us, length us, event | category | flops | bytes accessed | tf_op | source)
XLA Modules:
  0.0 119.9 jit_solution(1720655148196963306)
XLA Ops:
  2.1 8.6 %all-to-all-start.1 = ((bf16[8,80,128]{2,1,0:T(8,128)(2,1)}), bf16[8,80,128]{2,1,0:T(8,128)(2,1)S(1)}, u32[]{:S(2)}, u32[]{:S(2)}) async-start(bf16[8,80,128]{2,1,0:T(8,128)(2,1)} %spread.1), calls=%async_computation.1 | async-start | bytes 327680 | tf_op jit(solution)/shard_map/all_to_all | solution.py:557
  10.7 1.6 %label_places.1 = (s32[1,256]{1,0:T(1,128)S(1)}, bf16[32,1024]{1,0:T(8,128)(2,1)S(1)}, s32[1,256]{1,0:T(1,128)S(1)}, bf16[32,1024]{1,0:T(8,128)(2,1)S(1)}, bf16[...) custom-call(s32[1,512]{1,0:T(1,128)} %bitcast.35), custom_call_target="tpu_custom_call" | custom-call | flops 2621440 | bytes 1048576 | tf_op jit(solution)/shard_map/label_places/pallas_call | solution.py:107
  12.3 6.5 %all-to-all-done.1.in_ref = bf16[8,80,128]{2,1,0:T(8,128)(2,1)S(1)} async-done(((bf16[8,80,128]{2,1,0:T(8,128)(2,1)}), bf16[8,80,128]{2,1,0:T(8,128)(2,1)S(1)}, u32[]{:S(2)}, u32[]{:S(2)}) %all-to-all-start.1) | async-done | bytes 163872 | tf_op jit(solution)/shard_map/all_to_all | solution.py:557
  19.7 5.7 %collective-permute-start.3 = (bf16[592,128]{1,0:T(8,128)(2,1)S(1)}, bf16[592,128]{1,0:T(8,128)(2,1)S(1)}, u32[]{:S(2)}, u32[]{:S(2)}) collective-permute-start(bf16[592,128]{1,0:T(8,128)(2,1)S(1)} %pack_tokens.1.refs_0_), channel_id=1, source_target_pairs={{0,36},{2,38},{4,32},{6,34},{8,44},{10,46},{12,40},{14,42},{16,52}... | collective-permute-start | bytes 454664 | tf_op jit(solution)/shard_map/ppermute | solution.py:517
  26.3 3.3 %collective-permute-done.3.refs_3_ = bf16[592,128]{1,0:T(8,128)(2,1)S(1)} collective-permute-done((bf16[592,128]{1,0:T(8,128)(2,1)S(1)}, bf16[592,128]{1,0:T(8,128)(2,1)S(1)}, u32[]{:S(2)}, u32[]{:S(2)}) %collective-permute-start.3) | collective-permute-done | bytes 151584 | tf_op jit(solution)/shard_map/ppermute | solution.py:517
  29.6 2.5 %collective-permute-done.2.refs_2_ = bf16[592,128]{1,0:T(8,128)(2,1)S(1)} collective-permute-done((bf16[592,128]{1,0:T(8,128)(2,1)S(1)}, bf16[592,128]{1,0:T(8,128)(2,1)S(1)}, u32[]{:S(2)}, u32[]{:S(2)}) %collective-permute-start.2) | collective-permute-done | bytes 151584 | tf_op jit(solution)/shard_map/ppermute | solution.py:517
  32.6 4.2 %collective-permute-start.7 = (bf16[4,592,128]{2,1,0:T(8,128)(2,1)S(1)}, bf16[4,592,128]{2,1,0:T(8,128)(2,1)S(1)}, u32[]{:S(2)}, u32[]{:S(2)}) collective-permute-start(bf16[4,592,128]{2,1,0:T(8,128)(2,1)S(1)} %in_order.1.refs_0_), channel_id=1, source_target_pairs={{0,54},{2,48},{4,50},{6,52},{8,62},{10,56},{12,58},{14,60},{16,6},... | collective-permute-start | bytes 1818632 | tf_op jit(solution)/shard_map/ppermute | solution.py:517
  37.1 7.3 %permute_embedding.1.refs_4_.embedding_ref = bf16[1024,4608]{1,0:T(8,128)(2,1)S(1)} custom-call(bf16[1000,4608]{1,0:T(8,128)(2,1)} %get-tuple-element.369), custom_call_target="tpu_custom_call" | custom-call | bytes 18432000 | tf_op jit(solution)/shard_map/permute_embedding/pallas_call | solution.py:152
  44.5 4.7 %collective-permute-done.7.refs_3_ = bf16[4,592,128]{2,1,0:T(8,128)(2,1)S(1)} collective-permute-done((bf16[4,592,128]{2,1,0:T(8,128)(2,1)S(1)}, bf16[4,592,128]{2,1,0:T(8,128)(2,1)S(1)}, u32[]{:S(2)}, u32[]{:S(2)}) %collective-permute-start.7) | collective-permute-done | bytes 606240 | tf_op jit(solution)/shard_map/ppermute | solution.py:517
  49.2 3.4 %collective-permute-done.6.refs_2_ = bf16[4,592,128]{2,1,0:T(8,128)(2,1)S(1)} collective-permute-done((bf16[4,592,128]{2,1,0:T(8,128)(2,1)S(1)}, bf16[4,592,128]{2,1,0:T(8,128)(2,1)S(1)}, u32[]{:S(2)}, u32[]{:S(2)}) %collective-permute-start.6) | collective-permute-done | bytes 606240 | tf_op jit(solution)/shard_map/ppermute | solution.py:517
  53.1 3.3 %logits.2 = (bf16[288,1024]{1,0:T(8,128)(2,1)S(1)}, f32[8,256]{1,0:T(8,128)S(1)}, f32[256,128]{1,0:T(8,128)S(1)}) custom-call(bf16[4,592,128]{2,1,0:T(8,128)(2,1)S(1)} %in_order.1.refs_0_, bf16[4,592,128]{2,1,0:T(8,128)(2,1)S(1)} %collective-permute-done.5.refs_1_, bf16[4,592,128]{2,1,0:T(8,128)(2,1)S(1)} %collective-permute-done.6.refs_2_, ...), custom_call_target="tpu_custom_call" | custom-call | flops 2415919104 | bytes 9437184 | tf_op jit(solution)/shard_map/logits/pallas_call | solution.py:293
  56.5 3.6 %logits.3 = (bf16[288,1024]{1,0:T(8,128)(2,1)S(1)}, f32[8,256]{1,0:T(8,128)S(1)}, f32[256,128]{1,0:T(8,128)}) custom-call(bf16[4,592,128]{2,1,0:T(8,128)(2,1)S(1)} %collective-permute-done.4.refs_0_, bf16[4,592,128]{2,1,0:T(8,128)(2,1)S(1)} %collective-permute-done.8.refs_1_, bf16[4,592,128]{2,1,0:T(8,128)(2,1)S(1)} %collective-permute-done.9.refs_2_, ...), custom_call_target="tpu_custom_call" | custom-call | flops 2415919104 | bytes 9437184 | tf_op jit(solution)/shard_map/logits/pallas_call | solution.py:293
  60.1 1.7 %gradient.2 = bf16[8,72,1152]{2,1,0:T(8,128)(2,1)S(1)} custom-call(bf16[288,1024]{1,0:T(8,128)(2,1)S(1)} %get-tuple-element.196.e_ref, bf16[1024,4608]{1,0:T(8,128)(2,1)S(1)} %permute_embedding.1.refs_4_.embedding_ref, f32[8,256]{1,0:T(8,128)S(1)} %get-tuple-element.195.stats_ref), custom_call_target="tpu_custom_call" | custom-call | flops 1358954496 | bytes 4718592 | tf_op jit(solution)/shard_map/gradient/pallas_call | solution.py:348
  62.4 1.7 %gradient.3 = bf16[8,72,1152]{2,1,0:T(8,128)(2,1)S(1)} custom-call(bf16[288,1024]{1,0:T(8,128)(2,1)S(1)} %get-tuple-element.196.e_ref, bf16[1024,4608]{1,0:T(8,128)(2,1)S(1)} %permute_embedding.1.refs_4_.embedding_ref, f32[8,256]{1,0:T(8,128)S(1)} %get-tuple-element.195.stats_ref), custom_call_target="tpu_custom_call" | custom-call | flops 1358954496 | bytes 4718592 | tf_op jit(solution)/shard_map/gradient/pallas_call | solution.py:348
  66.6 1.6 %product.3.term_ref = f32[288,2304]{1,0:T(8,128)S(1)} custom-call(bf16[288,1024]{1,0:T(8,128)(2,1)S(1)} %get-tuple-element.203.e_ref, bf16[1024,4608]{1,0:T(8,128)(2,1)S(1)} %permute_embedding.1.refs_4_.embedding_ref), custom_call_target="tpu_custom_call" | custom-call | flops 1358954496 | bytes 4718592 | tf_op jit(solution)/shard_map/product/pallas_call | solution.py:366
  70.4 4.3 %collective-permute-start.15 = (bf16[4,72,1152]{2,1,0:T(8,128)(2,1)S(1)}, bf16[4,72,1152]{2,1,0:T(8,128)(2,1)S(1)}, u32[]{:S(2)}, u32[]{:S(2)}) collective-permute-start(bf16[4,72,1152]{2,1,0:T(8,128)(2,1)S(1)} %get-tuple-element.208), channel_id=1, source_target_pairs={{0,54},{2,48},{4,50},{6,52},{8,62},{10,56},{12,58},{14,60},{16,6},... | collective-permute-start | bytes 1990664 | tf_op jit(solution)/shard_map/ppermute | solution.py:517
  74.8 12.6 %collective-permute-done.13.refs_1_ = bf16[4,72,1152]{2,1,0:T(8,128)(2,1)S(1)} collective-permute-done((bf16[4,72,1152]{2,1,0:T(8,128)(2,1)S(1)}, bf16[4,72,1152]{2,1,0:T(8,128)(2,1)S(1)}, u32[]{:S(2)}, u32[]{:S(2)}) %collective-permute-start.13) | collective-permute-done | bytes 663584 | tf_op jit(solution)/shard_map/ppermute | solution.py:517
  90.3 2.9 %collective-permute-start.17 = (bf16[96,1152]{1,0:T(8,128)(2,1)S(1)}, bf16[96,1152]{1,0:T(8,128)(2,1)S(1)}, u32[]{:S(2)}, u32[]{:S(2)}) collective-permute-start(bf16[96,1152]{1,0:T(8,128)(2,1)S(1)} %get-tuple-element.211), channel_id=1, source_target_pairs={{0,32},{2,34},{4,36},{6,38},{8,40},{10,42},{12,44},{14,46},{16,48}... | collective-permute-start | bytes 663560 | tf_op jit(solution)/shard_map/ppermute | solution.py:517
  93.2 2.8 %collective-permute-start.18 = (bf16[96,1152]{1,0:T(8,128)(2,1)S(1)}, bf16[96,1152]{1,0:T(8,128)(2,1)S(1)}, u32[]{:S(2)}, u32[]{:S(2)}) collective-permute-start(bf16[96,1152]{1,0:T(8,128)(2,1)S(1)} %get-tuple-element.212), channel_id=1, source_target_pairs={{0,36},{2,38},{4,32},{6,34},{8,44},{10,46},{12,40},{14,42},{16,52}... | collective-permute-start | bytes 663560 | tf_op jit(solution)/shard_map/ppermute | solution.py:517
  96.0 2.6 %collective-permute-done.16.refs_1_ = bf16[96,1152]{1,0:T(8,128)(2,1)S(1)} collective-permute-done((bf16[96,1152]{1,0:T(8,128)(2,1)S(1)}, bf16[96,1152]{1,0:T(8,128)(2,1)S(1)}, u32[]{:S(2)}, u32[]{:S(2)}) %collective-permute-start.16) | collective-permute-done | bytes 221216 | tf_op jit(solution)/shard_map/ppermute | solution.py:517
  98.6 3.0 %collective-permute-done.17.refs_2_ = bf16[96,1152]{1,0:T(8,128)(2,1)S(1)} collective-permute-done((bf16[96,1152]{1,0:T(8,128)(2,1)S(1)}, bf16[96,1152]{1,0:T(8,128)(2,1)S(1)}, u32[]{:S(2)}, u32[]{:S(2)}) %collective-permute-start.17) | collective-permute-done | bytes 221216 | tf_op jit(solution)/shard_map/ppermute | solution.py:517
  101.6 2.5 %collective-permute-done.18.refs_3_ = bf16[96,1152]{1,0:T(8,128)(2,1)S(1)} collective-permute-done((bf16[96,1152]{1,0:T(8,128)(2,1)S(1)}, bf16[96,1152]{1,0:T(8,128)(2,1)S(1)}, u32[]{:S(2)}, u32[]{:S(2)}) %collective-permute-start.18) | collective-permute-done | bytes 221216 | tf_op jit(solution)/shard_map/ppermute | solution.py:517
  105.2 3.5 %all-to-all-start.2 = ((bf16[8,32,640]{2,1,0:T(8,128)(2,1)}), bf16[8,32,640]{2,1,0:T(8,128)(2,1)S(1)}, u32[]{:S(2)}, u32[]{:S(2)}) async-start(bf16[8,32,640]{2,1,0:T(8,128)(2,1)} %plane_sum.1), calls=%async_computation.2 | async-start | bytes 655360 | tf_op jit(solution)/shard_map/all_to_all | solution.py:580
  108.6 10.4 %all-to-all-done.2.in_ref = bf16[8,32,640]{2,1,0:T(8,128)(2,1)S(1)} async-done(((bf16[8,32,640]{2,1,0:T(8,128)(2,1)}), bf16[8,32,640]{2,1,0:T(8,128)(2,1)S(1)}, u32[]{:S(2)}, u32[]{:S(2)}) %all-to-all-start.2) | async-done | bytes 327712 | tf_op jit(solution)/shard_map/all_to_all | solution.py:580
  (41 shorter events, 14.7 us)
Async XLA Ops:
  2.1 16.7 %all-to-all-start.1 = ((bf16[8,80,128]{2,1,0:T(8,128)(2,1)}), bf16[8,80,128]{2,1,0:T(8,128)(2,1)S(1)}, u32[]{:S(2)}, u32[]{:S(2)}) async-start(bf16[8,80,128]{2,1,0:T(8,128)(2,1)} %spread.1), calls=%async_computation.1 | async-start | bytes 327680 | tf_op jit(solution)/shard_map/all_to_all | solution.py:557
  19.7 9.9 %collective-permute-start.3 = (bf16[592,128]{1,0:T(8,128)(2,1)S(1)}, bf16[592,128]{1,0:T(8,128)(2,1)S(1)}, u32[]{:S(2)}, u32[]{:S(2)}) collective-permute-start(bf16[592,128]{1,0:T(8,128)(2,1)S(1)} %pack_tokens.1.refs_0_), channel_id=1, source_target_pairs={{0,36},{2,38},{4,32},{6,34},{8,44},{10,46},{12,40},{14,42},{16,52}... | collective-permute-start | bytes 454664 | tf_op jit(solution)/shard_map/ppermute | solution.py:517
  25.5 6.7 %collective-permute-start.2 = (bf16[592,128]{1,0:T(8,128)(2,1)S(1)}, bf16[592,128]{1,0:T(8,128)(2,1)S(1)}, u32[]{:S(2)}, u32[]{:S(2)}) collective-permute-start(bf16[592,128]{1,0:T(8,128)(2,1)S(1)} %pack_tokens.1.refs_0_), channel_id=1, source_target_pairs={{0,32},{2,34},{4,36},{6,38},{8,40},{10,42},{12,44},{14,46},{16,48}... | collective-permute-start | bytes 454664 | tf_op jit(solution)/shard_map/ppermute | solution.py:517
  25.8 6.7 %collective-permute-start.1 = (bf16[592,128]{1,0:T(8,128)(2,1)S(1)}, bf16[592,128]{1,0:T(8,128)(2,1)S(1)}, u32[]{:S(2)}, u32[]{:S(2)}) collective-permute-start(bf16[592,128]{1,0:T(8,128)(2,1)S(1)} %pack_tokens.1.refs_0_), channel_id=1, source_target_pairs={{0,4},{2,6},{4,0},{6,2},{8,12},{10,14},{12,8},{14,10},{16,20},{18,... | collective-permute-start | bytes 454664 | tf_op jit(solution)/shard_map/ppermute | solution.py:517
  32.6 16.6 %collective-permute-start.7 = (bf16[4,592,128]{2,1,0:T(8,128)(2,1)S(1)}, bf16[4,592,128]{2,1,0:T(8,128)(2,1)S(1)}, u32[]{:S(2)}, u32[]{:S(2)}) collective-permute-start(bf16[4,592,128]{2,1,0:T(8,128)(2,1)S(1)} %in_order.1.refs_0_), channel_id=1, source_target_pairs={{0,54},{2,48},{4,50},{6,52},{8,62},{10,56},{12,58},{14,60},{16,6},... | collective-permute-start | bytes 1818632 | tf_op jit(solution)/shard_map/ppermute | solution.py:517
  36.7 15.9 %collective-permute-start.6 = (bf16[4,592,128]{2,1,0:T(8,128)(2,1)S(1)}, bf16[4,592,128]{2,1,0:T(8,128)(2,1)S(1)}, u32[]{:S(2)}, u32[]{:S(2)}) collective-permute-start(bf16[4,592,128]{2,1,0:T(8,128)(2,1)S(1)} %in_order.1.refs_0_), channel_id=1, source_target_pairs={{0,16},{2,18},{4,20},{6,22},{8,24},{10,26},{12,28},{14,30},{16,32}... | collective-permute-start | bytes 1818632 | tf_op jit(solution)/shard_map/ppermute | solution.py:517
  36.7 15.9 %collective-permute-start.5 = (bf16[4,592,128]{2,1,0:T(8,128)(2,1)S(1)}, bf16[4,592,128]{2,1,0:T(8,128)(2,1)S(1)}, u32[]{:S(2)}, u32[]{:S(2)}) collective-permute-start(bf16[4,592,128]{2,1,0:T(8,128)(2,1)S(1)} %in_order.1.refs_0_), channel_id=1, source_target_pairs={{0,2},{2,4},{4,6},{6,0},{8,10},{10,12},{12,14},{14,8},{16,18},{18,... | collective-permute-start | bytes 1818632 | tf_op jit(solution)/shard_map/ppermute | solution.py:517
  44.4 12.0 %collective-permute-start.4 = (bf16[4,592,128]{2,1,0:T(8,128)(2,1)S(1)}, bf16[4,592,128]{2,1,0:T(8,128)(2,1)S(1)}, u32[]{:S(2)}, u32[]{:S(2)}) collective-permute-start(bf16[4,592,128]{2,1,0:T(8,128)(2,1)S(1)} %in_order.1.refs_0_), channel_id=1, source_target_pairs={{0,1},{1,0},{2,3},{3,2},{4,5},{5,4},{6,7},{7,6},{8,9},{9,8},{10,11... | collective-permute-start | bytes 1818632 | tf_op jit(solution)/shard_map/ppermute | solution.py:509
  52.6 3.9 %collective-permute-start.8 = (bf16[4,592,128]{2,1,0:T(8,128)(2,1)S(1)}, bf16[4,592,128]{2,1,0:T(8,128)(2,1)S(1)}, u32[]{:S(2)}, u32[]{:S(2)}) collective-permute-start(bf16[4,592,128]{2,1,0:T(8,128)(2,1)S(1)} %collective-permute-done.5.refs_1_), channel_id=1, source_target_pairs={{0,1},{1,0},{2,3},{3,2},{4,5},{5,4},{6,7},{7,6},{8,9},{9,8},{10,11... | collective-permute-start | bytes 1818632 | tf_op jit(solution)/shard_map/ppermute | solution.py:509
  52.6 3.9 %collective-permute-start.9 = (bf16[4,592,128]{2,1,0:T(8,128)(2,1)S(1)}, bf16[4,592,128]{2,1,0:T(8,128)(2,1)S(1)}, u32[]{:S(2)}, u32[]{:S(2)}) collective-permute-start(bf16[4,592,128]{2,1,0:T(8,128)(2,1)S(1)} %collective-permute-done.6.refs_2_), channel_id=1, source_target_pairs={{0,1},{1,0},{2,3},{3,2},{4,5},{5,4},{6,7},{7,6},{8,9},{9,8},{10,11... | collective-permute-start | bytes 1818632 | tf_op jit(solution)/shard_map/ppermute | solution.py:509
  53.1 3.4 %collective-permute-start.10 = (bf16[4,592,128]{2,1,0:T(8,128)(2,1)S(1)}, bf16[4,592,128]{2,1,0:T(8,128)(2,1)S(1)}, u32[]{:S(2)}, u32[]{:S(2)}) collective-permute-start(bf16[4,592,128]{2,1,0:T(8,128)(2,1)S(1)} %collective-permute-done.7.refs_3_), channel_id=1, source_target_pairs={{0,1},{1,0},{2,3},{3,2},{4,5},{5,4},{6,7},{7,6},{8,9},{9,8},{10,11... | collective-permute-start | bytes 1818632 | tf_op jit(solution)/shard_map/ppermute | solution.py:509
  61.8 4.2 %collective-permute-start.11 = (bf16[8,72,1152]{2,1,0:T(8,128)(2,1)S(1)}, bf16[8,72,1152]{2,1,0:T(8,128)(2,1)S(1)}, u32[]{:S(2)}, u32[]{:S(2)}) collective-permute-start(bf16[8,72,1152]{2,1,0:T(8,128)(2,1)S(1)} %gradient.2), channel_id=1, source_target_pairs={{0,1},{1,0},{2,3},{3,2},{4,5},{5,4},{6,7},{7,6},{8,9},{9,8},{10,11... | collective-permute-start | bytes 3981320 | tf_op jit(solution)/shard_map/ppermute | solution.py:509
  64.1 4.0 %collective-permute-start.12 = (bf16[8,72,1152]{2,1,0:T(8,128)(2,1)S(1)}, bf16[8,72,1152]{2,1,0:T(8,128)(2,1)S(1)}, u32[]{:S(2)}, u32[]{:S(2)}) collective-permute-start(bf16[8,72,1152]{2,1,0:T(8,128)(2,1)S(1)} %gradient.3), channel_id=1, source_target_pairs={{0,1},{1,0},{2,3},{3,2},{4,5},{5,4},{6,7},{7,6},{8,9},{9,8},{10,11... | collective-permute-start | bytes 3981320 | tf_op jit(solution)/shard_map/ppermute | solution.py:509
  68.7 39.9 %copy-start.2 = (bf16[288]{0:T(512)(128)(2,1)S(1)}, bf16[288]{0:T(512)(128)(2,1)}, u32[]{:S(2)}) copy-start(bf16[288]{0:T(512)(128)(2,1)} %gain_hbm.1) | copy-start | bytes 1732
  68.7 50.3 %copy-start = (bf16[32,288]{1,0:T(8,128)(2,1)S(1)}, bf16[32,288]{1,0:T(8,128)(2,1)}, u32[]{:S(2)}) copy-start(bf16[32,288]{1,0:T(8,128)(2,1)} %values_ref.1) | copy-start | bytes 55300
  68.8 50.2 %copy-start.1 = (f32[512]{0:T(512)S(1)}, f32[512]{0:T(512)}, u32[]{:S(2)}) copy-start(f32[512]{0:T(512)} %param.11) | copy-start | bytes 6148
  68.8 18.6 %collective-permute-start.13 = (bf16[4,72,1152]{2,1,0:T(8,128)(2,1)S(1)}, bf16[4,72,1152]{2,1,0:T(8,128)(2,1)S(1)}, u32[]{:S(2)}, u32[]{:S(2)}) collective-permute-start(bf16[4,72,1152]{2,1,0:T(8,128)(2,1)S(1)} %get-tuple-element.206), channel_id=1, source_target_pairs={{0,2},{2,4},{4,6},{6,0},{8,10},{10,12},{12,14},{14,8},{16,18},{18,... | collective-permute-start | bytes 1990664 | tf_op jit(solution)/shard_map/ppermute | solution.py:517
  69.3 18.2 %collective-permute-start.14 = (bf16[4,72,1152]{2,1,0:T(8,128)(2,1)S(1)}, bf16[4,72,1152]{2,1,0:T(8,128)(2,1)S(1)}, u32[]{:S(2)}, u32[]{:S(2)}) collective-permute-start(bf16[4,72,1152]{2,1,0:T(8,128)(2,1)S(1)} %get-tuple-element.207), channel_id=1, source_target_pairs={{0,16},{2,18},{4,20},{6,22},{8,24},{10,26},{12,28},{14,30},{16,32}... | collective-permute-start | bytes 1990664 | tf_op jit(solution)/shard_map/ppermute | solution.py:517
  70.4 18.6 %collective-permute-start.15 = (bf16[4,72,1152]{2,1,0:T(8,128)(2,1)S(1)}, bf16[4,72,1152]{2,1,0:T(8,128)(2,1)S(1)}, u32[]{:S(2)}, u32[]{:S(2)}) collective-permute-start(bf16[4,72,1152]{2,1,0:T(8,128)(2,1)S(1)} %get-tuple-element.208), channel_id=1, source_target_pairs={{0,54},{2,48},{4,50},{6,52},{8,62},{10,56},{12,58},{14,60},{16,6},... | collective-permute-start | bytes 1990664 | tf_op jit(solution)/shard_map/ppermute | solution.py:517
  89.4 9.2 %collective-permute-start.16 = (bf16[96,1152]{1,0:T(8,128)(2,1)S(1)}, bf16[96,1152]{1,0:T(8,128)(2,1)S(1)}, u32[]{:S(2)}, u32[]{:S(2)}) collective-permute-start(bf16[96,1152]{1,0:T(8,128)(2,1)S(1)} %get-tuple-element.210), channel_id=1, source_target_pairs={{0,4},{2,6},{4,0},{6,2},{8,12},{10,14},{12,8},{14,10},{16,20},{18,... | collective-permute-start | bytes 663560 | tf_op jit(solution)/shard_map/ppermute | solution.py:517
  90.3 11.4 %collective-permute-start.17 = (bf16[96,1152]{1,0:T(8,128)(2,1)S(1)}, bf16[96,1152]{1,0:T(8,128)(2,1)S(1)}, u32[]{:S(2)}, u32[]{:S(2)}) collective-permute-start(bf16[96,1152]{1,0:T(8,128)(2,1)S(1)} %get-tuple-element.211), channel_id=1, source_target_pairs={{0,32},{2,34},{4,36},{6,38},{8,40},{10,42},{12,44},{14,46},{16,48}... | collective-permute-start | bytes 663560 | tf_op jit(solution)/shard_map/ppermute | solution.py:517
  93.2 11.0 %collective-permute-start.18 = (bf16[96,1152]{1,0:T(8,128)(2,1)S(1)}, bf16[96,1152]{1,0:T(8,128)(2,1)S(1)}, u32[]{:S(2)}, u32[]{:S(2)}) collective-permute-start(bf16[96,1152]{1,0:T(8,128)(2,1)S(1)} %get-tuple-element.212), channel_id=1, source_target_pairs={{0,36},{2,38},{4,32},{6,34},{8,44},{10,46},{12,40},{14,42},{16,52}... | collective-permute-start | bytes 663560 | tf_op jit(solution)/shard_map/ppermute | solution.py:517
  105.2 13.8 %all-to-all-start.2 = ((bf16[8,32,640]{2,1,0:T(8,128)(2,1)}), bf16[8,32,640]{2,1,0:T(8,128)(2,1)S(1)}, u32[]{:S(2)}, u32[]{:S(2)}) async-start(bf16[8,32,640]{2,1,0:T(8,128)(2,1)} %plane_sum.1), calls=%async_computation.2 | async-start | bytes 655360 | tf_op jit(solution)/shard_map/all_to_all | solution.py:580

commit v5 on v4

--- a/solution.py
+++ b/solution.py
@@ -250,7 +250,7 @@
 
 
 def logits_kernel(*refs):
-    blocks, (embedding_ref, labels_ref, slot_ref, e_ref, stats_ref, scale_ref, normed) = refs[:4], refs[4:]
+    blocks, (embedding_ref, labels_ref, slot_ref, e_near, e_far, stats_ref, scale_ref, normed) = refs[:4], refs[4:]
     gains = [
         [blocks[ry * 2][y1 * 2, TILES * BLOCK : PACKED, :].astype(F32) for y1 in range(2)] for ry in range(2)
     ]
@@ -285,17 +285,19 @@
     stats_ref[1:2, :] = jnp.sum(others * raw, axis=0, keepdims=True)
     stats_ref[2:3, :] = jnp.sum(jnp.where(is_label, raw, 0.0), axis=0, keepdims=True)
     stats_ref[3:8, :] = jnp.zeros((5, raw.shape[1]), F32)
-    e_ref[0:256, :] = others.T.astype(BF16)
-    e_ref[256:288, :] = slot_ref[...]
+    for rx, e_ref in enumerate((e_near, e_far)):
+        e_ref[0:128, :] = others[:, rx * 128 : (rx + 1) * 128].T.astype(BF16)
+        e_ref[128:144, :] = slot_ref[rx * 16 : (rx + 1) * 16, :]
 
 
 def logits_of(blocks, embedding, labels, slots):
     return pl.pallas_call(
         logits_kernel,
         in_specs=[WHOLE] * 7,
-        out_specs=[WHOLE] * 3,
+        out_specs=[WHOLE] * 4,
         out_shape=[
-            pltpu.VMEM((288, PADDED), BF16),
+            pltpu.VMEM((144, PADDED), BF16),
+            pltpu.VMEM((144, PADDED), BF16),
             pltpu.VMEM((8, 256), F32),
             pltpu.VMEM((256, 128), F32),
         ],
@@ -328,77 +330,95 @@
     ]
 
 
-def gradient_kernel(ry, e_ref, embedding_ref, stats_ref, out_ref):
+def rows_of(term, parity, x1):
+    at = parity * 144
+    return term[at + x1 * BLOCK : at + (x1 + 1) * BLOCK, :], term[at + 128 + 8 * x1 : at + 128 + 8 * x1 + 8, :]
+
+
+def gradient_kernel(ry, parities, *refs):
+    e_refs, (embedding_ref, stats_ref, *out_refs) = refs[: len(parities)], refs[len(parities) :]
     last = lax.broadcasted_iota(jnp.int32, (8, WIDE), 0) == 7
-    rows = []
-    for x in range(4):
-        values = [stats_ref[i : i + 1, x * BLOCK : (x + 1) * BLOCK] for i in range(3)]
-        rows.append(jnp.broadcast_to(stats_row(values), (8, WIDE)))
+    left = jnp.concatenate([ref[...] for ref in e_refs], axis=0)
+    rows = {}
+    for rx in parities:
+        for x1 in range(2):
+            at = (rx * 2 + x1) * BLOCK
+            values = [stats_ref[i : i + 1, at : at + BLOCK] for i in range(3)]
+            rows[rx, x1] = jnp.broadcast_to(stats_row(values), (8, WIDE))
     for y1 in range(2):
         column = ry * HALF + y1 * WIDE
-        term = jnp.dot(e_ref[...], embedding_ref[:, column : column + WIDE], preferred_element_type=F32)
-        for x in range(4):
-            at = (x // 2 * 2 + y1) * 2 + x % 2
-            out_ref[at, 0:BLOCK, :] = term[x * BLOCK : (x + 1) * BLOCK, :].astype(BF16)
-            extra = term[256 + 8 * x : 256 + 8 * x + 8, :]
-            out_ref[at, BLOCK:ROOM, :] = jnp.where(last, rows[x], extra).astype(BF16)
-
-
-def gradient_of(ry, e, embedding, stats):
-    return pl.pallas_call(
-        functools.partial(gradient_kernel, ry),
-        in_specs=[WHOLE] * 3,
+        term = jnp.dot(left, embedding_ref[:, column : column + WIDE], preferred_element_type=F32)
+        for place, rx in enumerate(parities):
+            for x1 in range(2):
+                out_ref, at = out_refs[y1 * len(out_refs) // 2], place * 4 // len(out_refs) + x1
+                at += y1 * 2 if len(out_refs) == 1 else 0
+                main, extra = rows_of(term, place, x1)
+                out_ref[at, 0:BLOCK, :] = main.astype(BF16)
+                out_ref[at, BLOCK:ROOM, :] = jnp.where(last, rows[rx, x1], extra).astype(BF16)
+
+
+def gradient_of(ry, parities, e, embedding, stats, pieces=1):
+    count = len(parities)
+    return pl.pallas_call(
+        functools.partial(gradient_kernel, ry, parities),
+        in_specs=[WHOLE] * (2 + count),
+        out_specs=[WHOLE] * pieces,
+        out_shape=[pltpu.VMEM((4 * count // pieces, ROOM, WIDE), BF16)] * pieces,
+        compiler_params=BIG,
+        cost_estimate=pl.CostEstimate(flops=144 * count * PADDED * D, bytes_accessed=PADDED * D, transcendentals=0),
+        name="gradient",
+    )(*(near(e[rx]) for rx in parities), near(embedding), near(stats))
+
+
+def product_kernel(ry, *refs):
+    e_refs, (embedding_ref, out_ref) = refs[:-2], refs[-2:]
+    left = jnp.concatenate([ref[...] for ref in e_refs], axis=0)
+    out_ref[...] = jnp.dot(left, embedding_ref[:, ry * HALF : (ry + 1) * HALF], preferred_element_type=F32)
+
+
+def product_of(ry, parities, e, embedding):
+    count = len(parities)
+    return pl.pallas_call(
+        functools.partial(product_kernel, ry),
+        in_specs=[WHOLE] * (1 + count),
         out_specs=WHOLE,
-        out_shape=pltpu.VMEM((8, ROOM, WIDE), BF16),
-        compiler_params=BIG,
-        cost_estimate=pl.CostEstimate(flops=288 * PADDED * D, bytes_accessed=PADDED * D, transcendentals=0),
-        name="gradient",
-    )(e, near(embedding), stats)
-
-
-def product_kernel(ry, e_ref, embedding_ref, out_ref):
-    out_ref[...] = jnp.dot(
-        e_ref[...], embedding_ref[:, ry * HALF : (ry + 1) * HALF], preferred_element_type=F32
-    )
-
-
-def product_of(ry, e, embedding):
-    return pl.pallas_call(
-        functools.partial(product_kernel, ry),
-        in_specs=[WHOLE] * 2,
-        out_specs=WHOLE,
-        out_shape=pltpu.VMEM((288, HALF), F32),
-        compiler_params=BIG,
-        cost_estimate=pl.CostEstimate(flops=288 * PADDED * D, bytes_accessed=PADDED * D, transcendentals=0),
+        out_shape=pltpu.VMEM((144 * count, HALF), F32),
+        compiler_params=BIG,
+        cost_estimate=pl.CostEstimate(flops=144 * count * PADDED * D, bytes_accessed=PADDED * D, transcendentals=0),
         name="product",
-    )(e, near(embedding))
-
-
-def combine_kernel(term_ref, stats_ref, other_ref, *out_refs):
+    )(*(near(e[rx]) for rx in parities), near(embedding))
+
+
+def combine_kernel(parities, term_ref, stats_ref, *refs):
+    other_refs, out_refs = refs[: -len(parities)], refs[-len(parities) :]
     last = lax.broadcasted_iota(jnp.int32, (8, WIDE), 0) == 7
-    for x in range(4):
-        values = [stats_ref[i : i + 1, x * BLOCK : (x + 1) * BLOCK] for i in range(3)]
-        others = read_stats(other_ref[x // 2 * 4 + x % 2, BLOCK:ROOM, :].astype(F32)[7:8, :])
-        row = jnp.broadcast_to(stats_row([a + b for a, b in zip(values, others)]), (8, WIDE))
-        for y1 in range(2):
-            at = (x // 2 * 2 + y1) * 2 + x % 2
-            out_ref = out_refs[x // 2]
-            columns = slice(y1 * WIDE, (y1 + 1) * WIDE)
-            main = term_ref[x * BLOCK : (x + 1) * BLOCK, columns] + other_ref[at, 0:BLOCK, :].astype(F32)
-            out_ref[y1 * 2 + x % 2, 0:BLOCK, :] = main.astype(BF16)
-            extra = term_ref[256 + 8 * x : 256 + 8 * x + 8, columns] + other_ref[at, BLOCK:ROOM, :].astype(F32)
-            out_ref[y1 * 2 + x % 2, BLOCK:ROOM, :] = jnp.where(last, row, extra).astype(BF16)
-
-
-def combine(term, stats, other):
-    return pl.pallas_call(
-        combine_kernel,
-        in_specs=[WHOLE] * 3,
-        out_specs=[WHOLE] * 2,
-        out_shape=[pltpu.VMEM((4, ROOM, WIDE), BF16)] * 2,
+    for place, rx in enumerate(parities):
+        for x1 in range(2):
+            at = (rx * 2 + x1) * BLOCK
+            values = [stats_ref[i : i + 1, at : at + BLOCK] for i in range(3)]
+            others = other_refs[0][place * 4 // len(other_refs) + x1, BLOCK:ROOM, :].astype(F32)
+            others = read_stats(others[7:8, :])
+            row = jnp.broadcast_to(stats_row([a + b for a, b in zip(values, others)]), (8, WIDE))
+            for y1 in range(2):
+                other_ref, at = other_refs[y1 * len(other_refs) // 2], place * 4 // len(other_refs) + x1
+                at += y1 * 2 if len(other_refs) == 1 else 0
+                main, extra = rows_of(term_ref[:, y1 * WIDE : (y1 + 1) * WIDE], place, x1)
+                main = main + other_ref[at, 0:BLOCK, :].astype(F32)
+                extra = extra + other_ref[at, BLOCK:ROOM, :].astype(F32)
+                out_refs[place][y1 * 2 + x1, 0:BLOCK, :] = main.astype(BF16)
+                out_refs[place][y1 * 2 + x1, BLOCK:ROOM, :] = jnp.where(last, row, extra).astype(BF16)
+
+
+def combine(parities, term, stats, other):
+    count = len(parities)
+    return pl.pallas_call(
+        functools.partial(combine_kernel, parities),
+        in_specs=[WHOLE] * (2 + len(other)),
+        out_specs=[WHOLE] * count,
+        out_shape=[pltpu.VMEM((4, ROOM, WIDE), BF16)] * count,
         compiler_params=BIG,
         name="combine",
-    )(term, stats, near(other))
+    )(near(term), near(stats), *(near(a) for a in other))
 
 
 def class_kernel(*refs):
@@ -556,25 +576,30 @@
     gain = final_gain.reshape(1, PIECE)
     gathered = lax.all_to_all(spread(residual, final_gain), ("z_lo", "z_hi"), 0, 0, tiled=True)
     *early, rounds = label_places(labels.reshape(1, 512))
-    early.append(later_rows(labels, embedding, rounds[0, 0]))
-    piece, embedding, early = lax.optimization_barrier((pack_tokens(gathered), embedding, early))
-    own_labels, own_slots, other_labels, other_slots, place, more = early
-
-    packed = in_order([piece] + [shifted(piece, 2 * dx, 2 * dy) for dy, dx in PLACES[1:]])
+    piece, embedding, rounds, early = lax.optimization_barrier((pack_tokens(gathered), embedding, rounds, early))
+    own_labels, own_slots, other_labels, other_slots, place = early
+    more = later_rows(labels, embedding, rounds[0, 0])
+
+    moved = [shifted(piece, 2 * dx, 2 * dy) for dy, dx in PLACES[1:]]
+    moved, more = lax.optimization_barrier((moved, more))
+    packed = in_order([piece] + moved)
     table = permute_embedding(embedding)
     blocks = [packed] + [shifted(packed, *SHIFTS[parity]) for parity in PLACES[1:]]
     blocks[1:], table = lax.optimization_barrier((blocks[1:], table))
     other_blocks = [swap_cores(block) for block in blocks]
 
-    e, stats, scale = logits_of(blocks, table, own_labels, own_slots)
+    *e, stats, scale = logits_of(blocks, table, own_labels, own_slots)
     other_blocks, e = lax.optimization_barrier((other_blocks, e))
-    e_other, stats_other, _ = logits_of(other_blocks, table, other_labels, other_slots)
-    far_part, e_other = lax.optimization_barrier((gradient_of(1, e_other, table, stats_other), e_other))
-    near_part, e = lax.optimization_barrier((gradient_of(0, e_other, table, stats_other), e))
-    far_blocks = combine(product_of(1, e, table), stats, swap_cores(far_part))
+    *e_other, stats_other, _ = logits_of(other_blocks, table, other_labels, other_slots)
+    far_part, e_other = lax.optimization_barrier((gradient_of(1, (0, 1), e_other, table, stats_other), e_other))
+    near_part, e = lax.optimization_barrier((gradient_of(0, (1,), e_other, table, stats_other), e))
+    far_blocks = combine((0, 1), product_of(1, (0, 1), e, table), stats, [swap_cores(part) for part in far_part])
     far_blocks, e = lax.optimization_barrier((far_blocks, e))
-    near_blocks = combine(product_of(0, e, table), stats, swap_cores(near_part))
-    parts = [*near_blocks, *far_blocks]
+    (near_block,) = combine((1,), product_of(0, (1,), e, table), stats, [swap_cores(part) for part in near_part])
+    near_block, e, e_other = lax.optimization_barrier((near_block, e, e_other))
+    stay_part, e = lax.optimization_barrier((gradient_of(0, (0,), e_other, table, stats_other, 2), e))
+    (stay_block,) = combine((0,), product_of(0, (0,), e, table), stats, [swap_cores(part) for part in stay_part])
+    parts = [stay_block, near_block, *far_blocks]
     sums = class_sum([parts[0]] + [shifted(part, *SHIFTS[parity]) for part, parity in zip(parts[1:], PLACES[1:])])
     plane = [sums[0]] + [shifted(block, 2 * dx, 2 * dy) for block, (dy, dx) in zip(sums[1:], PLACES[1:])]
     column = lax.all_to_all(plane_sum(plane, place, more), ("z_lo", "z_hi"), 0, 0, tiled=True)

time: 121 us -> 118 us (0.975)
  waiting for transfers between devices: 53.6 us -> 51.1 us
    ppermute x12, waiting for transfers between devices: 36.7 us -> 33.8 us  [shifted(): return lax.ppermute(array, CHIPS, pairs)]
    pallas_call x6 -> x8, Pallas kernels: 11.5 us -> 11.9 us  [the longest x2 7.17 us: logits_of(): pl.pallas_call(logits_kernel, in_specs=[WHOLE] * 7, out_specs=[WHOLE] * 4...]
    pallas_call x2 -> x3, Pallas kernels: 3.13 us -> 3.24 us  [product_of(): pl.pallas_call(functools.partial(product_kernel, ry), in_specs=[WHOLE] *...]
  transfers between devices with their start and end apart: 20 -> 22, of which waited for: 13 -> 16; matrix products, arithmetic and copies ran while one was open for 0% -> 0% of each run, Pallas kernels for 15% -> 16%
where the time goes in v5:
time: 118 us; the launch traced here: 117 us
  waiting for transfers between devices  51.1 us (43%)
  starting transfers between devices  36.5 us (31%)
  Pallas kernels  28.1 us (24%)
    ppermute x12, waiting for transfers between devices, shifted(): return lax.ppermute(array, CHIPS, pairs)  33.8 us
    ppermute x12, starting transfers between devices, shifted(): return lax.ppermute(array, CHIPS, pairs)  22.6 us
    all_to_all x1, waiting for transfers between devices, on_device(): lax.all_to_all(plane_sum(plane, place, more), ('z_lo', 'z_hi'), 0, 0, til...  9.96 us
    all_to_all x1, starting transfers between devices, on_device(): lax.all_to_all(spread(residual, final_gain), ('z_lo', 'z_hi'), 0, 0, tile...  8.58 us
    pallas_call x1, Pallas kernels, permute_embedding(): pl.pallas_call(permute_kernel, grid=(PADDED // step,), in_specs=[pl.Block...  7.28 us
    pallas_call x2, Pallas kernels, logits_of(): pl.pallas_call(logits_kernel, in_specs=[WHOLE] * 7, out_specs=[WHOLE] * 4...  7.17 us
    all_to_all x1, waiting for transfers between devices, on_device(): lax.all_to_all(spread(residual, final_gain), ('z_lo', 'z_hi'), 0, 0, tile...  6.47 us
    pallas_call x3, Pallas kernels, gradient_of(): pl.pallas_call(functools.partial(gradient_kernel, ry, parities), in_specs...  3.58 us
  transfers between devices with their start and end apart: 22, of which 16 were waited for; matrix products, arithmetic and copies ran while one was open for 0% of the time, Pallas kernels for 16%

profile of v5, /device:TPU:32, one launch (start us, length us, event | category | flops | bytes accessed | tf_op | source)
XLA Modules:
  0.0 117.2 jit_solution(10009367041333872194)
XLA Ops:
  0.6 1.5 %spread.1 = bf16[8,80,128]{2,1,0:T(8,128)(2,1)} custom-call(bf16[32,288]{1,0:T(8,128)(2,1)} %values_ref.1, bf16[288]{0:T(512)(128)(2,1)} %gain_hbm.1), custom_call_target="tpu_custom_call" | custom-call | tf_op jit(solution)/shard_map/spread/pallas_call | solution.py:184
  2.1 8.6 %all-to-all-start.1 = ((bf16[8,80,128]{2,1,0:T(8,128)(2,1)}), bf16[8,80,128]{2,1,0:T(8,128)(2,1)S(1)}, u32[]{:S(2)}, u32[]{:S(2)}) async-start(bf16[8,80,128]{2,1,0:T(8,128)(2,1)} %spread.1), calls=%async_computation.1 | async-start | bytes 327680 | tf_op jit(solution)/shard_map/all_to_all | solution.py:577
  10.7 1.6 %label_places.1 = (s32[1,256]{1,0:T(1,128)S(1)}, bf16[32,1024]{1,0:T(8,128)(2,1)S(1)}, s32[1,256]{1,0:T(1,128)S(1)}, bf16[32,1024]{1,0:T(8,128)(2,1)S(1)}, bf16[...) custom-call(s32[1,512]{1,0:T(1,128)} %bitcast.35), custom_call_target="tpu_custom_call" | custom-call | flops 2621440 | bytes 1048576 | tf_op jit(solution)/shard_map/label_places/pallas_call | solution.py:107
  12.3 6.5 %all-to-all-done.1.in_ref = bf16[8,80,128]{2,1,0:T(8,128)(2,1)S(1)} async-done(((bf16[8,80,128]{2,1,0:T(8,128)(2,1)}), bf16[8,80,128]{2,1,0:T(8,128)(2,1)S(1)}, u32[]{:S(2)}, u32[]{:S(2)}) %all-to-all-start.1) | async-done | bytes 163872 | tf_op jit(solution)/shard_map/all_to_all | solution.py:577
  19.0 5.7 %collective-permute-start.3 = (bf16[592,128]{1,0:T(8,128)(2,1)S(1)}, bf16[592,128]{1,0:T(8,128)(2,1)S(1)}, u32[]{:S(2)}, u32[]{:S(2)}) collective-permute-start(bf16[592,128]{1,0:T(8,128)(2,1)S(1)} %pack_tokens.1.refs_0_), channel_id=1, source_target_pairs={{0,36},{2,38},{4,32},{6,34},{8,44},{10,46},{12,40},{14,42},{16,52}... | collective-permute-start | bytes 454664 | tf_op jit(solution)/shard_map/ppermute | solution.py:537
  26.3 2.6 %collective-permute-done.3.refs_3_ = bf16[592,128]{1,0:T(8,128)(2,1)S(1)} collective-permute-done((bf16[592,128]{1,0:T(8,128)(2,1)S(1)}, bf16[592,128]{1,0:T(8,128)(2,1)S(1)}, u32[]{:S(2)}, u32[]{:S(2)}) %collective-permute-start.3) | collective-permute-done | bytes 151584 | tf_op jit(solution)/shard_map/ppermute | solution.py:537
  28.9 2.5 %collective-permute-done.2.refs_2_ = bf16[592,128]{1,0:T(8,128)(2,1)S(1)} collective-permute-done((bf16[592,128]{1,0:T(8,128)(2,1)S(1)}, bf16[592,128]{1,0:T(8,128)(2,1)S(1)}, u32[]{:S(2)}, u32[]{:S(2)}) %collective-permute-start.2) | collective-permute-done | bytes 151584 | tf_op jit(solution)/shard_map/ppermute | solution.py:537
  31.9 4.2 %collective-permute-start.7 = (bf16[4,592,128]{2,1,0:T(8,128)(2,1)S(1)}, bf16[4,592,128]{2,1,0:T(8,128)(2,1)S(1)}, u32[]{:S(2)}, u32[]{:S(2)}) collective-permute-start(bf16[4,592,128]{2,1,0:T(8,128)(2,1)S(1)} %in_order.1.refs_0_), channel_id=1, source_target_pairs={{0,54},{2,48},{4,50},{6,52},{8,62},{10,56},{12,58},{14,60},{16,6},... | collective-permute-start | bytes 1818632 | tf_op jit(solution)/shard_map/ppermute | solution.py:537
  36.4 7.3 %permute_embedding.1.refs_4_.refs_2_.refs_1_ = bf16[1024,4608]{1,0:T(8,128)(2,1)S(1)} custom-call(bf16[1000,4608]{1,0:T(8,128)(2,1)} %get-tuple-element.405), custom_call_target="tpu_custom_call" | custom-call | bytes 18432000 | tf_op jit(solution)/shard_map/permute_embedding/pallas_call | solution.py:152
  43.8 4.7 %collective-permute-done.7.refs_3_ = bf16[4,592,128]{2,1,0:T(8,128)(2,1)S(1)} collective-permute-done((bf16[4,592,128]{2,1,0:T(8,128)(2,1)S(1)}, bf16[4,592,128]{2,1,0:T(8,128)(2,1)S(1)}, u32[]{:S(2)}, u32[]{:S(2)}) %collective-permute-start.7) | collective-permute-done | bytes 606240 | tf_op jit(solution)/shard_map/ppermute | solution.py:537
  48.5 3.4 %collective-permute-done.6.refs_2_ = bf16[4,592,128]{2,1,0:T(8,128)(2,1)S(1)} collective-permute-done((bf16[4,592,128]{2,1,0:T(8,128)(2,1)S(1)}, bf16[4,592,128]{2,1,0:T(8,128)(2,1)S(1)}, u32[]{:S(2)}, u32[]{:S(2)}) %collective-permute-start.6) | collective-permute-done | bytes 606240 | tf_op jit(solution)/shard_map/ppermute | solution.py:537
  52.4 3.3 %logits.2 = (bf16[144,1024]{1,0:T(8,128)(2,1)S(1)}, bf16[144,1024]{1,0:T(8,128)(2,1)S(1)}, f32[8,256]{1,0:T(8,128)S(1)}, f32[256,128]{1,0:T(8,128)S(1)}) custom-call(bf16[4,592,128]{2,1,0:T(8,128)(2,1)S(1)} %in_order.1.refs_0_, bf16[4,592,128]{2,1,0:T(8,128)(2,1)S(1)} %collective-permute-done.5.refs_1_, ...), custom_call_target="tpu_custom_call" | custom-call | flops 2415919104 | bytes 9437184 | tf_op jit(solution)/shard_map/logits/pallas_call | solution.py:294
  55.7 3.9 %logits.3 = (bf16[144,1024]{1,0:T(8,128)(2,1)S(1)}, bf16[144,1024]{1,0:T(8,128)(2,1)S(1)}, f32[8,256]{1,0:T(8,128)S(1)}, f32[256,128]{1,0:T(8,128)}) custom-call(bf16[4,592,128]{2,1,0:T(8,128)(2,1)S(1)} %collective-permute-done.4.refs_0_, bf16[4,592,128]{2,1,0:T(8,128)(2,1)S(1)} %collective-permute-done.8.refs_1_, ...), custom_call_target="tpu_custom_call" | custom-call | flops 2415919104 | bytes 9437184 | tf_op jit(solution)/shard_map/logits/pallas_call | solution.py:294
  59.6 1.7 %gradient.3 = bf16[8,72,1152]{2,1,0:T(8,128)(2,1)S(1)} custom-call(bf16[144,1024]{1,0:T(8,128)(2,1)S(1)} %get-tuple-element.231.refs_0_, bf16[144,1024]{1,0:T(8,128)(2,1)S(1)} %get-tuple-element.218.refs_1_.refs_0_, bf16[1024,4608]{1,0:T(8,128)(2,1)S(1)} %permute_embedding.1.refs_4_.refs_2_.refs_1_, f32[8,256]{1,0:T(8,128)S(1)} %get-tuple-element.217.refs_3_.refs_2_), custom_call_target="tpu_custom_call" | custom-call | flops 1358954496 | bytes 4718592 | tf_op jit(solution)/shard_map/gradient/pallas_call | solution.py:362
  63.0 1.5 %product.3.term_ref = f32[288,2304]{1,0:T(8,128)S(1)} custom-call(bf16[144,1024]{1,0:T(8,128)(2,1)S(1)} %get-tuple-element.235.refs_0_, bf16[144,1024]{1,0:T(8,128)(2,1)S(1)} %get-tuple-element.227.refs_1_.refs_0_, bf16[1024,4608]{1,0:T(8,128)(2,1)S(1)} %permute_embedding.1.refs_4_.refs_2_.refs_1_), custom_call_target="tpu_custom_call" | custom-call | flops 1358954496 | bytes 4718592 | tf_op jit(solution)/shard_map/product/pallas_call | solution.py:381
  65.1 1.6 %collective-permute-start.16 = (bf16[4,72,1152]{2,1,0:T(8,128)(2,1)S(1)}, bf16[4,72,1152]{2,1,0:T(8,128)(2,1)S(1)}, u32[]{:S(2)}, u32[]{:S(2)}) collective-permute-start(bf16[4,72,1152]{2,1,0:T(8,128)(2,1)S(1)} %get-tuple-element.239), channel_id=1, source_target_pairs={{0,16},{2,18},{4,20},{6,22},{8,24},{10,26},{12,28},{14,30},{16,32}... | collective-permute-start | bytes 1990664 | tf_op jit(solution)/shard_map/ppermute | solution.py:537
  69.2 1.9 %collective-permute-start.15 = (bf16[4,72,1152]{2,1,0:T(8,128)(2,1)S(1)}, bf16[4,72,1152]{2,1,0:T(8,128)(2,1)S(1)}, u32[]{:S(2)}, u32[]{:S(2)}) collective-permute-start(bf16[4,72,1152]{2,1,0:T(8,128)(2,1)S(1)} %combine.4), channel_id=1, source_target_pairs={{0,2},{2,4},{4,6},{6,0},{8,10},{10,12},{12,14},{14,8},{16,18},{18,... | collective-permute-start | bytes 1990664 | tf_op jit(solution)/shard_map/ppermute | solution.py:537
  74.7 9.0 %collective-permute-done.16.refs_2_ = bf16[4,72,1152]{2,1,0:T(8,128)(2,1)S(1)} collective-permute-done((bf16[4,72,1152]{2,1,0:T(8,128)(2,1)S(1)}, bf16[4,72,1152]{2,1,0:T(8,128)(2,1)S(1)}, u32[]{:S(2)}, u32[]{:S(2)}) %collective-permute-start.16) | collective-permute-done | bytes 663584 | tf_op jit(solution)/shard_map/ppermute | solution.py:537
  84.6 2.7 %collective-permute-done.15.refs_1_ = bf16[4,72,1152]{2,1,0:T(8,128)(2,1)S(1)} collective-permute-done((bf16[4,72,1152]{2,1,0:T(8,128)(2,1)S(1)}, bf16[4,72,1152]{2,1,0:T(8,128)(2,1)S(1)}, u32[]{:S(2)}, u32[]{:S(2)}) %collective-permute-start.15) | collective-permute-done | bytes 663584 | tf_op jit(solution)/shard_map/ppermute | solution.py:537
  89.6 4.7 %collective-permute-start.20 = (bf16[96,1152]{1,0:T(8,128)(2,1)S(1)}, bf16[96,1152]{1,0:T(8,128)(2,1)S(1)}, u32[]{:S(2)}, u32[]{:S(2)}) collective-permute-start(bf16[96,1152]{1,0:T(8,128)(2,1)S(1)} %get-tuple-element.244), channel_id=1, source_target_pairs={{0,36},{2,38},{4,32},{6,34},{8,44},{10,46},{12,40},{14,42},{16,52}... | collective-permute-start | bytes 663560 | tf_op jit(solution)/shard_map/ppermute | solution.py:537
  94.3 2.5 %collective-permute-done.18.refs_1_ = bf16[96,1152]{1,0:T(8,128)(2,1)S(1)} collective-permute-done((bf16[96,1152]{1,0:T(8,128)(2,1)S(1)}, bf16[96,1152]{1,0:T(8,128)(2,1)S(1)}, u32[]{:S(2)}, u32[]{:S(2)}) %collective-permute-start.18) | collective-permute-done | bytes 221216 | tf_op jit(solution)/shard_map/ppermute | solution.py:537
  97.9 4.0 %collective-permute-done.20.refs_3_ = bf16[96,1152]{1,0:T(8,128)(2,1)S(1)} collective-permute-done((bf16[96,1152]{1,0:T(8,128)(2,1)S(1)}, bf16[96,1152]{1,0:T(8,128)(2,1)S(1)}, u32[]{:S(2)}, u32[]{:S(2)}) %collective-permute-start.20) | collective-permute-done | bytes 221216 | tf_op jit(solution)/shard_map/ppermute | solution.py:537
  102.9 3.4 %all-to-all-start.2 = ((bf16[8,32,640]{2,1,0:T(8,128)(2,1)}), bf16[8,32,640]{2,1,0:T(8,128)(2,1)S(1)}, u32[]{:S(2)}, u32[]{:S(2)}) async-start(bf16[8,32,640]{2,1,0:T(8,128)(2,1)} %plane_sum.1), calls=%async_computation.2 | async-start | bytes 655360 | tf_op jit(solution)/shard_map/all_to_all | solution.py:605
  106.3 10.0 %all-to-all-done.2.in_ref = bf16[8,32,640]{2,1,0:T(8,128)(2,1)S(1)} async-done(((bf16[8,32,640]{2,1,0:T(8,128)(2,1)}), bf16[8,32,640]{2,1,0:T(8,128)(2,1)S(1)}, u32[]{:S(2)}, u32[]{:S(2)}) %all-to-all-start.2) | async-done | bytes 327712 | tf_op jit(solution)/shard_map/all_to_all | solution.py:605
  (48 shorter events, 17.6 us)
Async XLA Ops:
  2.1 16.7 %all-to-all-start.1 = ((bf16[8,80,128]{2,1,0:T(8,128)(2,1)}), bf16[8,80,128]{2,1,0:T(8,128)(2,1)S(1)}, u32[]{:S(2)}, u32[]{:S(2)}) async-start(bf16[8,80,128]{2,1,0:T(8,128)(2,1)} %spread.1), calls=%async_computation.1 | async-start | bytes 327680 | tf_op jit(solution)/shard_map/all_to_all | solution.py:577
  19.0 9.9 %collective-permute-start.3 = (bf16[592,128]{1,0:T(8,128)(2,1)S(1)}, bf16[592,128]{1,0:T(8,128)(2,1)S(1)}, u32[]{:S(2)}, u32[]{:S(2)}) collective-permute-start(bf16[592,128]{1,0:T(8,128)(2,1)S(1)} %pack_tokens.1.refs_0_), channel_id=1, source_target_pairs={{0,36},{2,38},{4,32},{6,34},{8,44},{10,46},{12,40},{14,42},{16,52}... | collective-permute-start | bytes 454664 | tf_op jit(solution)/shard_map/ppermute | solution.py:537
  24.8 6.7 %collective-permute-start.2 = (bf16[592,128]{1,0:T(8,128)(2,1)S(1)}, bf16[592,128]{1,0:T(8,128)(2,1)S(1)}, u32[]{:S(2)}, u32[]{:S(2)}) collective-permute-start(bf16[592,128]{1,0:T(8,128)(2,1)S(1)} %pack_tokens.1.refs_0_), channel_id=1, source_target_pairs={{0,32},{2,34},{4,36},{6,38},{8,40},{10,42},{12,44},{14,46},{16,48}... | collective-permute-start | bytes 454664 | tf_op jit(solution)/shard_map/ppermute | solution.py:537
  25.1 6.7 %collective-permute-start.1 = (bf16[592,128]{1,0:T(8,128)(2,1)S(1)}, bf16[592,128]{1,0:T(8,128)(2,1)S(1)}, u32[]{:S(2)}, u32[]{:S(2)}) collective-permute-start(bf16[592,128]{1,0:T(8,128)(2,1)S(1)} %pack_tokens.1.refs_0_), channel_id=1, source_target_pairs={{0,4},{2,6},{4,0},{6,2},{8,12},{10,14},{12,8},{14,10},{16,20},{18,... | collective-permute-start | bytes 454664 | tf_op jit(solution)/shard_map/ppermute | solution.py:537
  31.9 16.6 %collective-permute-start.7 = (bf16[4,592,128]{2,1,0:T(8,128)(2,1)S(1)}, bf16[4,592,128]{2,1,0:T(8,128)(2,1)S(1)}, u32[]{:S(2)}, u32[]{:S(2)}) collective-permute-start(bf16[4,592,128]{2,1,0:T(8,128)(2,1)S(1)} %in_order.1.refs_0_), channel_id=1, source_target_pairs={{0,54},{2,48},{4,50},{6,52},{8,62},{10,56},{12,58},{14,60},{16,6},... | collective-permute-start | bytes 1818632 | tf_op jit(solution)/shard_map/ppermute | solution.py:537
  36.0 15.9 %collective-permute-start.6 = (bf16[4,592,128]{2,1,0:T(8,128)(2,1)S(1)}, bf16[4,592,128]{2,1,0:T(8,128)(2,1)S(1)}, u32[]{:S(2)}, u32[]{:S(2)}) collective-permute-start(bf16[4,592,128]{2,1,0:T(8,128)(2,1)S(1)} %in_order.1.refs_0_), channel_id=1, source_target_pairs={{0,16},{2,18},{4,20},{6,22},{8,24},{10,26},{12,28},{14,30},{16,32}... | collective-permute-start | bytes 1818632 | tf_op jit(solution)/shard_map/ppermute | solution.py:537
  36.0 15.9 %collective-permute-start.5 = (bf16[4,592,128]{2,1,0:T(8,128)(2,1)S(1)}, bf16[4,592,128]{2,1,0:T(8,128)(2,1)S(1)}, u32[]{:S(2)}, u32[]{:S(2)}) collective-permute-start(bf16[4,592,128]{2,1,0:T(8,128)(2,1)S(1)} %in_order.1.refs_0_), channel_id=1, source_target_pairs={{0,2},{2,4},{4,6},{6,0},{8,10},{10,12},{12,14},{14,8},{16,18},{18,... | collective-permute-start | bytes 1818632 | tf_op jit(solution)/shard_map/ppermute | solution.py:537
  43.7 12.0 %collective-permute-start.4 = (bf16[4,592,128]{2,1,0:T(8,128)(2,1)S(1)}, bf16[4,592,128]{2,1,0:T(8,128)(2,1)S(1)}, u32[]{:S(2)}, u32[]{:S(2)}) collective-permute-start(bf16[4,592,128]{2,1,0:T(8,128)(2,1)S(1)} %in_order.1.refs_0_), channel_id=1, source_target_pairs={{0,1},{1,0},{2,3},{3,2},{4,5},{5,4},{6,7},{7,6},{8,9},{9,8},{10,11... | collective-permute-start | bytes 1818632 | tf_op jit(solution)/shard_map/ppermute | solution.py:529
  51.9 3.8 %collective-permute-start.8 = (bf16[4,592,128]{2,1,0:T(8,128)(2,1)S(1)}, bf16[4,592,128]{2,1,0:T(8,128)(2,1)S(1)}, u32[]{:S(2)}, u32[]{:S(2)}) collective-permute-start(bf16[4,592,128]{2,1,0:T(8,128)(2,1)S(1)} %collective-permute-done.5.refs_1_), channel_id=1, source_target_pairs={{0,1},{1,0},{2,3},{3,2},{4,5},{5,4},{6,7},{7,6},{8,9},{9,8},{10,11... | collective-permute-start | bytes 1818632 | tf_op jit(solution)/shard_map/ppermute | solution.py:529
  51.9 3.8 %collective-permute-start.9 = (bf16[4,592,128]{2,1,0:T(8,128)(2,1)S(1)}, bf16[4,592,128]{2,1,0:T(8,128)(2,1)S(1)}, u32[]{:S(2)}, u32[]{:S(2)}) collective-permute-start(bf16[4,592,128]{2,1,0:T(8,128)(2,1)S(1)} %collective-permute-done.6.refs_2_), channel_id=1, source_target_pairs={{0,1},{1,0},{2,3},{3,2},{4,5},{5,4},{6,7},{7,6},{8,9},{9,8},{10,11... | collective-permute-start | bytes 1818632 | tf_op jit(solution)/shard_map/ppermute | solution.py:529
  52.4 3.3 %collective-permute-start.10 = (bf16[4,592,128]{2,1,0:T(8,128)(2,1)S(1)}, bf16[4,592,128]{2,1,0:T(8,128)(2,1)S(1)}, u32[]{:S(2)}, u32[]{:S(2)}) collective-permute-start(bf16[4,592,128]{2,1,0:T(8,128)(2,1)S(1)} %collective-permute-done.7.refs_3_), channel_id=1, source_target_pairs={{0,1},{1,0},{2,3},{3,2},{4,5},{5,4},{6,7},{7,6},{8,9},{9,8},{10,11... | collective-permute-start | bytes 1818632 | tf_op jit(solution)/shard_map/ppermute | solution.py:529
  61.3 3.3 %collective-permute-start.11 = (bf16[8,72,1152]{2,1,0:T(8,128)(2,1)S(1)}, bf16[8,72,1152]{2,1,0:T(8,128)(2,1)S(1)}, u32[]{:S(2)}, u32[]{:S(2)}) collective-permute-start(bf16[8,72,1152]{2,1,0:T(8,128)(2,1)S(1)} %gradient.3), channel_id=1, source_target_pairs={{0,1},{1,0},{2,3},{3,2},{4,5},{5,4},{6,7},{7,6},{8,9},{9,8},{10,11... | collective-permute-start | bytes 3981320 | tf_op jit(solution)/shard_map/ppermute | solution.py:529
  62.9 6.1 %collective-permute-start.12 = (bf16[4,72,1152]{2,1,0:T(8,128)(2,1)S(1)}, bf16[4,72,1152]{2,1,0:T(8,128)(2,1)S(1)}, u32[]{:S(2)}, u32[]{:S(2)}) collective-permute-start(bf16[4,72,1152]{2,1,0:T(8,128)(2,1)S(1)} %gradient.4), channel_id=1, source_target_pairs={{0,1},{1,0},{2,3},{3,2},{4,5},{5,4},{6,7},{7,6},{8,9},{9,8},{10,11... | collective-permute-start | bytes 1990664 | tf_op jit(solution)/shard_map/ppermute | solution.py:529
  65.1 18.5 %collective-permute-start.16 = (bf16[4,72,1152]{2,1,0:T(8,128)(2,1)S(1)}, bf16[4,72,1152]{2,1,0:T(8,128)(2,1)S(1)}, u32[]{:S(2)}, u32[]{:S(2)}) collective-permute-start(bf16[4,72,1152]{2,1,0:T(8,128)(2,1)S(1)} %get-tuple-element.239), channel_id=1, source_target_pairs={{0,16},{2,18},{4,20},{6,22},{8,24},{10,26},{12,28},{14,30},{16,32}... | collective-permute-start | bytes 1990664 | tf_op jit(solution)/shard_map/ppermute | solution.py:537
  66.7 17.9 %collective-permute-start.17 = (bf16[4,72,1152]{2,1,0:T(8,128)(2,1)S(1)}, bf16[4,72,1152]{2,1,0:T(8,128)(2,1)S(1)}, u32[]{:S(2)}, u32[]{:S(2)}) collective-permute-start(bf16[4,72,1152]{2,1,0:T(8,128)(2,1)S(1)} %get-tuple-element.240), channel_id=1, source_target_pairs={{0,54},{2,48},{4,50},{6,52},{8,62},{10,56},{12,58},{14,60},{16,6},... | collective-permute-start | bytes 1990664 | tf_op jit(solution)/shard_map/ppermute | solution.py:537
  69.2 18.1 %collective-permute-start.15 = (bf16[4,72,1152]{2,1,0:T(8,128)(2,1)S(1)}, bf16[4,72,1152]{2,1,0:T(8,128)(2,1)S(1)}, u32[]{:S(2)}, u32[]{:S(2)}) collective-permute-start(bf16[4,72,1152]{2,1,0:T(8,128)(2,1)S(1)} %combine.4), channel_id=1, source_target_pairs={{0,2},{2,4},{4,6},{6,0},{8,10},{10,12},{12,14},{14,8},{16,18},{18,... | collective-permute-start | bytes 1990664 | tf_op jit(solution)/shard_map/ppermute | solution.py:537
  72.1 1.7 %collective-permute-start.13 = (bf16[2,72,1152]{2,1,0:T(8,128)(2,1)S(1)}, bf16[2,72,1152]{2,1,0:T(8,128)(2,1)S(1)}, u32[]{:S(2)}, u32[]{:S(2)}) collective-permute-start(bf16[2,72,1152]{2,1,0:T(8,128)(2,1)S(1)} %get-tuple-element.236), channel_id=1, source_target_pairs={{0,1},{1,0},{2,3},{3,2},{4,5},{5,4},{6,7},{7,6},{8,9},{9,8},{10,11... | collective-permute-start | bytes 995336 | tf_op jit(solution)/shard_map/ppermute | solution.py:529
  72.2 2.1 %collective-permute-start.14 = (bf16[2,72,1152]{2,1,0:T(8,128)(2,1)S(1)}, bf16[2,72,1152]{2,1,0:T(8,128)(2,1)S(1)}, u32[]{:S(2)}, u32[]{:S(2)}) collective-permute-start(bf16[2,72,1152]{2,1,0:T(8,128)(2,1)S(1)} %get-tuple-element.237), channel_id=1, source_target_pairs={{0,1},{1,0},{2,3},{3,2},{4,5},{5,4},{6,7},{7,6},{8,9},{9,8},{10,11... | collective-permute-start | bytes 995336 | tf_op jit(solution)/shard_map/ppermute | solution.py:529
  74.6 41.6 %copy-start = (bf16[32,288]{1,0:T(8,128)(2,1)S(1)}, bf16[32,288]{1,0:T(8,128)(2,1)}, u32[]{:S(2)}) copy-start(bf16[32,288]{1,0:T(8,128)(2,1)} %values_ref.1) | copy-start | bytes 55300
  74.7 41.6 %copy-start.1 = (f32[512]{0:T(512)S(1)}, f32[512]{0:T(512)}, u32[]{:S(2)}) copy-start(f32[512]{0:T(512)} %param.11) | copy-start | bytes 6148
  87.7 9.1 %collective-permute-start.18 = (bf16[96,1152]{1,0:T(8,128)(2,1)S(1)}, bf16[96,1152]{1,0:T(8,128)(2,1)S(1)}, u32[]{:S(2)}, u32[]{:S(2)}) collective-permute-start(bf16[96,1152]{1,0:T(8,128)(2,1)S(1)} %get-tuple-element.242), channel_id=1, source_target_pairs={{0,4},{2,6},{4,0},{6,2},{8,12},{10,14},{12,8},{14,10},{16,20},{18,... | collective-permute-start | bytes 663560 | tf_op jit(solution)/shard_map/ppermute | solution.py:537
  88.9 8.9 %collective-permute-start.19 = (bf16[96,1152]{1,0:T(8,128)(2,1)S(1)}, bf16[96,1152]{1,0:T(8,128)(2,1)S(1)}, u32[]{:S(2)}, u32[]{:S(2)}) collective-permute-start(bf16[96,1152]{1,0:T(8,128)(2,1)S(1)} %get-tuple-element.243), channel_id=1, source_target_pairs={{0,32},{2,34},{4,36},{6,38},{8,40},{10,42},{12,44},{14,46},{16,48}... | collective-permute-start | bytes 663560 | tf_op jit(solution)/shard_map/ppermute | solution.py:537
  89.6 12.2 %collective-permute-start.20 = (bf16[96,1152]{1,0:T(8,128)(2,1)S(1)}, bf16[96,1152]{1,0:T(8,128)(2,1)S(1)}, u32[]{:S(2)}, u32[]{:S(2)}) collective-permute-start(bf16[96,1152]{1,0:T(8,128)(2,1)S(1)} %get-tuple-element.244), channel_id=1, source_target_pairs={{0,36},{2,38},{4,32},{6,34},{8,44},{10,46},{12,40},{14,42},{16,52}... | collective-permute-start | bytes 663560 | tf_op jit(solution)/shard_map/ppermute | solution.py:537
  102.9 13.4 %all-to-all-start.2 = ((bf16[8,32,640]{2,1,0:T(8,128)(2,1)}), bf16[8,32,640]{2,1,0:T(8,128)(2,1)S(1)}, u32[]{:S(2)}, u32[]{:S(2)}) async-start(bf16[8,32,640]{2,1,0:T(8,128)(2,1)} %plane_sum.1), calls=%async_computation.2 | async-start | bytes 655360 | tf_op jit(solution)/shard_map/all_to_all | solution.py:605
  (1 other events, 31.7 us)

commit v6 on v5

--- a/solution.py
+++ b/solution.py
@@ -250,7 +250,7 @@
 
 
 def logits_kernel(*refs):
-    blocks, (embedding_ref, labels_ref, slot_ref, e_near, e_far, stats_ref, scale_ref, normed) = refs[:4], refs[4:]
+    blocks, (embedding_ref, labels_ref, slot_ref, e_near, e_far, stats_ref, *scale_ref, normed) = refs[:4], refs[4:]
     gains = [
         [blocks[ry * 2][y1 * 2, TILES * BLOCK : PACKED, :].astype(F32) for y1 in range(2)] for ry in range(2)
     ]
@@ -266,7 +266,8 @@
             v = tile(*place)
             squares += v * v
         scale = lax.rsqrt(jnp.sum(squares, axis=1, keepdims=True) / D + EPS)
-        scale_ref[tokens, :] = jnp.broadcast_to(scale, (BLOCK, 128))
+        for ref in scale_ref:
+            ref[tokens, :] = jnp.broadcast_to(scale, (BLOCK, 128))
         for ry, y1, k in places:
             column = ry * HALF + y1 * WIDE + k * 128
             normed[tokens, column : column + 128] = (
@@ -290,17 +291,17 @@
         e_ref[128:144, :] = slot_ref[rx * 16 : (rx + 1) * 16, :]
 
 
-def logits_of(blocks, embedding, labels, slots):
+def logits_of(blocks, embedding, labels, slots, with_scale):
     return pl.pallas_call(
         logits_kernel,
         in_specs=[WHOLE] * 7,
-        out_specs=[WHOLE] * 4,
+        out_specs=[WHOLE] * (3 + with_scale),
         out_shape=[
             pltpu.VMEM((144, PADDED), BF16),
             pltpu.VMEM((144, PADDED), BF16),
             pltpu.VMEM((8, 256), F32),
-            pltpu.VMEM((256, 128), F32),
-        ],
+        ]
+        + [pltpu.VMEM((256, 128), F32)] * with_scale,
         scratch_shapes=[pltpu.VMEM((256, D), BF16)],
         compiler_params=BIG,
         cost_estimate=pl.CostEstimate(flops=2 * 256 * PADDED * D, bytes_accessed=2 * PADDED * D, transcendentals=2 * 256 * PADDED),
@@ -449,7 +450,14 @@
 
 
 def plane_kernel(*refs):
-    in_refs, (place_ref, more_ref, out_ref) = refs[:4], refs[4:]
+    in_refs, (place_ref, more_ref, values_ref, gain_ref, weight_ref, scale_ref, out_ref, *kept) = refs[:4], refs[4:]
+    zh, x1, x0, core = (lax.axis_index(name) for name in ("z_hi", "x1", "x0", "core"))
+    own = (((zh * 2 + x1) * 2 + x0) * 2 + core) * 32 + lax.broadcasted_iota(jnp.int32, (32, 512), 0)
+    own_weight = jnp.where(lax.broadcasted_iota(jnp.int32, (32, 512), 1) == own, weight_ref[...], 0.0)
+    kept[0][...] = values_ref[...].astype(F32)
+    kept[1][...] = gain_ref[...].astype(F32)
+    kept[2][...] = jnp.broadcast_to(jnp.sum(own_weight, axis=1, keepdims=True), (32, 128))
+    kept[3][...] = scale_ref[pl.ds(pl.multiple_of(x1 * BLOCK + zh * 32, 32), 32), :]
     total = in_refs[0][0:BLOCK, :].astype(F32)
     for ref in in_refs[1:]:
         total += ref[0:BLOCK, :].astype(F32)
@@ -468,19 +476,26 @@
             out_ref[zl * 2 + zh] = jnp.concatenate([main, rows, sums], axis=1).astype(BF16)
 
 
-def plane_sum(received, place, more):
+def plane_sum(received, place, more, values, gain, weight, scale):
+    args = (*received, place, more, values, gain, weight, scale)
     return pl.pallas_call(
         plane_kernel,
-        in_specs=[WHOLE] * 6,
-        out_specs=WHOLE,
-        out_shape=pltpu.VMEM((8, 32, 640), BF16),
+        in_specs=[WHOLE] * len(args),
+        out_specs=[WHOLE] * 5,
+        out_shape=[
+            pltpu.VMEM((8, 32, 640), BF16),
+            pltpu.VMEM((32, PIECE), F32),
+            pltpu.VMEM((1, PIECE), F32),
+            pltpu.VMEM((32, 128), F32),
+            pltpu.VMEM((32, 128), F32),
+        ],
         compiler_params=BIG,
         name="plane_sum",
-    )(*(near(a) for a in (*received, place, more)))
+    )(*(near(a) for a in args))
 
 
 def final_kernel(in_ref, values_ref, gain_ref, weight_ref, scale_ref, loss_ref, grad_ref):
-    zh, x1, x0, core = (lax.axis_index(name) for name in ("z_hi", "x1", "x0", "core"))
+    zh = lax.axis_index("z_hi")
     total = in_ref[0].astype(F32)
     for source in range(1, 8):
         total += in_ref[source].astype(F32)
@@ -494,10 +509,8 @@
         return jnp.sum(jnp.where(pick, jnp.broadcast_to(value, (32, BLOCK)), 0.0), axis=1, keepdims=True)
 
     sum_exp, inner_others, raw = column(0), column(1), column(2)
-    own = (((zh * 2 + x1) * 2 + x0) * 2 + core) * 32 + lax.broadcasted_iota(jnp.int32, (32, 512), 0)
-    own_weight = jnp.where(lax.broadcasted_iota(jnp.int32, (32, 512), 1) == own, weight_ref[...], 0.0)
-    weight = jnp.sum(own_weight, axis=1, keepdims=True)
-    scaling = scale_ref[pl.ds(pl.multiple_of(x1 * BLOCK + zh * 32, 32), 32), 0:1]
+    weight = weight_ref[:, 0:1]
+    scaling = scale_ref[:, 0:1]
     ratio = jnp.tanh(raw / CAP)
     capped = CAP * ratio
     log_total = jnp.log(sum_exp)
@@ -507,8 +520,8 @@
     share = weight / sum_exp
     grad_normed = total[:, 0:PIECE] * share + total[:, PIECE : 2 * PIECE] * coefficient
     inner = (inner_others * share + coefficient * raw) / scaling
-    upstream = grad_normed * gain_ref[...].astype(F32)
-    values = values_ref[...].astype(F32)
+    upstream = grad_normed * gain_ref[...]
+    values = values_ref[...]
     grad_ref[...] = scaling * upstream - values * (scaling * scaling * scaling * inner / D)
     eye = lax.broadcasted_iota(jnp.int32, (32, 32), 0) == lax.broadcasted_iota(jnp.int32, (32, 32), 1)
     loss_ref[...] = jnp.sum(jnp.where(eye, jnp.broadcast_to(loss, (32, 32)), 0.0), axis=0, keepdims=True)
@@ -575,22 +588,22 @@
 def on_device(residual, final_gain, embedding, labels, token_weight):
     gain = final_gain.reshape(1, PIECE)
     gathered = lax.all_to_all(spread(residual, final_gain), ("z_lo", "z_hi"), 0, 0, tiled=True)
+    piece, embedding, labels = lax.optimization_barrier((pack_tokens(gathered), embedding, labels))
+
+    moved = [shifted(piece, 2 * dx, 2 * dy) for dy, dx in PLACES[1:]]
     *early, rounds = label_places(labels.reshape(1, 512))
-    piece, embedding, rounds, early = lax.optimization_barrier((pack_tokens(gathered), embedding, rounds, early))
+    more = later_rows(labels, embedding, rounds[0, 0])
+    moved, more, early = lax.optimization_barrier((moved, more, early))
     own_labels, own_slots, other_labels, other_slots, place = early
-    more = later_rows(labels, embedding, rounds[0, 0])
-
-    moved = [shifted(piece, 2 * dx, 2 * dy) for dy, dx in PLACES[1:]]
-    moved, more = lax.optimization_barrier((moved, more))
     packed = in_order([piece] + moved)
     table = permute_embedding(embedding)
     blocks = [packed] + [shifted(packed, *SHIFTS[parity]) for parity in PLACES[1:]]
     blocks[1:], table = lax.optimization_barrier((blocks[1:], table))
     other_blocks = [swap_cores(block) for block in blocks]
 
-    *e, stats, scale = logits_of(blocks, table, own_labels, own_slots)
+    *e, stats, scale = logits_of(blocks, table, own_labels, own_slots, True)
     other_blocks, e = lax.optimization_barrier((other_blocks, e))
-    *e_other, stats_other, _ = logits_of(other_blocks, table, other_labels, other_slots)
+    *e_other, stats_other = logits_of(other_blocks, table, other_labels, other_slots, False)
     far_part, e_other = lax.optimization_barrier((gradient_of(1, (0, 1), e_other, table, stats_other), e_other))
     near_part, e = lax.optimization_barrier((gradient_of(0, (1,), e_other, table, stats_other), e))
     far_blocks = combine((0, 1), product_of(1, (0, 1), e, table), stats, [swap_cores(part) for part in far_part])
@@ -601,10 +614,11 @@
     (stay_block,) = combine((0,), product_of(0, (0,), e, table), stats, [swap_cores(part) for part in stay_part])
     parts = [stay_block, near_block, *far_blocks]
     sums = class_sum([parts[0]] + [shifted(part, *SHIFTS[parity]) for part, parity in zip(parts[1:], PLACES[1:])])
-    plane = [sums[0]] + [shifted(block, 2 * dx, 2 * dy) for block, (dy, dx) in zip(sums[1:], PLACES[1:])]
-    column = lax.all_to_all(plane_sum(plane, place, more), ("z_lo", "z_hi"), 0, 0, tiled=True)
-
-    loss, grad = finish(column, residual, gain, token_weight.reshape(1, 512), scale)
+    plane = [shifted(block, 2 * dx, 2 * dy) for block, (dy, dx) in zip(sums[:0:-1], PLACES[:0:-1])]
+    plane = [sums[0]] + plane[::-1]
+    plane, *kept = plane_sum(plane, place, more, residual, gain, token_weight.reshape(1, 512), scale)
+    column = lax.all_to_all(plane, ("z_lo", "z_hi"), 0, 0, tiled=True)
+    loss, grad = finish(column, *kept)
     return (loss.reshape(32), grad)
 
 

time: 118 us -> 117 us (level)
  blocking collectives: 0 us -> 13.5 us
  waiting for transfers between devices: 51.1 us -> 41.1 us
  starting transfers between devices: 36.5 us -> 33.1 us
  Pallas kernels: 28.1 us -> 26.9 us
    all_to_all x0 -> x1, blocking collectives: none -> 13.5 us  [on_device(): column = lax.all_to_all(plane, ('z_lo', 'z_hi'), 0, 0, tiled=True)]
    all_to_all x1 -> x0, waiting for transfers between devices: 9.96 us -> none  [on_device(): lax.all_to_all(plane_sum(plane, place, more), ('z_lo', 'z_hi'), 0, 0, til...]
    all_to_all x1 -> x0, starting transfers between devices: 3.44 us -> none  [on_device(): lax.all_to_all(plane_sum(plane, place, more), ('z_lo', 'z_hi'), 0, 0, til...]
    all_to_all x1, waiting for transfers between devices: 6.47 us -> 8.09 us  [on_device(): lax.all_to_all(spread(residual, final_gain), ('z_lo', 'z_hi'), 0, 0, tile...]
    ppermute x12, waiting for transfers between devices: 33.8 us -> 32.2 us  [shifted(): return lax.ppermute(array, CHIPS, pairs)]
    pallas_call x3, Pallas kernels: 8.18 us -> 6.87 us  [the longest x2 6.59 us: logits_of(): pl.pallas_call(logits_kernel, in_specs=[WHOLE] * 7, out_specs=[WHOLE] * (...]
  transfers between devices with their start and end apart: 22 -> 21, of which waited for: 16 -> 15; matrix products, arithmetic and copies ran while one was open for 0% -> 0% of each run, Pallas kernels for 16% -> 16%
where the time goes in v6:
time: 117 us; the launch traced here: 116 us
  waiting for transfers between devices  41.1 us (35%)
  starting transfers between devices  33.1 us (28%)
  Pallas kernels  26.9 us (23%)
  blocking collectives  13.5 us (12%)
    ppermute x12, waiting for transfers between devices, shifted(): return lax.ppermute(array, CHIPS, pairs)  32.2 us
    ppermute x12, starting transfers between devices, shifted(): return lax.ppermute(array, CHIPS, pairs)  22.6 us
    all_to_all x1, blocking collectives, on_device(): column = lax.all_to_all(plane, ('z_lo', 'z_hi'), 0, 0, tiled=True)  13.5 us
    all_to_all x1, starting transfers between devices, on_device(): lax.all_to_all(spread(residual, final_gain), ('z_lo', 'z_hi'), 0, 0, tile...  8.58 us
    all_to_all x1, waiting for transfers between devices, on_device(): lax.all_to_all(spread(residual, final_gain), ('z_lo', 'z_hi'), 0, 0, tile...  8.09 us
    pallas_call x1, Pallas kernels, permute_embedding(): pl.pallas_call(permute_kernel, grid=(PADDED // step,), in_specs=[pl.Block...  7.28 us
    pallas_call x2, Pallas kernels, logits_of(): pl.pallas_call(logits_kernel, in_specs=[WHOLE] * 7, out_specs=[WHOLE] * (...  6.59 us
    pallas_call x3, Pallas kernels, gradient_of(): pl.pallas_call(functools.partial(gradient_kernel, ry, parities), in_specs...  3.58 us
  transfers between devices with their start and end apart: 21, of which 15 were waited for; matrix products, arithmetic and copies ran while one was open for 0% of the time, Pallas kernels for 16%

profile of v6, /device:TPU:32, one launch (start us, length us, event | category | flops | bytes accessed | tf_op | source)
XLA Modules:
  0.0 116.1 jit_solution(4881520794458266011)
XLA Ops:
  0.6 1.5 %spread.1 = bf16[8,80,128]{2,1,0:T(8,128)(2,1)} custom-call(bf16[32,288]{1,0:T(8,128)(2,1)} %refs_6_.1, bf16[288]{0:T(512)(128)(2,1)} %gain_hbm.1), custom_call_target="tpu_custom_call" | custom-call | tf_op jit(solution)/shard_map/spread/pallas_call | solution.py:184
  2.1 8.6 %all-to-all-start.1 = ((bf16[8,80,128]{2,1,0:T(8,128)(2,1)}), bf16[8,80,128]{2,1,0:T(8,128)(2,1)S(1)}, u32[]{:S(2)}, u32[]{:S(2)}) async-start(bf16[8,80,128]{2,1,0:T(8,128)(2,1)} %spread.1), calls=%async_computation.1 | async-start | bytes 327680 | tf_op jit(solution)/shard_map/all_to_all | solution.py:590
  10.7 8.1 %all-to-all-done.1.in_ref = bf16[8,80,128]{2,1,0:T(8,128)(2,1)S(1)} async-done(((bf16[8,80,128]{2,1,0:T(8,128)(2,1)}), bf16[8,80,128]{2,1,0:T(8,128)(2,1)S(1)}, u32[]{:S(2)}, u32[]{:S(2)}) %all-to-all-start.1) | async-done | bytes 163872 | tf_op jit(solution)/shard_map/all_to_all | solution.py:590
  19.0 5.7 %collective-permute-start.3 = (bf16[592,128]{1,0:T(8,128)(2,1)S(1)}, bf16[592,128]{1,0:T(8,128)(2,1)S(1)}, u32[]{:S(2)}, u32[]{:S(2)}) collective-permute-start(bf16[592,128]{1,0:T(8,128)(2,1)S(1)} %pack_tokens.1.refs_0_), channel_id=1, source_target_pairs={{0,36},{2,38},{4,32},{6,34},{8,44},{10,46},{12,40},{14,42},{16,52}... | collective-permute-start | bytes 454664 | tf_op jit(solution)/shard_map/ppermute | solution.py:550
  25.6 1.6 %label_places.1 = (s32[1,256]{1,0:T(1,128)S(1)}, bf16[32,1024]{1,0:T(8,128)(2,1)S(1)}, s32[1,256]{1,0:T(1,128)S(1)}, bf16[32,1024]{1,0:T(8,128)(2,1)S(1)}, bf16[...) custom-call(s32[1,512]{1,0:T(1,128)} %bitcast.35), custom_call_target="tpu_custom_call" | custom-call | flops 2621440 | bytes 1048576 | tf_op jit(solution)/shard_map/label_places/pallas_call | solution.py:107
  28.9 2.5 %collective-permute-done.2.refs_2_ = bf16[592,128]{1,0:T(8,128)(2,1)S(1)} collective-permute-done((bf16[592,128]{1,0:T(8,128)(2,1)S(1)}, bf16[592,128]{1,0:T(8,128)(2,1)S(1)}, u32[]{:S(2)}, u32[]{:S(2)}) %collective-permute-start.2) | collective-permute-done | bytes 151584 | tf_op jit(solution)/shard_map/ppermute | solution.py:550
  31.9 4.2 %collective-permute-start.7 = (bf16[4,592,128]{2,1,0:T(8,128)(2,1)S(1)}, bf16[4,592,128]{2,1,0:T(8,128)(2,1)S(1)}, u32[]{:S(2)}, u32[]{:S(2)}) collective-permute-start(bf16[4,592,128]{2,1,0:T(8,128)(2,1)S(1)} %in_order.1.refs_0_), channel_id=1, source_target_pairs={{0,54},{2,48},{4,50},{6,52},{8,62},{10,56},{12,58},{14,60},{16,6},... | collective-permute-start | bytes 1818632 | tf_op jit(solution)/shard_map/ppermute | solution.py:550
  36.4 7.3 %permute_embedding.1.refs_4_.refs_2_.refs_1_ = bf16[1024,4608]{1,0:T(8,128)(2,1)S(1)} custom-call(bf16[1000,4608]{1,0:T(8,128)(2,1)} %get-tuple-element.414), custom_call_target="tpu_custom_call" | custom-call | bytes 18432000 | tf_op jit(solution)/shard_map/permute_embedding/pallas_call | solution.py:152
  43.8 4.7 %collective-permute-done.7.refs_3_ = bf16[4,592,128]{2,1,0:T(8,128)(2,1)S(1)} collective-permute-done((bf16[4,592,128]{2,1,0:T(8,128)(2,1)S(1)}, bf16[4,592,128]{2,1,0:T(8,128)(2,1)S(1)}, u32[]{:S(2)}, u32[]{:S(2)}) %collective-permute-start.7) | collective-permute-done | bytes 606240 | tf_op jit(solution)/shard_map/ppermute | solution.py:550
  48.5 3.4 %collective-permute-done.6.refs_2_ = bf16[4,592,128]{2,1,0:T(8,128)(2,1)S(1)} collective-permute-done((bf16[4,592,128]{2,1,0:T(8,128)(2,1)S(1)}, bf16[4,592,128]{2,1,0:T(8,128)(2,1)S(1)}, u32[]{:S(2)}, u32[]{:S(2)}) %collective-permute-start.6) | collective-permute-done | bytes 606240 | tf_op jit(solution)/shard_map/ppermute | solution.py:550
  52.4 3.3 %logits.2 = (bf16[144,1024]{1,0:T(8,128)(2,1)S(1)}, bf16[144,1024]{1,0:T(8,128)(2,1)S(1)}, f32[8,256]{1,0:T(8,128)S(1)}, f32[256,128]{1,0:T(8,128)S(1)}) custom-call(bf16[4,592,128]{2,1,0:T(8,128)(2,1)S(1)} %in_order.1.refs_0_, bf16[4,592,128]{2,1,0:T(8,128)(2,1)S(1)} %collective-permute-done.5.refs_1_, ...), custom_call_target="tpu_custom_call" | custom-call | flops 2415919104 | bytes 9437184 | tf_op jit(solution)/shard_map/logits/pallas_call | solution.py:295
  55.8 3.3 %logits.3 = (bf16[144,1024]{1,0:T(8,128)(2,1)S(1)}, bf16[144,1024]{1,0:T(8,128)(2,1)S(1)}, f32[8,256]{1,0:T(8,128)S(1)}) custom-call(bf16[4,592,128]{2,1,0:T(8,128)(2,1)S(1)} %collective-permute-done.4.refs_0_, bf16[4,592,128]{2,1,0:T(8,128)(2,1)S(1)} %collective-permute-done.8.refs_1_, bf16[4,592,128]{2,1,0:T(8,128)(2,1)S(1)} %collective-permute-done.9.refs_2_, ...), custom_call_target="tpu_custom_call" | custom-call | flops 2415919104 | bytes 9437184 | tf_op jit(solution)/shard_map/logits/pallas_call | solution.py:295
  59.1 1.7 %gradient.3 = bf16[8,72,1152]{2,1,0:T(8,128)(2,1)S(1)} custom-call(bf16[144,1024]{1,0:T(8,128)(2,1)S(1)} %get-tuple-element.236.refs_0_, bf16[144,1024]{1,0:T(8,128)(2,1)S(1)} %get-tuple-element.223.refs_1_.refs_0_, bf16[1024,4608]{1,0:T(8,128)(2,1)S(1)} %permute_embedding.1.refs_4_.refs_2_.refs_1_, f32[8,256]{1,0:T(8,128)S(1)} %get-tuple-element.222.refs_3_.refs_2_), custom_call_target="tpu_custom_call" | custom-call | flops 1358954496 | bytes 4718592 | tf_op jit(solution)/shard_map/gradient/pallas_call | solution.py:363
  62.4 1.5 %product.3.term_ref = f32[288,2304]{1,0:T(8,128)S(1)} custom-call(bf16[144,1024]{1,0:T(8,128)(2,1)S(1)} %get-tuple-element.240.refs_0_, bf16[144,1024]{1,0:T(8,128)(2,1)S(1)} %get-tuple-element.232.refs_1_.refs_0_, bf16[1024,4608]{1,0:T(8,128)(2,1)S(1)} %permute_embedding.1.refs_4_.refs_2_.refs_1_), custom_call_target="tpu_custom_call" | custom-call | flops 1358954496 | bytes 4718592 | tf_op jit(solution)/shard_map/product/pallas_call | solution.py:382
  64.6 1.6 %collective-permute-start.16 = (bf16[4,72,1152]{2,1,0:T(8,128)(2,1)S(1)}, bf16[4,72,1152]{2,1,0:T(8,128)(2,1)S(1)}, u32[]{:S(2)}, u32[]{:S(2)}) collective-permute-start(bf16[4,72,1152]{2,1,0:T(8,128)(2,1)S(1)} %get-tuple-element.244), channel_id=1, source_target_pairs={{0,16},{2,18},{4,20},{6,22},{8,24},{10,26},{12,28},{14,30},{16,32}... | collective-permute-start | bytes 1990664 | tf_op jit(solution)/shard_map/ppermute | solution.py:550
  66.2 1.4 %collective-permute-start.17 = (bf16[4,72,1152]{2,1,0:T(8,128)(2,1)S(1)}, bf16[4,72,1152]{2,1,0:T(8,128)(2,1)S(1)}, u32[]{:S(2)}, u32[]{:S(2)}) collective-permute-start(bf16[4,72,1152]{2,1,0:T(8,128)(2,1)S(1)} %get-tuple-element.245), channel_id=1, source_target_pairs={{0,54},{2,48},{4,50},{6,52},{8,62},{10,56},{12,58},{14,60},{16,6},... | collective-permute-start | bytes 1990664 | tf_op jit(solution)/shard_map/ppermute | solution.py:550
  68.7 1.9 %collective-permute-start.15 = (bf16[4,72,1152]{2,1,0:T(8,128)(2,1)S(1)}, bf16[4,72,1152]{2,1,0:T(8,128)(2,1)S(1)}, u32[]{:S(2)}, u32[]{:S(2)}) collective-permute-start(bf16[4,72,1152]{2,1,0:T(8,128)(2,1)S(1)} %combine.4), channel_id=1, source_target_pairs={{0,2},{2,4},{4,6},{6,0},{8,10},{10,12},{12,14},{14,8},{16,18},{18,... | collective-permute-start | bytes 1990664 | tf_op jit(solution)/shard_map/ppermute | solution.py:550
  74.1 9.0 %collective-permute-done.16.refs_2_ = bf16[4,72,1152]{2,1,0:T(8,128)(2,1)S(1)} collective-permute-done((bf16[4,72,1152]{2,1,0:T(8,128)(2,1)S(1)}, bf16[4,72,1152]{2,1,0:T(8,128)(2,1)S(1)}, u32[]{:S(2)}, u32[]{:S(2)}) %collective-permute-start.16) | collective-permute-done | bytes 663584 | tf_op jit(solution)/shard_map/ppermute | solution.py:550
  84.1 2.7 %collective-permute-done.15.refs_1_ = bf16[4,72,1152]{2,1,0:T(8,128)(2,1)S(1)} collective-permute-done((bf16[4,72,1152]{2,1,0:T(8,128)(2,1)S(1)}, bf16[4,72,1152]{2,1,0:T(8,128)(2,1)S(1)}, u32[]{:S(2)}, u32[]{:S(2)}) %collective-permute-start.15) | collective-permute-done | bytes 663584 | tf_op jit(solution)/shard_map/ppermute | solution.py:550
  87.2 1.2 %collective-permute-start.18 = (bf16[96,1152]{1,0:T(8,128)(2,1)S(1)}, bf16[96,1152]{1,0:T(8,128)(2,1)S(1)}, u32[]{:S(2)}, u32[]{:S(2)}) collective-permute-start(bf16[96,1152]{1,0:T(8,128)(2,1)S(1)} %get-tuple-element.247), channel_id=1, source_target_pairs={{0,4},{2,6},{4,0},{6,2},{8,12},{10,14},{12,8},{14,10},{16,20},{18,... | collective-permute-start | bytes 663560 | tf_op jit(solution)/shard_map/ppermute | solution.py:550
  89.1 4.7 %collective-permute-start.20 = (bf16[96,1152]{1,0:T(8,128)(2,1)S(1)}, bf16[96,1152]{1,0:T(8,128)(2,1)S(1)}, u32[]{:S(2)}, u32[]{:S(2)}) collective-permute-start(bf16[96,1152]{1,0:T(8,128)(2,1)S(1)} %get-tuple-element.249), channel_id=1, source_target_pairs={{0,36},{2,38},{4,32},{6,34},{8,44},{10,46},{12,40},{14,42},{16,52}... | collective-permute-start | bytes 663560 | tf_op jit(solution)/shard_map/ppermute | solution.py:550
  93.8 2.5 %collective-permute-done.18.refs_1_ = bf16[96,1152]{1,0:T(8,128)(2,1)S(1)} collective-permute-done((bf16[96,1152]{1,0:T(8,128)(2,1)S(1)}, bf16[96,1152]{1,0:T(8,128)(2,1)S(1)}, u32[]{:S(2)}, u32[]{:S(2)}) %collective-permute-start.18) | collective-permute-done | bytes 221216 | tf_op jit(solution)/shard_map/ppermute | solution.py:550
  97.3 4.0 %collective-permute-done.20.refs_3_ = bf16[96,1152]{1,0:T(8,128)(2,1)S(1)} collective-permute-done((bf16[96,1152]{1,0:T(8,128)(2,1)S(1)}, bf16[96,1152]{1,0:T(8,128)(2,1)S(1)}, u32[]{:S(2)}, u32[]{:S(2)}) %collective-permute-start.20) | collective-permute-done | bytes 221216 | tf_op jit(solution)/shard_map/ppermute | solution.py:550
  101.6 13.5 %all_to_all.20.in_ref = bf16[8,32,640]{2,1,0:T(8,128)(2,1)S(1)} all-to-all(bf16[8,32,640]{2,1,0:T(8,128)(2,1)S(1)} %get-tuple-element.253), channel_id=1, replica_groups=mesh['z_lo'=4,'y1'=2,'y0'=2,'z_hi'=2,'x1'=2,'x0'=2,'core'=2] {'z_lo','z_..., dimensions={0} | all-to-all | bytes 655360 | tf_op jit(solution)/shard_map/all_to_all | solution.py:620
  (47 shorter events, 15.3 us)
Async XLA Ops:
  2.1 16.7 %all-to-all-start.1 = ((bf16[8,80,128]{2,1,0:T(8,128)(2,1)}), bf16[8,80,128]{2,1,0:T(8,128)(2,1)S(1)}, u32[]{:S(2)}, u32[]{:S(2)}) async-start(bf16[8,80,128]{2,1,0:T(8,128)(2,1)} %spread.1), calls=%async_computation.1 | async-start | bytes 327680 | tf_op jit(solution)/shard_map/all_to_all | solution.py:590
  19.0 9.9 %collective-permute-start.3 = (bf16[592,128]{1,0:T(8,128)(2,1)S(1)}, bf16[592,128]{1,0:T(8,128)(2,1)S(1)}, u32[]{:S(2)}, u32[]{:S(2)}) collective-permute-start(bf16[592,128]{1,0:T(8,128)(2,1)S(1)} %pack_tokens.1.refs_0_), channel_id=1, source_target_pairs={{0,36},{2,38},{4,32},{6,34},{8,44},{10,46},{12,40},{14,42},{16,52}... | collective-permute-start | bytes 454664 | tf_op jit(solution)/shard_map/ppermute | solution.py:550
  24.8 6.7 %collective-permute-start.2 = (bf16[592,128]{1,0:T(8,128)(2,1)S(1)}, bf16[592,128]{1,0:T(8,128)(2,1)S(1)}, u32[]{:S(2)}, u32[]{:S(2)}) collective-permute-start(bf16[592,128]{1,0:T(8,128)(2,1)S(1)} %pack_tokens.1.refs_0_), channel_id=1, source_target_pairs={{0,32},{2,34},{4,36},{6,38},{8,40},{10,42},{12,44},{14,46},{16,48}... | collective-permute-start | bytes 454664 | tf_op jit(solution)/shard_map/ppermute | solution.py:550
  25.1 6.7 %collective-permute-start.1 = (bf16[592,128]{1,0:T(8,128)(2,1)S(1)}, bf16[592,128]{1,0:T(8,128)(2,1)S(1)}, u32[]{:S(2)}, u32[]{:S(2)}) collective-permute-start(bf16[592,128]{1,0:T(8,128)(2,1)S(1)} %pack_tokens.1.refs_0_), channel_id=1, source_target_pairs={{0,4},{2,6},{4,0},{6,2},{8,12},{10,14},{12,8},{14,10},{16,20},{18,... | collective-permute-start | bytes 454664 | tf_op jit(solution)/shard_map/ppermute | solution.py:550
  31.9 16.6 %collective-permute-start.7 = (bf16[4,592,128]{2,1,0:T(8,128)(2,1)S(1)}, bf16[4,592,128]{2,1,0:T(8,128)(2,1)S(1)}, u32[]{:S(2)}, u32[]{:S(2)}) collective-permute-start(bf16[4,592,128]{2,1,0:T(8,128)(2,1)S(1)} %in_order.1.refs_0_), channel_id=1, source_target_pairs={{0,54},{2,48},{4,50},{6,52},{8,62},{10,56},{12,58},{14,60},{16,6},... | collective-permute-start | bytes 1818632 | tf_op jit(solution)/shard_map/ppermute | solution.py:550
  36.0 15.9 %collective-permute-start.6 = (bf16[4,592,128]{2,1,0:T(8,128)(2,1)S(1)}, bf16[4,592,128]{2,1,0:T(8,128)(2,1)S(1)}, u32[]{:S(2)}, u32[]{:S(2)}) collective-permute-start(bf16[4,592,128]{2,1,0:T(8,128)(2,1)S(1)} %in_order.1.refs_0_), channel_id=1, source_target_pairs={{0,16},{2,18},{4,20},{6,22},{8,24},{10,26},{12,28},{14,30},{16,32}... | collective-permute-start | bytes 1818632 | tf_op jit(solution)/shard_map/ppermute | solution.py:550
  36.0 15.9 %collective-permute-start.5 = (bf16[4,592,128]{2,1,0:T(8,128)(2,1)S(1)}, bf16[4,592,128]{2,1,0:T(8,128)(2,1)S(1)}, u32[]{:S(2)}, u32[]{:S(2)}) collective-permute-start(bf16[4,592,128]{2,1,0:T(8,128)(2,1)S(1)} %in_order.1.refs_0_), channel_id=1, source_target_pairs={{0,2},{2,4},{4,6},{6,0},{8,10},{10,12},{12,14},{14,8},{16,18},{18,... | collective-permute-start | bytes 1818632 | tf_op jit(solution)/shard_map/ppermute | solution.py:550
  43.7 12.0 %collective-permute-start.4 = (bf16[4,592,128]{2,1,0:T(8,128)(2,1)S(1)}, bf16[4,592,128]{2,1,0:T(8,128)(2,1)S(1)}, u32[]{:S(2)}, u32[]{:S(2)}) collective-permute-start(bf16[4,592,128]{2,1,0:T(8,128)(2,1)S(1)} %in_order.1.refs_0_), channel_id=1, source_target_pairs={{0,1},{1,0},{2,3},{3,2},{4,5},{5,4},{6,7},{7,6},{8,9},{9,8},{10,11... | collective-permute-start | bytes 1818632 | tf_op jit(solution)/shard_map/ppermute | solution.py:542
  51.9 3.8 %collective-permute-start.8 = (bf16[4,592,128]{2,1,0:T(8,128)(2,1)S(1)}, bf16[4,592,128]{2,1,0:T(8,128)(2,1)S(1)}, u32[]{:S(2)}, u32[]{:S(2)}) collective-permute-start(bf16[4,592,128]{2,1,0:T(8,128)(2,1)S(1)} %collective-permute-done.5.refs_1_), channel_id=1, source_target_pairs={{0,1},{1,0},{2,3},{3,2},{4,5},{5,4},{6,7},{7,6},{8,9},{9,8},{10,11... | collective-permute-start | bytes 1818632 | tf_op jit(solution)/shard_map/ppermute | solution.py:542
  51.9 3.8 %collective-permute-start.9 = (bf16[4,592,128]{2,1,0:T(8,128)(2,1)S(1)}, bf16[4,592,128]{2,1,0:T(8,128)(2,1)S(1)}, u32[]{:S(2)}, u32[]{:S(2)}) collective-permute-start(bf16[4,592,128]{2,1,0:T(8,128)(2,1)S(1)} %collective-permute-done.6.refs_2_), channel_id=1, source_target_pairs={{0,1},{1,0},{2,3},{3,2},{4,5},{5,4},{6,7},{7,6},{8,9},{9,8},{10,11... | collective-permute-start | bytes 1818632 | tf_op jit(solution)/shard_map/ppermute | solution.py:542
  52.4 3.3 %collective-permute-start.10 = (bf16[4,592,128]{2,1,0:T(8,128)(2,1)S(1)}, bf16[4,592,128]{2,1,0:T(8,128)(2,1)S(1)}, u32[]{:S(2)}, u32[]{:S(2)}) collective-permute-start(bf16[4,592,128]{2,1,0:T(8,128)(2,1)S(1)} %collective-permute-done.7.refs_3_), channel_id=1, source_target_pairs={{0,1},{1,0},{2,3},{3,2},{4,5},{5,4},{6,7},{7,6},{8,9},{9,8},{10,11... | collective-permute-start | bytes 1818632 | tf_op jit(solution)/shard_map/ppermute | solution.py:542
  60.8 3.3 %collective-permute-start.11 = (bf16[8,72,1152]{2,1,0:T(8,128)(2,1)S(1)}, bf16[8,72,1152]{2,1,0:T(8,128)(2,1)S(1)}, u32[]{:S(2)}, u32[]{:S(2)}) collective-permute-start(bf16[8,72,1152]{2,1,0:T(8,128)(2,1)S(1)} %gradient.3), channel_id=1, source_target_pairs={{0,1},{1,0},{2,3},{3,2},{4,5},{5,4},{6,7},{7,6},{8,9},{9,8},{10,11... | collective-permute-start | bytes 3981320 | tf_op jit(solution)/shard_map/ppermute | solution.py:542
  62.3 6.1 %collective-permute-start.12 = (bf16[4,72,1152]{2,1,0:T(8,128)(2,1)S(1)}, bf16[4,72,1152]{2,1,0:T(8,128)(2,1)S(1)}, u32[]{:S(2)}, u32[]{:S(2)}) collective-permute-start(bf16[4,72,1152]{2,1,0:T(8,128)(2,1)S(1)} %gradient.4), channel_id=1, source_target_pairs={{0,1},{1,0},{2,3},{3,2},{4,5},{5,4},{6,7},{7,6},{8,9},{9,8},{10,11... | collective-permute-start | bytes 1990664 | tf_op jit(solution)/shard_map/ppermute | solution.py:542
  64.6 18.5 %collective-permute-start.16 = (bf16[4,72,1152]{2,1,0:T(8,128)(2,1)S(1)}, bf16[4,72,1152]{2,1,0:T(8,128)(2,1)S(1)}, u32[]{:S(2)}, u32[]{:S(2)}) collective-permute-start(bf16[4,72,1152]{2,1,0:T(8,128)(2,1)S(1)} %get-tuple-element.244), channel_id=1, source_target_pairs={{0,16},{2,18},{4,20},{6,22},{8,24},{10,26},{12,28},{14,30},{16,32}... | collective-permute-start | bytes 1990664 | tf_op jit(solution)/shard_map/ppermute | solution.py:550
  66.2 17.9 %collective-permute-start.17 = (bf16[4,72,1152]{2,1,0:T(8,128)(2,1)S(1)}, bf16[4,72,1152]{2,1,0:T(8,128)(2,1)S(1)}, u32[]{:S(2)}, u32[]{:S(2)}) collective-permute-start(bf16[4,72,1152]{2,1,0:T(8,128)(2,1)S(1)} %get-tuple-element.245), channel_id=1, source_target_pairs={{0,54},{2,48},{4,50},{6,52},{8,62},{10,56},{12,58},{14,60},{16,6},... | collective-permute-start | bytes 1990664 | tf_op jit(solution)/shard_map/ppermute | solution.py:550
  68.7 18.1 %collective-permute-start.15 = (bf16[4,72,1152]{2,1,0:T(8,128)(2,1)S(1)}, bf16[4,72,1152]{2,1,0:T(8,128)(2,1)S(1)}, u32[]{:S(2)}, u32[]{:S(2)}) collective-permute-start(bf16[4,72,1152]{2,1,0:T(8,128)(2,1)S(1)} %combine.4), channel_id=1, source_target_pairs={{0,2},{2,4},{4,6},{6,0},{8,10},{10,12},{12,14},{14,8},{16,18},{18,... | collective-permute-start | bytes 1990664 | tf_op jit(solution)/shard_map/ppermute | solution.py:550
  71.6 1.7 %collective-permute-start.13 = (bf16[2,72,1152]{2,1,0:T(8,128)(2,1)S(1)}, bf16[2,72,1152]{2,1,0:T(8,128)(2,1)S(1)}, u32[]{:S(2)}, u32[]{:S(2)}) collective-permute-start(bf16[2,72,1152]{2,1,0:T(8,128)(2,1)S(1)} %get-tuple-element.241), channel_id=1, source_target_pairs={{0,1},{1,0},{2,3},{3,2},{4,5},{5,4},{6,7},{7,6},{8,9},{9,8},{10,11... | collective-permute-start | bytes 995336 | tf_op jit(solution)/shard_map/ppermute | solution.py:542
  71.7 2.1 %collective-permute-start.14 = (bf16[2,72,1152]{2,1,0:T(8,128)(2,1)S(1)}, bf16[2,72,1152]{2,1,0:T(8,128)(2,1)S(1)}, u32[]{:S(2)}, u32[]{:S(2)}) collective-permute-start(bf16[2,72,1152]{2,1,0:T(8,128)(2,1)S(1)} %get-tuple-element.242), channel_id=1, source_target_pairs={{0,1},{1,0},{2,3},{3,2},{4,5},{5,4},{6,7},{7,6},{8,9},{9,8},{10,11... | collective-permute-start | bytes 995336 | tf_op jit(solution)/shard_map/ppermute | solution.py:542
  73.1 20.7 %copy-start.2 = (bf16[288]{0:T(512)(128)(2,1)S(1)}, bf16[288]{0:T(512)(128)(2,1)}, u32[]{:S(2)}) copy-start(bf16[288]{0:T(512)(128)(2,1)} %gain_hbm.1) | copy-start | bytes 1732
  73.1 28.3 %copy-start = (bf16[32,288]{1,0:T(8,128)(2,1)S(1)}, bf16[32,288]{1,0:T(8,128)(2,1)}, u32[]{:S(2)}) copy-start(bf16[32,288]{1,0:T(8,128)(2,1)} %refs_6_.1) | copy-start | bytes 55300
  73.1 28.3 %copy-start.1 = (f32[512]{0:T(512)S(1)}, f32[512]{0:T(512)}, u32[]{:S(2)}) copy-start(f32[512]{0:T(512)} %param.11) | copy-start | bytes 6148
  87.2 9.1 %collective-permute-start.18 = (bf16[96,1152]{1,0:T(8,128)(2,1)S(1)}, bf16[96,1152]{1,0:T(8,128)(2,1)S(1)}, u32[]{:S(2)}, u32[]{:S(2)}) collective-permute-start(bf16[96,1152]{1,0:T(8,128)(2,1)S(1)} %get-tuple-element.247), channel_id=1, source_target_pairs={{0,4},{2,6},{4,0},{6,2},{8,12},{10,14},{12,8},{14,10},{16,20},{18,... | collective-permute-start | bytes 663560 | tf_op jit(solution)/shard_map/ppermute | solution.py:550
  88.4 8.9 %collective-permute-start.19 = (bf16[96,1152]{1,0:T(8,128)(2,1)S(1)}, bf16[96,1152]{1,0:T(8,128)(2,1)S(1)}, u32[]{:S(2)}, u32[]{:S(2)}) collective-permute-start(bf16[96,1152]{1,0:T(8,128)(2,1)S(1)} %get-tuple-element.248), channel_id=1, source_target_pairs={{0,32},{2,34},{4,36},{6,38},{8,40},{10,42},{12,44},{14,46},{16,48}... | collective-permute-start | bytes 663560 | tf_op jit(solution)/shard_map/ppermute | solution.py:550
  89.1 12.2 %collective-permute-start.20 = (bf16[96,1152]{1,0:T(8,128)(2,1)S(1)}, bf16[96,1152]{1,0:T(8,128)(2,1)S(1)}, u32[]{:S(2)}, u32[]{:S(2)}) collective-permute-start(bf16[96,1152]{1,0:T(8,128)(2,1)S(1)} %get-tuple-element.249), channel_id=1, source_target_pairs={{0,36},{2,38},{4,32},{6,34},{8,44},{10,46},{12,40},{14,42},{16,52}... | collective-permute-start | bytes 663560 | tf_op jit(solution)/shard_map/ppermute | solution.py:550

commit v7 on v6

--- a/solution.py
+++ b/solution.py
@@ -598,7 +598,7 @@
     packed = in_order([piece] + moved)
     table = permute_embedding(embedding)
     blocks = [packed] + [shifted(packed, *SHIFTS[parity]) for parity in PLACES[1:]]
-    blocks[1:], table = lax.optimization_barrier((blocks[1:], table))
+    blocks[1], table = lax.optimization_barrier((blocks[1], table))
     other_blocks = [swap_cores(block) for block in blocks]
 
     *e, stats, scale = logits_of(blocks, table, own_labels, own_slots, True)

time: 117 us -> 117 us (level)
    ppermute x12, starting transfers between devices: 22.6 us -> 23.8 us  [shifted(): return lax.ppermute(array, CHIPS, pairs)]
  transfers between devices with their start and end apart: 21 -> 21, of which waited for: 15 -> 13; matrix products, arithmetic and copies ran while one was open for 0% -> 0% of each run, Pallas kernels for 16% -> 16%
where the time goes in v7:
time: 117 us; the launch traced here: 116 us
  waiting for transfers between devices  40 us (34%)
  starting transfers between devices  34.2 us (29%)
  Pallas kernels  26.9 us (23%)
  blocking collectives  13.3 us (11%)
    ppermute x12, waiting for transfers between devices, shifted(): return lax.ppermute(array, CHIPS, pairs)  31.2 us
    ppermute x12, starting transfers between devices, shifted(): return lax.ppermute(array, CHIPS, pairs)  23.8 us
    all_to_all x1, blocking collectives, on_device(): column = lax.all_to_all(plane, ('z_lo', 'z_hi'), 0, 0, tiled=True)  13.3 us
    all_to_all x1, starting transfers between devices, on_device(): lax.all_to_all(spread(residual, final_gain), ('z_lo', 'z_hi'), 0, 0, tile...  8.58 us
    all_to_all x1, waiting for transfers between devices, on_device(): lax.all_to_all(spread(residual, final_gain), ('z_lo', 'z_hi'), 0, 0, tile...  8.09 us
    pallas_call x1, Pallas kernels, permute_embedding(): pl.pallas_call(permute_kernel, grid=(PADDED // step,), in_specs=[pl.Block...  7.28 us
    pallas_call x2, Pallas kernels, logits_of(): pl.pallas_call(logits_kernel, in_specs=[WHOLE] * 7, out_specs=[WHOLE] * (...  6.59 us
    pallas_call x3, Pallas kernels, gradient_of(): pl.pallas_call(functools.partial(gradient_kernel, ry, parities), in_specs...  3.58 us
  transfers between devices with their start and end apart: 21, of which 13 were waited for; matrix products, arithmetic and copies ran while one was open for 0% of the time, Pallas kernels for 16%

profile of v7, /device:TPU:32, one launch (start us, length us, event | category | flops | bytes accessed | tf_op | source)
XLA Modules:
  0.0 116.0 jit_solution(15171649603091021428)
XLA Ops:
  0.6 1.5 %spread.1 = bf16[8,80,128]{2,1,0:T(8,128)(2,1)} custom-call(bf16[32,288]{1,0:T(8,128)(2,1)} %refs_6_.1, bf16[288]{0:T(512)(128)(2,1)} %gain_hbm.1), custom_call_target="tpu_custom_call" | custom-call | tf_op jit(solution)/shard_map/spread/pallas_call | solution.py:184
  2.1 8.6 %all-to-all-start.1 = ((bf16[8,80,128]{2,1,0:T(8,128)(2,1)}), bf16[8,80,128]{2,1,0:T(8,128)(2,1)S(1)}, u32[]{:S(2)}, u32[]{:S(2)}) async-start(bf16[8,80,128]{2,1,0:T(8,128)(2,1)} %spread.1), calls=%async_computation.1 | async-start | bytes 327680 | tf_op jit(solution)/shard_map/all_to_all | solution.py:590
  10.7 8.1 %all-to-all-done.1.in_ref = bf16[8,80,128]{2,1,0:T(8,128)(2,1)S(1)} async-done(((bf16[8,80,128]{2,1,0:T(8,128)(2,1)}), bf16[8,80,128]{2,1,0:T(8,128)(2,1)S(1)}, u32[]{:S(2)}, u32[]{:S(2)}) %all-to-all-start.1) | async-done | bytes 163872 | tf_op jit(solution)/shard_map/all_to_all | solution.py:590
  19.0 5.7 %collective-permute-start.3 = (bf16[592,128]{1,0:T(8,128)(2,1)S(1)}, bf16[592,128]{1,0:T(8,128)(2,1)S(1)}, u32[]{:S(2)}, u32[]{:S(2)}) collective-permute-start(bf16[592,128]{1,0:T(8,128)(2,1)S(1)} %pack_tokens.1.refs_0_), channel_id=1, source_target_pairs={{0,36},{2,38},{4,32},{6,34},{8,44},{10,46},{12,40},{14,42},{16,52}... | collective-permute-start | bytes 454664 | tf_op jit(solution)/shard_map/ppermute | solution.py:550
  25.6 1.6 %label_places.1 = (s32[1,256]{1,0:T(1,128)S(1)}, bf16[32,1024]{1,0:T(8,128)(2,1)S(1)}, s32[1,256]{1,0:T(1,128)S(1)}, bf16[32,1024]{1,0:T(8,128)(2,1)S(1)}, bf16[...) custom-call(s32[1,512]{1,0:T(1,128)} %bitcast.35), custom_call_target="tpu_custom_call" | custom-call | flops 2621440 | bytes 1048576 | tf_op jit(solution)/shard_map/label_places/pallas_call | solution.py:107
  28.9 2.5 %collective-permute-done.2.refs_2_ = bf16[592,128]{1,0:T(8,128)(2,1)S(1)} collective-permute-done((bf16[592,128]{1,0:T(8,128)(2,1)S(1)}, bf16[592,128]{1,0:T(8,128)(2,1)S(1)}, u32[]{:S(2)}, u32[]{:S(2)}) %collective-permute-start.2) | collective-permute-done | bytes 151584 | tf_op jit(solution)/shard_map/ppermute | solution.py:550
  31.9 1.5 %collective-permute-start.5 = (bf16[4,592,128]{2,1,0:T(8,128)(2,1)S(1)}, bf16[4,592,128]{2,1,0:T(8,128)(2,1)S(1)}, u32[]{:S(2)}, u32[]{:S(2)}) collective-permute-start(bf16[4,592,128]{2,1,0:T(8,128)(2,1)S(1)} %in_order.1.refs_0_), channel_id=1, source_target_pairs={{0,2},{2,4},{4,6},{6,0},{8,10},{10,12},{12,14},{14,8},{16,18},{18,... | collective-permute-start | bytes 1818632 | tf_op jit(solution)/shard_map/ppermute | solution.py:550
  33.3 4.3 %collective-permute-start.9 = (bf16[4,592,128]{2,1,0:T(8,128)(2,1)S(1)}, bf16[4,592,128]{2,1,0:T(8,128)(2,1)S(1)}, u32[]{:S(2)}, u32[]{:S(2)}) collective-permute-start(bf16[4,592,128]{2,1,0:T(8,128)(2,1)S(1)} %in_order.1.refs_0_), channel_id=1, source_target_pairs={{0,54},{2,48},{4,50},{6,52},{8,62},{10,56},{12,58},{14,60},{16,6},... | collective-permute-start | bytes 1818632 | tf_op jit(solution)/shard_map/ppermute | solution.py:550
  37.6 7.3 %permute_embedding.1.refs_4_.refs_2_.refs_1_ = bf16[1024,4608]{1,0:T(8,128)(2,1)S(1)} custom-call(bf16[1000,4608]{1,0:T(8,128)(2,1)} %get-tuple-element.410), custom_call_target="tpu_custom_call" | custom-call | bytes 18432000 | tf_op jit(solution)/shard_map/permute_embedding/pallas_call | solution.py:152
  45.0 2.9 %collective-permute-done.5.refs_1_ = bf16[4,592,128]{2,1,0:T(8,128)(2,1)S(1)} collective-permute-done((bf16[4,592,128]{2,1,0:T(8,128)(2,1)S(1)}, bf16[4,592,128]{2,1,0:T(8,128)(2,1)S(1)}, u32[]{:S(2)}, u32[]{:S(2)}) %collective-permute-start.5) | collective-permute-done | bytes 606240 | tf_op jit(solution)/shard_map/ppermute | solution.py:550
  48.0 1.9 %collective-permute-done.9.refs_3_ = bf16[4,592,128]{2,1,0:T(8,128)(2,1)S(1)} collective-permute-done((bf16[4,592,128]{2,1,0:T(8,128)(2,1)S(1)}, bf16[4,592,128]{2,1,0:T(8,128)(2,1)S(1)}, u32[]{:S(2)}, u32[]{:S(2)}) %collective-permute-start.9) | collective-permute-done | bytes 606240 | tf_op jit(solution)/shard_map/ppermute | solution.py:550
  49.9 3.4 %collective-permute-done.7.refs_2_ = bf16[4,592,128]{2,1,0:T(8,128)(2,1)S(1)} collective-permute-done((bf16[4,592,128]{2,1,0:T(8,128)(2,1)S(1)}, bf16[4,592,128]{2,1,0:T(8,128)(2,1)S(1)}, u32[]{:S(2)}, u32[]{:S(2)}) %collective-permute-start.7) | collective-permute-done | bytes 606240 | tf_op jit(solution)/shard_map/ppermute | solution.py:550
  53.8 3.3 %logits.2 = (bf16[144,1024]{1,0:T(8,128)(2,1)S(1)}, bf16[144,1024]{1,0:T(8,128)(2,1)S(1)}, f32[8,256]{1,0:T(8,128)S(1)}, f32[256,128]{1,0:T(8,128)S(1)}) custom-call(bf16[4,592,128]{2,1,0:T(8,128)(2,1)S(1)} %in_order.1.refs_0_, bf16[4,592,128]{2,1,0:T(8,128)(2,1)S(1)} %collective-permute-done.5.refs_1_, ...), custom_call_target="tpu_custom_call" | custom-call | flops 2415919104 | bytes 9437184 | tf_op jit(solution)/shard_map/logits/pallas_call | solution.py:295
  57.2 3.3 %logits.3 = (bf16[144,1024]{1,0:T(8,128)(2,1)S(1)}, bf16[144,1024]{1,0:T(8,128)(2,1)S(1)}, f32[8,256]{1,0:T(8,128)S(1)}) custom-call(bf16[4,592,128]{2,1,0:T(8,128)(2,1)S(1)} %collective-permute-done.4.refs_0_, bf16[4,592,128]{2,1,0:T(8,128)(2,1)S(1)} %collective-permute-done.6.refs_1_, bf16[4,592,128]{2,1,0:T(8,128)(2,1)S(1)} %collective-permute-done.8.refs_2_, ...), custom_call_target="tpu_custom_call" | custom-call | flops 2415919104 | bytes 9437184 | tf_op jit(solution)/shard_map/logits/pallas_call | solution.py:295
  60.4 1.7 %gradient.3 = bf16[8,72,1152]{2,1,0:T(8,128)(2,1)S(1)} custom-call(bf16[144,1024]{1,0:T(8,128)(2,1)S(1)} %get-tuple-element.232.refs_0_, bf16[144,1024]{1,0:T(8,128)(2,1)S(1)} %get-tuple-element.219.refs_1_.refs_0_, bf16[1024,4608]{1,0:T(8,128)(2,1)S(1)} %permute_embedding.1.refs_4_.refs_2_.refs_1_, f32[8,256]{1,0:T(8,128)S(1)} %get-tuple-element.218.refs_3_.refs_2_), custom_call_target="tpu_custom_call" | custom-call | flops 1358954496 | bytes 4718592 | tf_op jit(solution)/shard_map/gradient/pallas_call | solution.py:363
  63.8 1.5 %product.3.term_ref = f32[288,2304]{1,0:T(8,128)S(1)} custom-call(bf16[144,1024]{1,0:T(8,128)(2,1)S(1)} %get-tuple-element.236.refs_0_, bf16[144,1024]{1,0:T(8,128)(2,1)S(1)} %get-tuple-element.228.refs_1_.refs_0_, bf16[1024,4608]{1,0:T(8,128)(2,1)S(1)} %permute_embedding.1.refs_4_.refs_2_.refs_1_), custom_call_target="tpu_custom_call" | custom-call | flops 1358954496 | bytes 4718592 | tf_op jit(solution)/shard_map/product/pallas_call | solution.py:382
  66.0 3.0 %collective-permute-start.17 = (bf16[4,72,1152]{2,1,0:T(8,128)(2,1)S(1)}, bf16[4,72,1152]{2,1,0:T(8,128)(2,1)S(1)}, u32[]{:S(2)}, u32[]{:S(2)}) collective-permute-start(bf16[4,72,1152]{2,1,0:T(8,128)(2,1)S(1)} %get-tuple-element.241), channel_id=1, source_target_pairs={{0,54},{2,48},{4,50},{6,52},{8,62},{10,56},{12,58},{14,60},{16,6},... | collective-permute-start | bytes 1990664 | tf_op jit(solution)/shard_map/ppermute | solution.py:550
  70.2 1.8 %collective-permute-start.15 = (bf16[4,72,1152]{2,1,0:T(8,128)(2,1)S(1)}, bf16[4,72,1152]{2,1,0:T(8,128)(2,1)S(1)}, u32[]{:S(2)}, u32[]{:S(2)}) collective-permute-start(bf16[4,72,1152]{2,1,0:T(8,128)(2,1)S(1)} %combine.4), channel_id=1, source_target_pairs={{0,2},{2,4},{4,6},{6,0},{8,10},{10,12},{12,14},{14,8},{16,18},{18,... | collective-permute-start | bytes 1990664 | tf_op jit(solution)/shard_map/ppermute | solution.py:550
  75.4 8.7 %collective-permute-done.16.refs_2_ = bf16[4,72,1152]{2,1,0:T(8,128)(2,1)S(1)} collective-permute-done((bf16[4,72,1152]{2,1,0:T(8,128)(2,1)S(1)}, bf16[4,72,1152]{2,1,0:T(8,128)(2,1)S(1)}, u32[]{:S(2)}, u32[]{:S(2)}) %collective-permute-start.16) | collective-permute-done | bytes 663584 | tf_op jit(solution)/shard_map/ppermute | solution.py:550
  84.1 4.1 %collective-permute-done.15.refs_1_ = bf16[4,72,1152]{2,1,0:T(8,128)(2,1)S(1)} collective-permute-done((bf16[4,72,1152]{2,1,0:T(8,128)(2,1)S(1)}, bf16[4,72,1152]{2,1,0:T(8,128)(2,1)S(1)}, u32[]{:S(2)}, u32[]{:S(2)}) %collective-permute-start.15) | collective-permute-done | bytes 663584 | tf_op jit(solution)/shard_map/ppermute | solution.py:550
  89.2 6.0 %collective-permute-start.20 = (bf16[96,1152]{1,0:T(8,128)(2,1)S(1)}, bf16[96,1152]{1,0:T(8,128)(2,1)S(1)}, u32[]{:S(2)}, u32[]{:S(2)}) collective-permute-start(bf16[96,1152]{1,0:T(8,128)(2,1)S(1)} %get-tuple-element.245), channel_id=1, source_target_pairs={{0,36},{2,38},{4,32},{6,34},{8,44},{10,46},{12,40},{14,42},{16,52}... | collective-permute-start | bytes 663560 | tf_op jit(solution)/shard_map/ppermute | solution.py:550
  95.2 3.3 %collective-permute-done.18.refs_1_ = bf16[96,1152]{1,0:T(8,128)(2,1)S(1)} collective-permute-done((bf16[96,1152]{1,0:T(8,128)(2,1)S(1)}, bf16[96,1152]{1,0:T(8,128)(2,1)S(1)}, u32[]{:S(2)}, u32[]{:S(2)}) %collective-permute-start.18) | collective-permute-done | bytes 221216 | tf_op jit(solution)/shard_map/ppermute | solution.py:550
  98.5 2.9 %collective-permute-done.19.refs_2_ = bf16[96,1152]{1,0:T(8,128)(2,1)S(1)} collective-permute-done((bf16[96,1152]{1,0:T(8,128)(2,1)S(1)}, bf16[96,1152]{1,0:T(8,128)(2,1)S(1)}, u32[]{:S(2)}, u32[]{:S(2)}) %collective-permute-start.19) | collective-permute-done | bytes 221216 | tf_op jit(solution)/shard_map/ppermute | solution.py:550
  101.7 13.3 %all_to_all.20.in_ref = bf16[8,32,640]{2,1,0:T(8,128)(2,1)S(1)} all-to-all(bf16[8,32,640]{2,1,0:T(8,128)(2,1)S(1)} %get-tuple-element.249), channel_id=1, replica_groups=mesh['z_lo'=4,'y1'=2,'y0'=2,'z_hi'=2,'x1'=2,'x0'=2,'core'=2] {'z_lo','z_..., dimensions={0} | all-to-all | bytes 655360 | tf_op jit(solution)/shard_map/all_to_all | solution.py:620
  (47 shorter events, 12.8 us)
Async XLA Ops:
  2.1 16.7 %all-to-all-start.1 = ((bf16[8,80,128]{2,1,0:T(8,128)(2,1)}), bf16[8,80,128]{2,1,0:T(8,128)(2,1)S(1)}, u32[]{:S(2)}, u32[]{:S(2)}) async-start(bf16[8,80,128]{2,1,0:T(8,128)(2,1)} %spread.1), calls=%async_computation.1 | async-start | bytes 327680 | tf_op jit(solution)/shard_map/all_to_all | solution.py:590
  19.0 9.9 %collective-permute-start.3 = (bf16[592,128]{1,0:T(8,128)(2,1)S(1)}, bf16[592,128]{1,0:T(8,128)(2,1)S(1)}, u32[]{:S(2)}, u32[]{:S(2)}) collective-permute-start(bf16[592,128]{1,0:T(8,128)(2,1)S(1)} %pack_tokens.1.refs_0_), channel_id=1, source_target_pairs={{0,36},{2,38},{4,32},{6,34},{8,44},{10,46},{12,40},{14,42},{16,52}... | collective-permute-start | bytes 454664 | tf_op jit(solution)/shard_map/ppermute | solution.py:550
  24.8 6.7 %collective-permute-start.2 = (bf16[592,128]{1,0:T(8,128)(2,1)S(1)}, bf16[592,128]{1,0:T(8,128)(2,1)S(1)}, u32[]{:S(2)}, u32[]{:S(2)}) collective-permute-start(bf16[592,128]{1,0:T(8,128)(2,1)S(1)} %pack_tokens.1.refs_0_), channel_id=1, source_target_pairs={{0,32},{2,34},{4,36},{6,38},{8,40},{10,42},{12,44},{14,46},{16,48}... | collective-permute-start | bytes 454664 | tf_op jit(solution)/shard_map/ppermute | solution.py:550
  25.1 6.7 %collective-permute-start.1 = (bf16[592,128]{1,0:T(8,128)(2,1)S(1)}, bf16[592,128]{1,0:T(8,128)(2,1)S(1)}, u32[]{:S(2)}, u32[]{:S(2)}) collective-permute-start(bf16[592,128]{1,0:T(8,128)(2,1)S(1)} %pack_tokens.1.refs_0_), channel_id=1, source_target_pairs={{0,4},{2,6},{4,0},{6,2},{8,12},{10,14},{12,8},{14,10},{16,20},{18,... | collective-permute-start | bytes 454664 | tf_op jit(solution)/shard_map/ppermute | solution.py:550
  31.9 16.1 %collective-permute-start.5 = (bf16[4,592,128]{2,1,0:T(8,128)(2,1)S(1)}, bf16[4,592,128]{2,1,0:T(8,128)(2,1)S(1)}, u32[]{:S(2)}, u32[]{:S(2)}) collective-permute-start(bf16[4,592,128]{2,1,0:T(8,128)(2,1)S(1)} %in_order.1.refs_0_), channel_id=1, source_target_pairs={{0,2},{2,4},{4,6},{6,0},{8,10},{10,12},{12,14},{14,8},{16,18},{18,... | collective-permute-start | bytes 1818632 | tf_op jit(solution)/shard_map/ppermute | solution.py:550
  33.3 16.6 %collective-permute-start.9 = (bf16[4,592,128]{2,1,0:T(8,128)(2,1)S(1)}, bf16[4,592,128]{2,1,0:T(8,128)(2,1)S(1)}, u32[]{:S(2)}, u32[]{:S(2)}) collective-permute-start(bf16[4,592,128]{2,1,0:T(8,128)(2,1)S(1)} %in_order.1.refs_0_), channel_id=1, source_target_pairs={{0,54},{2,48},{4,50},{6,52},{8,62},{10,56},{12,58},{14,60},{16,6},... | collective-permute-start | bytes 1818632 | tf_op jit(solution)/shard_map/ppermute | solution.py:550
  37.6 15.7 %collective-permute-start.7 = (bf16[4,592,128]{2,1,0:T(8,128)(2,1)S(1)}, bf16[4,592,128]{2,1,0:T(8,128)(2,1)S(1)}, u32[]{:S(2)}, u32[]{:S(2)}) collective-permute-start(bf16[4,592,128]{2,1,0:T(8,128)(2,1)S(1)} %in_order.1.refs_0_), channel_id=1, source_target_pairs={{0,16},{2,18},{4,20},{6,22},{8,24},{10,26},{12,28},{14,30},{16,32}... | collective-permute-start | bytes 1818632 | tf_op jit(solution)/shard_map/ppermute | solution.py:550
  44.9 12.2 %collective-permute-start.4 = (bf16[4,592,128]{2,1,0:T(8,128)(2,1)S(1)}, bf16[4,592,128]{2,1,0:T(8,128)(2,1)S(1)}, u32[]{:S(2)}, u32[]{:S(2)}) collective-permute-start(bf16[4,592,128]{2,1,0:T(8,128)(2,1)S(1)} %in_order.1.refs_0_), channel_id=1, source_target_pairs={{0,1},{1,0},{2,3},{3,2},{4,5},{5,4},{6,7},{7,6},{8,9},{9,8},{10,11... | collective-permute-start | bytes 1818632 | tf_op jit(solution)/shard_map/ppermute | solution.py:542
  49.9 7.2 %collective-permute-start.10 = (bf16[4,592,128]{2,1,0:T(8,128)(2,1)S(1)}, bf16[4,592,128]{2,1,0:T(8,128)(2,1)S(1)}, u32[]{:S(2)}, u32[]{:S(2)}) collective-permute-start(bf16[4,592,128]{2,1,0:T(8,128)(2,1)S(1)} %collective-permute-done.9.refs_3_), channel_id=1, source_target_pairs={{0,1},{1,0},{2,3},{3,2},{4,5},{5,4},{6,7},{7,6},{8,9},{9,8},{10,11... | collective-permute-start | bytes 1818632 | tf_op jit(solution)/shard_map/ppermute | solution.py:542
  53.3 3.8 %collective-permute-start.8 = (bf16[4,592,128]{2,1,0:T(8,128)(2,1)S(1)}, bf16[4,592,128]{2,1,0:T(8,128)(2,1)S(1)}, u32[]{:S(2)}, u32[]{:S(2)}) collective-permute-start(bf16[4,592,128]{2,1,0:T(8,128)(2,1)S(1)} %collective-permute-done.7.refs_2_), channel_id=1, source_target_pairs={{0,1},{1,0},{2,3},{3,2},{4,5},{5,4},{6,7},{7,6},{8,9},{9,8},{10,11... | collective-permute-start | bytes 1818632 | tf_op jit(solution)/shard_map/ppermute | solution.py:542
  53.3 3.9 %collective-permute-start.6 = (bf16[4,592,128]{2,1,0:T(8,128)(2,1)S(1)}, bf16[4,592,128]{2,1,0:T(8,128)(2,1)S(1)}, u32[]{:S(2)}, u32[]{:S(2)}) collective-permute-start(bf16[4,592,128]{2,1,0:T(8,128)(2,1)S(1)} %collective-permute-done.5.refs_1_), channel_id=1, source_target_pairs={{0,1},{1,0},{2,3},{3,2},{4,5},{5,4},{6,7},{7,6},{8,9},{9,8},{10,11... | collective-permute-start | bytes 1818632 | tf_op jit(solution)/shard_map/ppermute | solution.py:542
  62.1 3.2 %collective-permute-start.11 = (bf16[8,72,1152]{2,1,0:T(8,128)(2,1)S(1)}, bf16[8,72,1152]{2,1,0:T(8,128)(2,1)S(1)}, u32[]{:S(2)}, u32[]{:S(2)}) collective-permute-start(bf16[8,72,1152]{2,1,0:T(8,128)(2,1)S(1)} %gradient.3), channel_id=1, source_target_pairs={{0,1},{1,0},{2,3},{3,2},{4,5},{5,4},{6,7},{7,6},{8,9},{9,8},{10,11... | collective-permute-start | bytes 3981320 | tf_op jit(solution)/shard_map/ppermute | solution.py:542
  63.2 6.7 %collective-permute-start.12 = (bf16[4,72,1152]{2,1,0:T(8,128)(2,1)S(1)}, bf16[4,72,1152]{2,1,0:T(8,128)(2,1)S(1)}, u32[]{:S(2)}, u32[]{:S(2)}) collective-permute-start(bf16[4,72,1152]{2,1,0:T(8,128)(2,1)S(1)} %gradient.4), channel_id=1, source_target_pairs={{0,1},{1,0},{2,3},{3,2},{4,5},{5,4},{6,7},{7,6},{8,9},{9,8},{10,11... | collective-permute-start | bytes 1990664 | tf_op jit(solution)/shard_map/ppermute | solution.py:542
  65.9 18.2 %collective-permute-start.16 = (bf16[4,72,1152]{2,1,0:T(8,128)(2,1)S(1)}, bf16[4,72,1152]{2,1,0:T(8,128)(2,1)S(1)}, u32[]{:S(2)}, u32[]{:S(2)}) collective-permute-start(bf16[4,72,1152]{2,1,0:T(8,128)(2,1)S(1)} %get-tuple-element.240), channel_id=1, source_target_pairs={{0,16},{2,18},{4,20},{6,22},{8,24},{10,26},{12,28},{14,30},{16,32}... | collective-permute-start | bytes 1990664 | tf_op jit(solution)/shard_map/ppermute | solution.py:550
  66.0 18.1 %collective-permute-start.17 = (bf16[4,72,1152]{2,1,0:T(8,128)(2,1)S(1)}, bf16[4,72,1152]{2,1,0:T(8,128)(2,1)S(1)}, u32[]{:S(2)}, u32[]{:S(2)}) collective-permute-start(bf16[4,72,1152]{2,1,0:T(8,128)(2,1)S(1)} %get-tuple-element.241), channel_id=1, source_target_pairs={{0,54},{2,48},{4,50},{6,52},{8,62},{10,56},{12,58},{14,60},{16,6},... | collective-permute-start | bytes 1990664 | tf_op jit(solution)/shard_map/ppermute | solution.py:550
  70.2 18.0 %collective-permute-start.15 = (bf16[4,72,1152]{2,1,0:T(8,128)(2,1)S(1)}, bf16[4,72,1152]{2,1,0:T(8,128)(2,1)S(1)}, u32[]{:S(2)}, u32[]{:S(2)}) collective-permute-start(bf16[4,72,1152]{2,1,0:T(8,128)(2,1)S(1)} %combine.4), channel_id=1, source_target_pairs={{0,2},{2,4},{4,6},{6,0},{8,10},{10,12},{12,14},{14,8},{16,18},{18,... | collective-permute-start | bytes 1990664 | tf_op jit(solution)/shard_map/ppermute | solution.py:550
  72.9 1.7 %collective-permute-start.13 = (bf16[2,72,1152]{2,1,0:T(8,128)(2,1)S(1)}, bf16[2,72,1152]{2,1,0:T(8,128)(2,1)S(1)}, u32[]{:S(2)}, u32[]{:S(2)}) collective-permute-start(bf16[2,72,1152]{2,1,0:T(8,128)(2,1)S(1)} %get-tuple-element.237), channel_id=1, source_target_pairs={{0,1},{1,0},{2,3},{3,2},{4,5},{5,4},{6,7},{7,6},{8,9},{9,8},{10,11... | collective-permute-start | bytes 995336 | tf_op jit(solution)/shard_map/ppermute | solution.py:542
  73.0 2.1 %collective-permute-start.14 = (bf16[2,72,1152]{2,1,0:T(8,128)(2,1)S(1)}, bf16[2,72,1152]{2,1,0:T(8,128)(2,1)S(1)}, u32[]{:S(2)}, u32[]{:S(2)}) collective-permute-start(bf16[2,72,1152]{2,1,0:T(8,128)(2,1)S(1)} %get-tuple-element.238), channel_id=1, source_target_pairs={{0,1},{1,0},{2,3},{3,2},{4,5},{5,4},{6,7},{7,6},{8,9},{9,8},{10,11... | collective-permute-start | bytes 995336 | tf_op jit(solution)/shard_map/ppermute | solution.py:542
  74.4 20.8 %copy-start.2 = (bf16[288]{0:T(512)(128)(2,1)S(1)}, bf16[288]{0:T(512)(128)(2,1)}, u32[]{:S(2)}) copy-start(bf16[288]{0:T(512)(128)(2,1)} %gain_hbm.1) | copy-start | bytes 1732
  74.4 27.0 %copy-start = (bf16[32,288]{1,0:T(8,128)(2,1)S(1)}, bf16[32,288]{1,0:T(8,128)(2,1)}, u32[]{:S(2)}) copy-start(bf16[32,288]{1,0:T(8,128)(2,1)} %refs_6_.1) | copy-start | bytes 55300
  74.4 27.0 %copy-start.1 = (f32[512]{0:T(512)S(1)}, f32[512]{0:T(512)}, u32[]{:S(2)}) copy-start(f32[512]{0:T(512)} %param.11) | copy-start | bytes 6148
  88.6 9.9 %collective-permute-start.18 = (bf16[96,1152]{1,0:T(8,128)(2,1)S(1)}, bf16[96,1152]{1,0:T(8,128)(2,1)S(1)}, u32[]{:S(2)}, u32[]{:S(2)}) collective-permute-start(bf16[96,1152]{1,0:T(8,128)(2,1)S(1)} %get-tuple-element.243), channel_id=1, source_target_pairs={{0,4},{2,6},{4,0},{6,2},{8,12},{10,14},{12,8},{14,10},{16,20},{18,... | collective-permute-start | bytes 663560 | tf_op jit(solution)/shard_map/ppermute | solution.py:550
  89.1 12.3 %collective-permute-start.19 = (bf16[96,1152]{1,0:T(8,128)(2,1)S(1)}, bf16[96,1152]{1,0:T(8,128)(2,1)S(1)}, u32[]{:S(2)}, u32[]{:S(2)}) collective-permute-start(bf16[96,1152]{1,0:T(8,128)(2,1)S(1)} %get-tuple-element.244), channel_id=1, source_target_pairs={{0,32},{2,34},{4,36},{6,38},{8,40},{10,42},{12,44},{14,46},{16,48}... | collective-permute-start | bytes 663560 | tf_op jit(solution)/shard_map/ppermute | solution.py:550
  89.2 12.2 %collective-permute-start.20 = (bf16[96,1152]{1,0:T(8,128)(2,1)S(1)}, bf16[96,1152]{1,0:T(8,128)(2,1)S(1)}, u32[]{:S(2)}, u32[]{:S(2)}) collective-permute-start(bf16[96,1152]{1,0:T(8,128)(2,1)S(1)} %get-tuple-element.245), channel_id=1, source_target_pairs={{0,36},{2,38},{4,32},{6,34},{8,44},{10,46},{12,40},{14,42},{16,52}... | collective-permute-start | bytes 663560 | tf_op jit(solution)/shard_map/ppermute | solution.py:550
